TPU v7x, 32 devices: a whole 2x2x4 slice. The times are simulated.
32 devices in a mesh: ctx: 8 (over y, x, core), exp: 4 (over z).
Axes of the slice: x: 2, y: 2, z: 4, core: 2. Of those that a mesh axis runs over, the one named last changes fastest.
Arguments:
- tokens: bfloat16 [4, 1024, 2048], P('exp', 'ctx'), may hold values from -6 to 6
- expert_ids: int32 [4, 1024, 8], P('exp', 'ctx'), may hold values from 0 to 31, all different within a row; in each aligned block of 128 rows (0 to 127, 128 to 255, ..., all dimensions but the last counted through in order) at most 48 rows name the same one
- cotangent: bfloat16 [4, 1024, 2048], P('exp', 'ctx'), may hold values from -6 to 6
- attn_gain: bfloat16 [2048], P(('ctx', 'exp')), may hold values from 0.5 to 1.5
- ffn_gain: bfloat16 [2048], P(('ctx', 'exp')), may hold values from 0.5 to 1.5
- query_gain: bfloat16 [128], P(('ctx', 'exp')), may hold values from 0.099609375 to 1.8984375
- key_gain: bfloat16 [128], P(('ctx', 'exp')), may hold values from 0.099609375 to 1.8984375
- query_weight: bfloat16 [2048, 4096], P(('ctx', 'exp')), may hold values from -0.125 to 0.125
- key_weight: bfloat16 [2048, 512], P(('ctx', 'exp')), may hold values from -0.125 to 0.125
- value_weight: bfloat16 [2048, 512], P(('ctx', 'exp')), may hold values from -0.125 to 0.125
- output_weight: bfloat16 [4096, 2048], P(('ctx', 'exp')), may hold values from -1.5 to 1.5
- router_weight: bfloat16 [2048, 32], P(('ctx', 'exp')), may hold values from -0.0625 to 0.0625
- gate_weight: bfloat16 [32, 2048, 768], P(('ctx', 'exp')), may hold values from -0.125 to 0.125
- up_weight: bfloat16 [32, 2048, 768], P(('ctx', 'exp')), may hold values from -0.125 to 0.125
- down_weight: bfloat16 [32, 768, 2048], P(('ctx', 'exp')), may hold values from -0.875 to 0.875
Outputs:
- layer_out: bfloat16 [4, 1024, 2048], P('exp', 'ctx')
- grad_tokens: float32 [4, 1024, 2048], P('exp', 'ctx')
- grad_attn_gain: float32 [2048], P(('ctx', 'exp'))
- grad_ffn_gain: float32 [2048], P(('ctx', 'exp'))
- grad_query_gain: float32 [128], P(('ctx', 'exp'))
- grad_key_gain: float32 [128], P(('ctx', 'exp'))
- grad_query: float32 [2048, 4096], P(('ctx', 'exp'))
- grad_key: float32 [2048, 512], P(('ctx', 'exp'))
- grad_value: float32 [2048, 512], P(('ctx', 'exp'))
- grad_output: float32 [4096, 2048], P(('ctx', 'exp'))
- grad_router: float32 [2048, 32], P(('ctx', 'exp'))
- grad_gate: float32 [32, 2048, 768], P(('ctx', 'exp'))
- grad_up: float32 [32, 2048, 768], P(('ctx', 'exp'))
- grad_down: float32 [32, 768, 2048], P(('ctx', 'exp'))
Inputs may be any that keep to these rules, and one draw needn't show every extreme that they name: `expert_ids`: each row names 8 different experts. Among the 128 rows of one device no expert is named more than 48 times, and in every draw some expert is named exactly 48 times in some device's rows.
All inputs are finite; a program needn't handle non-finite values.
Results may differ from a plain program's by a relative error of at most 0.03.
Values may be sent and summed in bfloat16 or wider, within the bound.
No kernel may reach another device: no remote copies, remote signals or barrier semaphores. Data moves between devices by JAX's collectives and lax.ppermute only.
A program may use at most 256 MiB of HBM per device.

v0:
```python
import math

import jax
import jax.numpy as jnp
from jax import lax
from jax.sharding import PartitionSpec as P

D = 2048
H = 32
KVH = 4
HD = 128
TOP = 8
BLK = 256


EPSILON = 1e-06
ROPE_BASE = 1000000.0
MASKED = -1e30


def norm_gain(values, gain_vec):
    inverse = lax.rsqrt(jnp.mean(values * values, axis=-1, keepdims=True) + EPSILON)
    return values * inverse * gain_vec


def rotary(values, positions):
    half_dim = values.shape[-1] // 2
    exponent = jnp.arange(half_dim).astype(jnp.float32) * (-2.0 / values.shape[-1])
    frequency = jnp.power(ROPE_BASE, exponent)
    angles = positions.astype(jnp.float32)[:, None] * frequency[None, :]
    cosine = jnp.cos(angles)[:, None, :]
    sine_vals = jnp.sin(angles)[:, None, :]
    first_half = values[..., :half_dim]
    second_half = values[..., half_dim:]
    return jnp.concatenate(
        [
            first_half * cosine - second_half * sine_vals,
            second_half * cosine + first_half * sine_vals,
        ],
        axis=-1,
    )


def prepare(raw_rows, gain_vec, row_pos):
    return rotary(norm_gain(raw_rows.reshape(raw_rows.shape[0], -1, HD), gain_vec), row_pos)


def silu_product(gate_act, up_act):
    return gate_act * jax.nn.sigmoid(gate_act) * up_act


def pick_softmax(logit_rows, selector):
    picked_logits = jnp.sum(selector * logit_rows[:, None, :], axis=-1)
    highest = jnp.max(picked_logits, axis=-1, keepdims=True)
    raised = jnp.exp(picked_logits - highest)
    return raised / jnp.sum(raised, axis=-1, keepdims=True)


def in_blocks(step_fn, carried, pieces):
    piece_rows = pieces[0].shape[0]
    part_rows = math.gcd(piece_rows, 512)

    def one_part(number, inner):
        part = tuple(
            (
                lax.dynamic_slice_in_dim(member, number * part_rows, part_rows, 0)
                for member in pieces
            )
        )
        return step_fn(inner, part, number * part_rows)

    return lax.fori_loop(0, piece_rows // part_rows, one_part, carried)


def route(buffer):
    return lax.all_to_all(buffer, ("ctx", "exp"), split_axis=0, concat_axis=0, tiled=True)


def on_device(
    tokens,
    expert_ids,
    cotangent,
    attn_gain,
    ffn_gain,
    query_gain,
    key_gain,
    query_weight,
    key_weight,
    value_weight,
    output_weight,
    router_weight,
    gate_weight,
    up_weight,
    down_weight,
):
    gathered = (
        lax.all_gather(query_weight, ("ctx", "exp"), axis=0, tiled=True),
        lax.all_gather(key_weight, ("ctx", "exp"), axis=0, tiled=True),
        lax.all_gather(value_weight, ("ctx", "exp"), axis=0, tiled=True),
        lax.all_gather(output_weight, ("ctx", "exp"), axis=0, tiled=True),
        lax.all_gather(router_weight, ("ctx", "exp"), axis=0, tiled=True),
        lax.all_gather(attn_gain, ("ctx", "exp"), axis=0, tiled=True),
        lax.all_gather(ffn_gain, ("ctx", "exp"), axis=0, tiled=True),
        lax.all_gather(query_gain, ("ctx", "exp"), axis=0, tiled=True),
        lax.all_gather(key_gain, ("ctx", "exp"), axis=0, tiled=True),
    )
    w_query, w_key, w_value, w_output, w_router, gain_attn, gain_ffn, gain_query, gain_key = (
        gathered
    )
    local_rows = tokens.shape[1]
    groups = H // KVH
    score_scale = HD ** (-0.5)
    ctx_count = lax.axis_size("ctx")
    ctx_index = lax.axis_index("ctx")
    seq_rows = local_rows * ctx_count
    positions = ctx_index * local_rows + lax.iota(jnp.int32, local_rows)
    inputs = tokens[0].astype(jnp.float32)
    query_gain_f32 = gain_query.astype(jnp.float32)
    key_gain_f32 = gain_key.astype(jnp.float32)
    normed_attn, pull_attn = jax.vjp(norm_gain, inputs, gain_attn.astype(jnp.float32))
    attn_in = normed_attn.astype(jnp.bfloat16)
    key_raw = jnp.dot(attn_in, w_key, preferred_element_type=jnp.float32)
    key_rot, pull_key = jax.vjp(
        lambda raw_rows, gain_vec: prepare(raw_rows, gain_vec, positions), key_raw, key_gain_f32
    )
    query_pos = jnp.tile(positions, groups)
    query_raw = jnp.dot(attn_in, w_query, preferred_element_type=jnp.float32)
    value_rows = jnp.dot(attn_in, w_value, preferred_element_type=jnp.float32).astype(jnp.bfloat16)
    query_rot, pull_query = jax.vjp(
        lambda raw_rows, gain_vec: prepare(raw_rows, gain_vec, positions), query_raw, query_gain_f32
    )
    query_rows = (
        query_rot.astype(jnp.bfloat16)
        .reshape(local_rows, KVH, groups, HD)
        .transpose(1, 2, 0, 3)
        .reshape(KVH, groups * local_rows, HD)
    )
    key_rows = key_rot.astype(jnp.bfloat16).reshape(local_rows, KVH * HD)

    def forward_step(carried, pieces, first_row):
        running_max, row_total, accumulated = carried
        key_part, value_part = pieces
        piece_rows = key_part.shape[0]
        key_heads = key_part.reshape(piece_rows, KVH, HD)
        value_heads = value_part.reshape(piece_rows, KVH, HD)
        scores = (
            jnp.einsum("kqd,skd->kqs", query_rows, key_heads, preferred_element_type=jnp.float32)
            * score_scale
        )
        key_pos = first_row + lax.iota(jnp.int32, piece_rows)
        allowed = ((key_pos // BLK)[None, :] <= (query_pos // BLK)[:, None])[None]
        scores = jnp.where(allowed, scores, MASKED)
        new_max = jnp.maximum(running_max, jnp.max(scores, axis=-1))
        weights = jnp.where(allowed, jnp.exp(scores - new_max[..., None]), 0.0)
        factor = jnp.exp(running_max - new_max)
        row_total = row_total * factor + jnp.sum(weights, axis=-1)
        accumulated = accumulated * factor[..., None] + jnp.einsum(
            "kqs,skd->kqd",
            weights.astype(jnp.bfloat16),
            value_heads,
            preferred_element_type=jnp.float32,
        )
        return (new_max, row_total, accumulated)

    initial = (
        jnp.full((KVH, groups * local_rows), MASKED, jnp.float32),
        jnp.zeros((KVH, groups * local_rows), jnp.float32),
        jnp.zeros((KVH, groups * local_rows, HD), jnp.float32),
    )
    running_max, row_total, accumulated = in_blocks(
        forward_step,
        initial,
        (
            lax.all_gather(key_rows, "ctx", axis=0, tiled=True),
            lax.all_gather(value_rows, "ctx", axis=0, tiled=True),
        ),
    )
    attn_f32 = accumulated / row_total[..., None]
    log_total = running_max + jnp.log(row_total)
    attn_flat = (
        attn_f32.astype(jnp.bfloat16)
        .reshape(KVH, groups, local_rows, HD)
        .transpose(2, 0, 1, 3)
        .reshape(local_rows, H * HD)
    )
    residual = inputs + jnp.dot(attn_flat, w_output, preferred_element_type=jnp.float32)
    normed_ffn, pull_ffn = jax.vjp(norm_gain, residual, gain_ffn.astype(jnp.float32))
    ffn_in = normed_ffn.astype(jnp.bfloat16)
    logits = jnp.dot(ffn_in, w_router, preferred_element_type=jnp.float32)
    experts = w_router.shape[1]
    capacity = max(2, local_rows * TOP * 3 // (2 * experts))
    chosen = expert_ids[0]
    selector = (chosen[:, :, None] == lax.iota(jnp.int32, experts)[None, None, :]).astype(
        jnp.float32
    )
    gate_probs, pull_gates = jax.vjp(lambda logit_rows: pick_softmax(logit_rows, selector), logits)
    flat_sel = selector.reshape(local_rows * TOP, experts).astype(jnp.int32)
    earlier = jnp.cumsum(flat_sel, axis=0) - flat_sel
    rank_rows = jnp.sum(earlier * flat_sel, axis=1)
    slot_rows = chosen.reshape(-1) * capacity + rank_rows
    send_rows = (
        jnp.zeros((experts * capacity, D), jnp.bfloat16)
        .at[slot_rows]
        .set(jnp.repeat(ffn_in, TOP, axis=0))
    )
    received = route(send_rows.reshape(experts, capacity, D)).reshape(-1, D)
    gate_act = jnp.dot(received, gate_weight[0], preferred_element_type=jnp.float32)
    up_act = jnp.dot(received, up_weight[0], preferred_element_type=jnp.float32)
    hidden_f32, pull_hidden = jax.vjp(silu_product, gate_act, up_act)
    hidden = hidden_f32.astype(jnp.bfloat16)
    expert_out = jnp.dot(hidden, down_weight[0], preferred_element_type=jnp.float32).astype(
        jnp.bfloat16
    )
    returned = route(expert_out.reshape(experts, capacity, D)).reshape(-1, D)
    picked = returned[slot_rows].reshape(local_rows, TOP, D).astype(jnp.float32)
    mixture = jnp.sum(gate_probs[..., None] * picked, axis=1)
    layer_out = (residual + mixture).astype(jnp.bfloat16)[None]
    upstream = cotangent[0].astype(jnp.float32)
    grad_gate_probs = jnp.sum(picked * upstream[:, None, :], axis=-1)
    grad_picked = (gate_probs[..., None] * upstream[:, None, :]).astype(jnp.bfloat16)
    grad_send = (
        jnp.zeros((experts * capacity, D), jnp.bfloat16)
        .at[slot_rows]
        .set(grad_picked.reshape(-1, D))
    )
    grad_expert_out = route(grad_send.reshape(experts, capacity, D)).reshape(-1, D)
    grad_hidden = jnp.einsum(
        "rd,fd->rf", grad_expert_out, down_weight[0], preferred_element_type=jnp.float32
    )
    grad_down = jnp.einsum("rf,rd->fd", hidden, grad_expert_out, preferred_element_type=jnp.float32)
    grad_gate_act, grad_up_act = pull_hidden(grad_hidden)
    grad_gate_low = grad_gate_act.astype(jnp.bfloat16)
    grad_up_low = grad_up_act.astype(jnp.bfloat16)
    grad_gate = jnp.einsum("rd,rf->df", received, grad_gate_low, preferred_element_type=jnp.float32)
    grad_up = jnp.einsum("rd,rf->df", received, grad_up_low, preferred_element_type=jnp.float32)
    grad_received = (
        jnp.einsum("rf,df->rd", grad_gate_low, gate_weight[0], preferred_element_type=jnp.float32)
        + jnp.einsum("rf,df->rd", grad_up_low, up_weight[0], preferred_element_type=jnp.float32)
    ).astype(jnp.bfloat16)
    grad_returned = route(grad_received.reshape(experts, capacity, D)).reshape(-1, D)
    grad_ffn_experts = jnp.sum(
        grad_returned[slot_rows].reshape(local_rows, TOP, D).astype(jnp.float32), axis=1
    )
    (grad_logits,) = pull_gates(grad_gate_probs)
    grad_logits_low = grad_logits.astype(jnp.bfloat16)
    grad_router = jnp.einsum(
        "td,te->de", ffn_in, grad_logits_low, preferred_element_type=jnp.float32
    )
    grad_ffn_in = grad_ffn_experts + jnp.einsum(
        "te,de->td", grad_logits_low, w_router, preferred_element_type=jnp.float32
    )
    grad_resid_norm, grad_gain_ffn = pull_ffn(grad_ffn_in)
    grad_residual = upstream + grad_resid_norm
    grad_branch = grad_residual.astype(jnp.bfloat16)
    grad_output = jnp.einsum(
        "tf,td->fd", attn_flat, grad_branch, preferred_element_type=jnp.float32
    )
    grad_attn = jnp.einsum(
        "td,fd->tf", grad_branch, w_output, preferred_element_type=jnp.float32
    ).astype(jnp.bfloat16)
    grad_attn_rows = (
        grad_attn.reshape(local_rows, KVH, groups, HD)
        .transpose(1, 2, 0, 3)
        .reshape(KVH, groups * local_rows, HD)
    )
    row_delta = jnp.sum(grad_attn_rows.astype(jnp.float32) * attn_f32, axis=-1)

    def backward_step(carried, pieces, first_row):
        grad_query_acc, grad_key_all, grad_value_all = carried
        key_part, value_part = pieces
        piece_rows = key_part.shape[0]
        key_heads = key_part.reshape(piece_rows, KVH, HD)
        value_heads = value_part.reshape(piece_rows, KVH, HD)
        scores = (
            jnp.einsum("kqd,skd->kqs", query_rows, key_heads, preferred_element_type=jnp.float32)
            * score_scale
        )
        key_pos = first_row + lax.iota(jnp.int32, piece_rows)
        allowed = ((key_pos // BLK)[None, :] <= (query_pos // BLK)[:, None])[None]
        scores = jnp.where(allowed, scores, MASKED)
        probs = jnp.where(allowed, jnp.exp(scores - log_total[..., None]), 0.0)
        grad_probs = jnp.einsum(
            "kqd,skd->kqs", grad_attn_rows, value_heads, preferred_element_type=jnp.float32
        )
        grad_scores = (probs * (grad_probs - row_delta[..., None])).astype(jnp.bfloat16)
        grad_query_acc = grad_query_acc + score_scale * jnp.einsum(
            "kqs,skd->kqd", grad_scores, key_heads, preferred_element_type=jnp.float32
        )
        grad_key_part = score_scale * jnp.einsum(
            "kqs,kqd->skd", grad_scores, query_rows, preferred_element_type=jnp.float32
        )
        grad_value_part = jnp.einsum(
            "kqs,kqd->skd",
            probs.astype(jnp.bfloat16),
            grad_attn_rows,
            preferred_element_type=jnp.float32,
        )
        grad_key_all = lax.dynamic_update_slice_in_dim(
            grad_key_all, grad_key_part.reshape(piece_rows, KVH * HD), first_row, 0
        )
        grad_value_all = lax.dynamic_update_slice_in_dim(
            grad_value_all, grad_value_part.reshape(piece_rows, KVH * HD), first_row, 0
        )
        return (grad_query_acc, grad_key_all, grad_value_all)

    back_initial = (
        jnp.zeros((KVH, groups * local_rows, HD), jnp.float32),
        jnp.zeros((seq_rows, KVH * HD), jnp.float32),
        jnp.zeros((seq_rows, KVH * HD), jnp.float32),
    )
    grad_query_acc, grad_key_all, grad_value_all = in_blocks(
        backward_step,
        back_initial,
        (
            lax.all_gather(key_rows, "ctx", axis=0, tiled=True),
            lax.all_gather(value_rows, "ctx", axis=0, tiled=True),
        ),
    )
    grad_keys, grad_values = (
        lax.psum_scatter(
            grad_key_all.astype(jnp.bfloat16), "ctx", scatter_dimension=0, tiled=True
        ).astype(jnp.float32),
        lax.psum_scatter(
            grad_value_all.astype(jnp.bfloat16), "ctx", scatter_dimension=0, tiled=True
        ).astype(jnp.float32),
    )
    grad_query_heads = (
        grad_query_acc.reshape(KVH, groups, local_rows, HD)
        .transpose(2, 0, 1, 3)
        .reshape(local_rows, H, HD)
    )
    grad_query_raw, grad_gain_query = pull_query(grad_query_heads)
    grad_query_low = grad_query_raw.astype(jnp.bfloat16)
    grad_query = jnp.einsum(
        "td,tf->df", attn_in, grad_query_low, preferred_element_type=jnp.float32
    )
    grad_attn_query = jnp.einsum(
        "tf,df->td", grad_query_low, w_query, preferred_element_type=jnp.float32
    )
    grad_key_raw, grad_gain_key = pull_key(grad_keys.reshape(local_rows, KVH, HD))
    grad_key_low = grad_key_raw.astype(jnp.bfloat16)
    grad_value_low = grad_values.astype(jnp.bfloat16)
    grad_key = jnp.einsum("td,tf->df", attn_in, grad_key_low, preferred_element_type=jnp.float32)
    grad_value = jnp.einsum(
        "td,tf->df", attn_in, grad_value_low, preferred_element_type=jnp.float32
    )
    grad_attn_in = grad_attn_query + jnp.einsum(
        "tf,df->td", grad_key_low, w_key, preferred_element_type=jnp.float32
    )
    grad_attn_in = grad_attn_in + jnp.einsum(
        "tf,df->td", grad_value_low, w_value, preferred_element_type=jnp.float32
    )
    grad_inputs_norm, grad_gain_attn = pull_attn(grad_attn_in)
    grad_tokens = (grad_residual + grad_inputs_norm)[None]
    all_sums = (
        lax.psum_scatter(grad_query, ("ctx", "exp"), scatter_dimension=0, tiled=True),
        lax.psum_scatter(grad_key, ("ctx", "exp"), scatter_dimension=0, tiled=True),
        lax.psum_scatter(grad_value, ("ctx", "exp"), scatter_dimension=0, tiled=True),
        lax.psum_scatter(grad_output, ("ctx", "exp"), scatter_dimension=0, tiled=True),
        lax.psum_scatter(grad_router, ("ctx", "exp"), scatter_dimension=0, tiled=True),
        lax.psum_scatter(grad_gain_attn, ("ctx", "exp"), scatter_dimension=0, tiled=True),
        lax.psum_scatter(grad_gain_ffn, ("ctx", "exp"), scatter_dimension=0, tiled=True),
        lax.psum_scatter(grad_gain_query, ("ctx", "exp"), scatter_dimension=0, tiled=True),
        lax.psum_scatter(grad_gain_key, ("ctx", "exp"), scatter_dimension=0, tiled=True),
    )
    (
        sum_query,
        sum_key,
        sum_value,
        sum_output,
        sum_router,
        sum_attn_gain,
        sum_ffn_gain,
        sum_query_gain,
        sum_key_gain,
    ) = all_sums
    return (
        layer_out,
        grad_tokens,
        sum_attn_gain,
        sum_ffn_gain,
        sum_query_gain,
        sum_key_gain,
        sum_query,
        sum_key,
        sum_value,
        sum_output,
        sum_router,
        grad_gate[None],
        grad_up[None],
        grad_down[None],
    )


def solution(mesh):
    return jax.shard_map(
        on_device,
        mesh=mesh,
        in_specs=(
            P("exp", "ctx", None),
            P("exp", "ctx", None),
            P("exp", "ctx", None),
            P(("ctx", "exp")),
            P(("ctx", "exp")),
            P(("ctx", "exp")),
            P(("ctx", "exp")),
            P(("ctx", "exp"), None),
            P(("ctx", "exp"), None),
            P(("ctx", "exp"), None),
            P(("ctx", "exp"), None),
            P(("ctx", "exp"), None),
            P(("ctx", "exp"), None, None),
            P(("ctx", "exp"), None, None),
            P(("ctx", "exp"), None, None),
        ),
        out_specs=(
            P("exp", "ctx", None),
            P("exp", "ctx", None),
            P(("ctx", "exp")),
            P(("ctx", "exp")),
            P(("ctx", "exp")),
            P(("ctx", "exp")),
            P(("ctx", "exp"), None),
            P(("ctx", "exp"), None),
            P(("ctx", "exp"), None),
            P(("ctx", "exp"), None),
            P(("ctx", "exp"), None),
            P(("ctx", "exp"), None, None),
            P(("ctx", "exp"), None, None),
            P(("ctx", "exp"), None, None),
        ),
        check_vma=False,
    )
```

profile of v0, /device:TPU:0, one launch (start us, length us, event | category | flops | bytes accessed | tf_op | source)
XLA Modules:
  0.0 3159.2 jit_solution(8509884060690705355)
XLA Ops:
  12.1 42.3 %all-reduce.13 = (bf16[2048]{0:T(1024)(128)(2,1)S(1)}, bf16[128]{0:T(256)(128)(2,1)S(1)}, bf16[128]{0:T(256)(128)(2,1)S(1)}, bf16[2048]{0:T(1024)(128)(2,1)S(1)}) all-reduce(bf16[2048]{0:T(1024)(128)(2,1)S(1)} %dynamic-update-slice, bf16[128]{0:T(256)(128)(2,1)S(1)} %dynamic-update-slice.1, ...), channel_id=1, replica_groups=mesh['ctx'=8,'exp'=4] {'ctx','exp'}, use_global_device_ids=true, to_apply=%add.4 | all-reduce | flops 4352 | bytes 17408
  55.9 14.3 all-gather.14.cloned.1.call-done
  74.0 54.5 %all-gather.8.cloned.1.call-done = bf16[2048,512]{1,0:T(8,128)(2,1)} async-done(((bf16[64,512]{1,0:T(8,128)(2,1)}), bf16[2048,512]{1,0:T(8,128)(2,1)}) %all-gather.8.cloned.1.call-update) | async-done | bytes 2097168 | tf_op jit(solution)/shard_map/all_gather | solution.py:98
  155.7 115.5 %all-gather.12.cloned.1.call-done = bf16[2048,4096]{1,0:T(8,128)(2,1)} async-done(((bf16[64,4096]{1,0:T(8,128)(2,1)}), bf16[2048,4096]{1,0:T(8,128)(2,1)}) %all-gather.12.cloned.1.call-update) | async-done | bytes 16777232 | tf_op jit(solution)/shard_map/all_gather | solution.py:97
  271.2 21.4 copy.172
  306.5 42.7 %while.42 = (s32[]{:T(128)}, f32[4,1024]{1,0:T(4,128)S(1)}, f32[4,1024]{1,0:T(4,128)S(1)}, f32[4,1024,128]{2,1,0:T(8,128)}, bf16[1024,512]{0,1:T(8,128)(2,1)}, /...) while((s32[]{:T(128)}, f32[4,1024]{1,0:T(4,128)S(1)}, ...), condition=%wide.region_6.7_spmd.clone, body=%wide.region_3.6_spmd.clone.sunk | while | flops 1103143936 | bytes 71589640 | solution.py:72
  354.4 58.6 %all-gather.18.cloned.1.call-done = bf16[4096,2048]{1,0:T(8,128)(2,1)} async-done(((bf16[128,2048]{1,0:T(8,128)(2,1)}), bf16[4096,2048]{1,0:T(8,128)(2,1)}) %all-gather.18.cloned.1.call-update) | async-done | bytes 16777232 | tf_op jit(solution)/shard_map/all_gather | solution.py:100
  438.0 201.1 %all-gather = bf16[32,64,32]{1,2,0:T(8,128)(2,1)S(1)} all-gather(bf16[1,64,32]{1,2,0:T(8,128)(2,1)S(1)} %bitcast.423), channel_id=1, replica_groups=mesh['ctx'=8,'exp'=4] {'ctx','exp'}, dimensions={0}, use_global_device_ids=true | all-gather | bytes 135168 | tf_op jit(solution)/shard_map/all_gather | solution.py:101
  678.1 118.8 %all-to-all-done.2 = bf16[32,48,2048]{2,1,0:T(8,128)(2,1)} async-done(((bf16[32,48,2048]{2,1,0:T(8,128)(2,1)}), bf16[32,48,2048]{2,1,0:T(8,128)(2,1)}, u32[]{:S(2)}, u32[]{:S(2)}) %all-to-all-start.2) | async-done | bytes 6291488 | tf_op jit(solution)/shard_map/all_to_all | solution.py:76
  843.2 128.3 %all-to-all-done.3 = bf16[32,48,2048]{2,1,0:T(8,128)(2,1)} async-done(((bf16[32,48,2048]{2,1,0:T(8,128)(2,1)}), bf16[32,48,2048]{2,1,0:T(8,128)(2,1)}, u32[]{:S(2)}, u32[]{:S(2)}) %all-to-all-start.3) | async-done | bytes 6291488 | tf_op jit(solution)/shard_map/all_to_all | solution.py:76
  997.1 118.4 %all-to-all-done.1 = bf16[32,48,2048]{2,1,0:T(8,128)(2,1)} async-done(((bf16[32,48,2048]{2,1,0:T(8,128)(2,1)}), bf16[32,48,2048]{2,1,0:T(8,128)(2,1)}, u32[]{:S(2)}, u32[]{:S(2)}) %all-to-all-start.1) | async-done | bytes 6291488 | tf_op jit(solution)/shard_map/all_to_all | solution.py:76
  1140.2 12.7 fusion.81
  1161.8 47.4 %while.43 = (s32[]{:T(128)}, f32[4,1024,128]{2,1,0:T(8,128)S(1)}, bf16[1024,512]{0,1:T(8,128)(2,1)}, bf16[1024,512]{0,1:T(8,128)(2,1)}, bf16[1024,512]{0,1:T(8,1...) while((s32[]{:T(128)}, f32[4,1024,128]{2,1,0:T(8,128)S(1)}, ...), condition=%wide.region_26.27_spmd.clone, body=%wide.region_25.26_spmd.clone.sunk | while | flops 2712163328 | bytes 167845904 | solution.py:72
  1215.5 34.6 %reduce-scatter.22.cloned.1.call-done = bf16[128,512]{1,0:T(8,128)(2,1)} async-done(((bf16[1024,512]{1,0:T(8,128)(2,1)}), bf16[128,512]{1,0:T(8,128)(2,1)}) %reduce-scatter.22.cloned.1.call-update) | async-done | bytes 131088
  1255.6 34.3 %reduce-scatter.24.cloned.1.call-done = bf16[128,512]{1,0:T(8,128)(2,1)} async-done(((bf16[1024,512]{1,0:T(8,128)(2,1)}), bf16[128,512]{1,0:T(8,128)(2,1)}) %reduce-scatter.24.cloned.1.call-update) | async-done | bytes 131088
  1300.5 13.3 fusion.105
  1315.4 13.2 fusion.108
  1360.4 12.5 fusion.134
  1372.9 55.0 %reduce-scatter.26.cloned.1.call-done = f32[64,32]{1,0:T(8,128)} async-done(((f32[2048,32]{1,0:T(8,128)}), f32[64,32]{1,0:T(8,128)}) %reduce-scatter.26.cloned.1.call-update) | async-done | bytes 8208
  1435.8 38.0 %all-reduce.12 = (f32[2048]{0:T(1024)S(1)}, f32[2048]{0:T(1024)S(1)}, f32[128]{0:T(128)S(1)}, f32[128]{0:T(128)S(1)}) all-reduce(f32[2048]{0:T(1024)S(1)} %get-tuple-element.802, f32[2048]{0:T(1024)S(1)} %copy-done.44, f32[128]{0:T(128)S(1)} %get-tuple-element.796, ...), channel_id=4, replica_groups=mesh['ctx'=8,'exp'=4] {'ctx','exp'}, use_global_device_ids=true, to_apply=%region_33.34.clone | all-reduce | flops 4352 | bytes 34816
  1479.2 95.9 %reduce-scatter.16.cloned.1.call-done = f32[64,512]{1,0:T(8,128)} async-done(((f32[2048,512]{1,0:T(8,128)}), f32[64,512]{1,0:T(8,128)}) %reduce-scatter.16.cloned.1.call-update) | async-done | bytes 131088 | tf_op jit(solution)/shard_map/reduce_scatter | solution.py:357
  1575.0 149.6 %reduce-scatter.18.cloned.1.call-done = f32[64,512]{1,0:T(8,128)} async-done(((f32[2048,512]{1,0:T(8,128)}), f32[64,512]{1,0:T(8,128)}) %reduce-scatter.18.cloned.1.call-update) | async-done | bytes 131088 | tf_op jit(solution)/shard_map/reduce_scatter | solution.py:358
  1724.6 713.6 %reduce-scatter.14.cloned.1.call-done = f32[64,4096]{1,0:T(8,128)} async-done(((f32[2048,4096]{1,0:T(8,128)}), f32[64,4096]{1,0:T(8,128)}) %reduce-scatter.14.cloned.1.call-update) | async-done | bytes 1048592 | tf_op jit(solution)/shard_map/reduce_scatter | solution.py:356
  2438.2 714.3 %reduce-scatter.20.cloned.1.call-done = f32[128,2048]{1,0:T(8,128)} async-done(((f32[4096,2048]{1,0:T(8,128)}), f32[128,2048]{1,0:T(8,128)}) %reduce-scatter.20.cloned.1.call-update) | async-done | bytes 1048592 | tf_op jit(solution)/shard_map/reduce_scatter | solution.py:359
  (364 shorter events, 383.8 us)
Async XLA Ops:
  7.2 789.7 %copy-start = (bf16[1,768,2048]{2,1,0:T(8,128)(2,1)S(1)}, bf16[1,768,2048]{2,1,0:T(8,128)(2,1)}, u32[]{:S(2)}) copy-start(bf16[1,768,2048]{2,1,0:T(8,128)(2,1)} %param.33) | copy-start | bytes 9437188
  7.2 63.0 %all-gather.14.cloned.1.call-start = ((), (), s32[]{:S(2)}) async-start(), calls=%async_computation.14 | async-start | bytes 2162688 | tf_op jit(solution)/shard_map/all_gather | solution.py:99
  7.9 120.6 %all-gather.8.cloned.1.call-start = ((), (), s32[]{:S(2)}) async-start(), calls=%async_computation.11 | async-start | bytes 2162688 | tf_op jit(solution)/shard_map/all_gather | solution.py:98
  8.7 144.8 %all-gather.16.cloned.1.call-start = ((), (), s32[]{:S(2)}) async-start(), calls=%async_computation.15 | async-start | bytes 1179648 | tf_op jit(solution)/shard_map/all_gather | solution.py:175
  54.5 238.1 %copy-start.34 = (f32[2048]{0:T(1024)}, f32[2048]{0:T(1024)S(1)}, u32[]{:S(2)}) copy-start(f32[2048]{0:T(1024)S(1)} %convert_element_type.204) | copy-start | bytes 24580
  55.9 236.7 %copy-start.45 = (f32[128]{0:T(128)}, f32[128]{0:T(128)S(1)}, u32[]{:S(2)}) copy-start(f32[128]{0:T(128)S(1)} %fusion.122) | copy-start | bytes 1540
  73.1 198.0 %all-gather.12.cloned.1.call-start = ((), (), s32[]{:S(2)}) async-start(), calls=%async_computation.13 | async-start | bytes 17301504 | tf_op jit(solution)/shard_map/all_gather | solution.py:97
  73.7 232.8 %all-gather.10.cloned.1.call-start = ((), (), s32[]{:S(2)}) async-start(), calls=%async_computation.12 | async-start | bytes 1179648 | tf_op jit(solution)/shard_map/all_gather | solution.py:174
  74.0 228.8 %copy-start.28 = (f32[128,64]{0,1:T(8,128)}, f32[128,64]{0,1:T(8,128)S(1)}, u32[]{:S(2)}) copy-start(f32[128,64]{0,1:T(8,128)S(1)} %get-tuple-element.884) | copy-start | bytes 98308
  74.0 228.8 %copy-start.31 = (f32[128,64]{0,1:T(8,128)}, f32[128,64]{0,1:T(8,128)S(1)}, u32[]{:S(2)}) copy-start(f32[128,64]{0,1:T(8,128)S(1)} %get-tuple-element.885) | copy-start | bytes 98308
  136.6 276.5 %all-gather.18.cloned.1.call-start = ((), (), s32[]{:S(2)}) async-start(), calls=%async_computation.16 | async-start | bytes 17301504 | tf_op jit(solution)/shard_map/all_gather | solution.py:100
  137.5 163.6 %copy-start.52 = (f32[128]{0:T(128)}, f32[128]{0:T(128)S(1)}, u32[]{:S(2)}) copy-start(f32[128]{0:T(128)S(1)} %convert_element_type.211) | copy-start | bytes 1540
  434.2 221.7 %all-to-all-start = ((bf16[32,48,2048]{2,1,0:T(8,128)(2,1)}), bf16[32,48,2048]{2,1,0:T(8,128)(2,1)}, u32[]{:S(2)}, u32[]{:S(2)}) async-start(bf16[32,48,2048]{2,1,0:T(8,128)(2,1)} %bitcast.389), calls=%async_computation | async-start | bytes 12582912 | tf_op jit(solution)/shard_map/all_to_all | solution.py:76
  655.9 140.9 %all-to-all-start.2 = ((bf16[32,48,2048]{2,1,0:T(8,128)(2,1)}), bf16[32,48,2048]{2,1,0:T(8,128)(2,1)}, u32[]{:S(2)}, u32[]{:S(2)}) async-start(bf16[32,48,2048]{2,1,0:T(8,128)(2,1)} %bitcast.390), calls=%async_computation.2 | async-start | bytes 12582912 | tf_op jit(solution)/shard_map/all_to_all | solution.py:76
  827.3 144.2 %all-to-all-start.3 = ((bf16[32,48,2048]{2,1,0:T(8,128)(2,1)}), bf16[32,48,2048]{2,1,0:T(8,128)(2,1)}, u32[]{:S(2)}, u32[]{:S(2)}) async-start(bf16[32,48,2048]{2,1,0:T(8,128)(2,1)} %bitcast.403), calls=%async_computation.3 | async-start | bytes 12582912 | tf_op jit(solution)/shard_map/all_to_all | solution.py:76
  971.5 144.0 %all-to-all-start.1 = ((bf16[32,48,2048]{2,1,0:T(8,128)(2,1)}), bf16[32,48,2048]{2,1,0:T(8,128)(2,1)}, u32[]{:S(2)}, u32[]{:S(2)}) async-start(bf16[32,48,2048]{2,1,0:T(8,128)(2,1)} %bitcast.402), calls=%async_computation.1 | async-start | bytes 12582912 | tf_op jit(solution)/shard_map/all_to_all | solution.py:76
  978.5 271.6 %reduce-scatter.22.cloned.1.call-start = ((), (), s32[]{:S(2)}) async-start(), calls=%async_computation.21 | async-start | bytes 1179648
  1211.6 78.3 %reduce-scatter.24.cloned.1.call-start = ((), (), s32[]{:S(2)}) async-start(), calls=%async_computation.22 | async-start | bytes 1179648
  1214.1 213.8 %reduce-scatter.26.cloned.1.call-start = ((), (), s32[]{:S(2)}) async-start(), calls=%async_computation.23 | async-start | bytes 1081344
  1215.5 359.6 %reduce-scatter.16.cloned.1.call-start = ((), (), s32[]{:S(2)}) async-start(), calls=%async_computation.18 | async-start | bytes 4325376 | tf_op jit(solution)/shard_map/reduce_scatter | solution.py:357
  1255.6 469.0 %reduce-scatter.18.cloned.1.call-start = ((), (), s32[]{:S(2)}) async-start(), calls=%async_computation.19 | async-start | bytes 4325376 | tf_op jit(solution)/shard_map/reduce_scatter | solution.py:358
  1293.6 1144.6 %reduce-scatter.14.cloned.1.call-start = ((), (), s32[]{:S(2)}) async-start(), calls=%async_computation.17 | async-start | bytes 34603008 | tf_op jit(solution)/shard_map/reduce_scatter | solution.py:356
  1313.9 1838.6 %reduce-scatter.20.cloned.1.call-start = ((), (), s32[]{:S(2)}) async-start(), calls=%async_computation.20 | async-start | bytes 34603008 | tf_op jit(solution)/shard_map/reduce_scatter | solution.py:359
  1429.3 1723.2 %copy-start.1 = (bf16[1,768,2048]{2,1,0:T(8,128)(2,1)S(1)}, bf16[1,768,2048]{2,1,0:T(8,128)(2,1)}, u32[]{:S(2)}) copy-start(bf16[1,768,2048]{2,1,0:T(8,128)(2,1)} %param.33) | copy-start | bytes 9437188
  (70 other events, 851.3 us)
Sparse Core Ops, SparseCore 0:
  11.0 59.1 all-gather.13
  73.1 55.3 all-gather.7
  131.0 22.4 all-gather.15
  156.3 114.8 all-gather.11
  273.5 21.7 all-gather.9
  298.1 114.8 all-gather.17
  1211.7 38.3 reduce-scatter.21
  1253.9 35.9 reduce-scatter.23
  1292.2 135.6 reduce-scatter.25
  1430.7 144.3 reduce-scatter.15
  1578.0 146.5 reduce-scatter.17
  1727.5 710.6 reduce-scatter.13
  2441.2 711.2 reduce-scatter.19
where the time goes:
time: 3160 us
  waiting for transfers between devices  2410 us (76%)
  blocking collectives  281 us (9%)
  matrix products  239 us (8%)
  local copies, waits for them, and re-layouts  118 us (4%)
  other arithmetic  68.5 us (2%)
    reduce_scatter x1, waiting for transfers between devices, on_device(): lax.psum_scatter(grad_output, ('ctx', 'exp'), scatter_dimension=0, tiled=...  714 us
    reduce_scatter x1, waiting for transfers between devices, on_device(): lax.psum_scatter(grad_query, ('ctx', 'exp'), scatter_dimension=0, tiled=T...  714 us
    all_to_all x4, waiting for transfers between devices, route(): lax.all_to_all(buffer, ('ctx', 'exp'), split_axis=0, concat_axis=0, tiled...  365 us
    all_gather x1, blocking collectives, on_device(): lax.all_gather(router_weight, ('ctx', 'exp'), axis=0, tiled=True)  201 us
    reduce_scatter x1, waiting for transfers between devices, on_device(): lax.psum_scatter(grad_value, ('ctx', 'exp'), scatter_dimension=0, tiled=T...  150 us
    unnamed x16, waiting for transfers between devices  126 us
    all_gather x1, waiting for transfers between devices, on_device(): lax.all_gather(query_weight, ('ctx', 'exp'), axis=0, tiled=True)  115 us
    reduce_scatter x1, waiting for transfers between devices, on_device(): lax.psum_scatter(grad_key, ('ctx', 'exp'), scatter_dimension=0, tiled=True)  95.9 us
  transfers between devices with their start and end apart: 17, of which 15 were waited for; matrix products, arithmetic and copies ran while one was open for 9% of the time, Pallas kernels for 0%

commit v1 on v0

v1 whole, which is shorter than its diff:
```python
import jax
import jax.numpy as jnp
import numpy as np
from jax import lax
from jax.experimental import pallas as pl
from jax.experimental.pallas import tpu as pltpu
from jax.sharding import PartitionSpec as P

D = 2048
H = 32
KVH = 4
HD = 128
TOP = 8
BLK = 256

EPSILON = 1e-06
ROPE_BASE = 1000000.0
SCALE = HD**-0.5
BF = jnp.bfloat16
F32 = jnp.float32
VMEM_LIMIT = 48 * 1024 * 1024


def rope_tables(rows):
    half = HD // 2
    freq = np.power(ROPE_BASE, np.arange(half) * (-2.0 / HD))
    angles = np.arange(rows)[:, None] * freq[None, :]
    cos, sin = np.cos(angles), np.sin(angles)
    return (
        np.concatenate([cos, cos], axis=1).astype(np.float32),
        np.concatenate([-sin, sin], axis=1).astype(np.float32),
    )


def inv_rms(values):
    return lax.rsqrt(jnp.mean(values * values, axis=-1, keepdims=True) + EPSILON)


def nt_dot(a, b):
    return lax.dot_general(a, b, (((1,), (1,)), ((), ())), preferred_element_type=F32)


def tn_dot(a, b):
    return lax.dot_general(a, b, (((0,), (0,)), ((), ())), preferred_element_type=F32)


def mm(a, b):
    return jnp.dot(a, b, preferred_element_type=F32)


def spin(values, cos, sin):
    return values * cos + pltpu.roll(values, HD // 2, 1) * sin


def unspin(values, cos, sin):
    return values * cos - pltpu.roll(values, HD // 2, 1) * sin


def attn_forward_kernel(blocks, raw, kraw, vraw, cos_all, sin_all, cos, sin, qgain, kgain, out, keys, vals):
    head, block = pl.program_id(0), pl.program_id(1)

    @pl.when((head == 0) & (block == 0))
    def _():
        rows = kraw[...]
        keys[...] = spin(rows * inv_rms(rows) * kgain[...], cos_all[...], sin_all[...]).astype(BF)
        vals[...] = vraw[...].astype(BF)

    rows = raw[...]
    query = spin(rows * inv_rms(rows) * qgain[...], cos[...], sin[...]).astype(BF)
    for n in range(blocks):

        @pl.when(block == n)
        def _(n=n):
            span = (n + 1) * BLK
            weights = jnp.exp(nt_dot(query, keys[:span, :]) * SCALE)
            total = jnp.sum(weights, axis=-1, keepdims=True)
            probs = (weights * (1.0 / total)).astype(BF)
            out[...] = mm(probs, vals[:span, :]).astype(BF)


def attn_backward_kernel(
    blocks, raw, kraw, vraw, cos_all, sin_all, cos, sin, qgain, kgain, gout,
    gq, gk, gv, gqgain, keys, vals,
):
    head, block = pl.program_id(0), pl.program_id(1)

    @pl.when((head == 0) & (block == 0))
    def _():
        rows = kraw[...]
        keys[...] = spin(rows * inv_rms(rows) * kgain[...], cos_all[...], sin_all[...]).astype(BF)
        vals[...] = vraw[...].astype(BF)
        gk[...] = jnp.zeros_like(gk)
        gv[...] = jnp.zeros_like(gv)
        gqgain[...] = jnp.zeros_like(gqgain)

    rows = raw[...]
    inverse = inv_rms(rows)
    normed = rows * inverse
    query = spin(normed * qgain[...], cos[...], sin[...]).astype(BF)
    grad_out = gout[...]

    def finish(grad_query):
        turned = unspin(grad_query, cos[...], sin[...])
        gqgain[...] += jnp.sum(turned * normed, axis=0, keepdims=True)
        scaled = turned * qgain[...]
        mean = jnp.mean(scaled * normed, axis=-1, keepdims=True)
        gq[...] = (inverse * (scaled - normed * mean)).astype(BF)

    for n in range(blocks):

        @pl.when(block == n)
        def _(n=n):
            span = (n + 1) * BLK
            seen, values = keys[:span, :], vals[:span, :]
            weights = jnp.exp(nt_dot(query, seen) * SCALE)
            total = jnp.sum(weights, axis=-1, keepdims=True)
            probs = weights * (1.0 / total)
            grad_probs = nt_dot(grad_out, values)
            delta = jnp.sum(probs * grad_probs, axis=-1, keepdims=True)
            grad_scores = (probs * (grad_probs - delta)).astype(BF)
            gv[:span, :] += tn_dot(probs.astype(BF), grad_out)
            gk[:span, :] += tn_dot(grad_scores, query) * SCALE
            finish(mm(grad_scores, seen) * SCALE)


def key_backward_kernel(count, kraw, cos, sin, kgain, *rest):
    gks, gvs, (gk_low, gv_low, gkgain) = rest[:count], rest[count : 2 * count], rest[2 * count :]
    grad_keys, grad_vals = gks[0][...], gvs[0][...]
    for n in range(1, count):
        grad_keys = grad_keys + gks[n][...]
        grad_vals = grad_vals + gvs[n][...]
    rows = kraw[...]
    inverse = inv_rms(rows)
    normed = rows * inverse
    turned = unspin(grad_keys, cos[...], sin[...])
    gkgain[...] = jnp.sum(turned * normed, axis=0, keepdims=True)
    scaled = turned * kgain[...]
    mean = jnp.mean(scaled * normed, axis=-1, keepdims=True)
    gk_low[...] = (inverse * (scaled - normed * mean)).astype(BF)
    gv_low[...] = grad_vals.astype(BF)


def attn_specs(rows, heads):
    return [
        pl.BlockSpec((BLK, HD), lambda h, i: (i, h)),
        pl.BlockSpec((rows, HD), lambda h, i: (0, 0)),
        pl.BlockSpec((rows, HD), lambda h, i: (0, 0)),
        pl.BlockSpec((rows, HD), lambda h, i: (0, 0)),
        pl.BlockSpec((rows, HD), lambda h, i: (0, 0)),
        pl.BlockSpec((BLK, HD), lambda h, i: (i, 0)),
        pl.BlockSpec((BLK, HD), lambda h, i: (i, 0)),
        pl.BlockSpec((1, HD), lambda h, i: (0, 0)),
        pl.BlockSpec((1, HD), lambda h, i: (0, 0)),
    ]


def attn_forward(raw, kraw, vraw, cos, sin, qgain, kgain, heads):
    rows = raw.shape[0]
    blocks = rows // BLK
    return pl.pallas_call(
        lambda *refs: attn_forward_kernel(blocks, *refs),
        grid=(heads, blocks),
        in_specs=attn_specs(rows, heads),
        out_specs=pl.BlockSpec((BLK, HD), lambda h, i: (i, h)),
        out_shape=jax.ShapeDtypeStruct((rows, heads * HD), BF),
        scratch_shapes=[pltpu.VMEM((rows, HD), BF), pltpu.VMEM((rows, HD), BF)],
        compiler_params=pltpu.CompilerParams(vmem_limit_bytes=VMEM_LIMIT),
        name="attn_fw",
    )(raw, kraw, vraw, cos, sin, cos, sin, qgain, kgain)


def attn_backward(raw, kraw, vraw, cos, sin, qgain, kgain, gout, heads):
    rows = raw.shape[0]
    blocks = rows // BLK
    return pl.pallas_call(
        lambda *refs: attn_backward_kernel(blocks, *refs),
        grid=(heads, blocks),
        in_specs=attn_specs(rows, heads) + [pl.BlockSpec((BLK, HD), lambda h, i: (i, h))],
        out_specs=[
            pl.BlockSpec((BLK, HD), lambda h, i: (i, h)),
            pl.BlockSpec((rows, HD), lambda h, i: (0, 0)),
            pl.BlockSpec((rows, HD), lambda h, i: (0, 0)),
            pl.BlockSpec((1, HD), lambda h, i: (0, 0)),
        ],
        out_shape=[
            jax.ShapeDtypeStruct((rows, heads * HD), BF),
            jax.ShapeDtypeStruct((rows, HD), F32),
            jax.ShapeDtypeStruct((rows, HD), F32),
            jax.ShapeDtypeStruct((1, HD), F32),
        ],
        scratch_shapes=[pltpu.VMEM((rows, HD), BF), pltpu.VMEM((rows, HD), BF)],
        compiler_params=pltpu.CompilerParams(vmem_limit_bytes=VMEM_LIMIT),
        name="attn_bw",
    )(raw, kraw, vraw, cos, sin, cos, sin, qgain, kgain, gout)


def key_backward(kraw, cos, sin, kgain, gks, gvs):
    rows = kraw.shape[0]
    return pl.pallas_call(
        lambda *refs: key_backward_kernel(len(gks), *refs),
        out_shape=[
            jax.ShapeDtypeStruct((rows, HD), BF),
            jax.ShapeDtypeStruct((rows, HD), BF),
            jax.ShapeDtypeStruct((1, HD), F32),
        ],
        compiler_params=pltpu.CompilerParams(vmem_limit_bytes=VMEM_LIMIT),
        name="key_bw",
    )(kraw, cos, sin, kgain, *gks, *gvs)


def on_device(
    tokens,
    expert_ids,
    cotangent,
    attn_gain,
    ffn_gain,
    query_gain,
    key_gain,
    query_weight,
    key_weight,
    value_weight,
    output_weight,
    router_weight,
    gate_weight,
    up_weight,
    down_weight,
):
    both = ("ctx", "exp")
    nc, ne = lax.axis_size("ctx"), lax.axis_size("exp")
    ci, ei = lax.axis_index("ctx"), lax.axis_index("exp")
    count = nc * ne
    rows = tokens.shape[1]
    seq = rows * nc
    heads = H // nc
    width = heads * HD
    share = nc // KVH
    piece = 2 * HD // share
    member = ci % share
    experts = router_weight.shape[1]
    cap = max(2, rows * TOP * 3 // (2 * experts))
    slots = nc * cap
    wrows = query_weight.shape[0]
    gain_rows, head_rows = attn_gain.shape[0], query_gain.shape[0]

    def mate(values, bit):
        return lax.ppermute(values, "ctx", [(i, i ^ bit) for i in range(nc)])

    def along(values):
        return lax.ppermute(values, "exp", [(i, (i + 1) % ne) for i in range(ne)])

    def spread(values):
        return lax.all_to_all(values, "ctx", split_axis=0, concat_axis=0, tiled=True)

    packed = jnp.concatenate(
        [
            attn_gain,
            ffn_gain,
            query_gain,
            key_gain,
            router_weight.reshape(-1),
            expert_ids.astype(BF).reshape(-1),
        ]
    )
    table = lax.all_gather(packed, both, axis=0, tiled=False)
    cuts = np.cumsum([gain_rows, gain_rows, head_rows, head_rows, wrows * experts]).tolist()
    gain_attn = table[:, : cuts[0]].reshape(1, D).astype(F32)
    gain_ffn = table[:, cuts[0] : cuts[1]].reshape(1, D).astype(F32)
    gain_query = table[:, cuts[1] : cuts[2]].reshape(1, HD).astype(F32)
    gain_key = table[:, cuts[2] : cuts[3]].reshape(1, HD).astype(F32)
    router = table[:, cuts[3] : cuts[4]].reshape(D, experts)
    ids_ctx = lax.dynamic_slice_in_dim(
        table[:, cuts[4] :].reshape(nc, ne, rows, TOP), ci, 1, 0
    )[0].astype(jnp.int32)

    own_tokens = tokens[0]
    x_all = lax.all_gather(own_tokens, "ctx", axis=0, tiled=True)
    kv = jnp.concatenate(
        [key_weight.reshape(wrows, KVH, HD), value_weight.reshape(wrows, KVH, HD)], axis=2
    ).reshape(wrows, nc, piece)
    part = jnp.concatenate([query_weight.reshape(wrows, nc, width), kv], axis=2)
    part = spread(part.transpose(1, 0, 2))
    w_in = (
        lax.all_gather(part, "exp", axis=0, tiled=False)
        .transpose(1, 0, 2, 3)
        .reshape(D, width + piece)
    )
    w_out = lax.all_gather(output_weight, "exp", axis=0, tiled=True)

    plane_ids = lax.iota(jnp.int32, nc) * ne + ei
    lower = (
        lax.broadcasted_iota(jnp.int32, (rows, rows), 0)
        > lax.broadcasted_iota(jnp.int32, (rows, rows), 1)
    ).astype(BF)
    picks = []
    for step in range(ne):
        ids = lax.dynamic_index_in_dim(ids_ctx, (ei - step) % ne, 0, keepdims=False)
        named = jnp.any(ids[:, :, None] == plane_ids[None, None, :], axis=1)
        rank = mm(lower, named.astype(BF)).astype(jnp.int32)
        place = jnp.where(named, rank, -1).T
        picks.append(
            (place[:, None, :] == lax.iota(jnp.int32, cap)[None, :, None])
            .astype(BF)
            .reshape(slots, rows)
        )

    def ring(values):
        chain = [values]
        for _ in range(1, ne):
            chain.append(along(chain[-1]))
        return chain

    def dispatch(step, values):
        return spread(mm(picks[step], values).astype(BF).reshape(nc, cap, D)).reshape(slots, D)

    cot_rows = [dispatch(step, values) for step, values in enumerate(ring(cotangent[0]))]

    cos, sin = (jnp.asarray(v) for v in rope_tables(seq))
    x_f32 = x_all.astype(F32)
    xa = (x_f32 * inv_rms(x_f32) * gain_attn).astype(BF)
    raw = mm(xa, w_in)
    q_raw = raw[:, :width]
    kv_own = raw[:, width:]
    kv_parts = [kv_own] + [mate(kv_own, bit) for bit in range(1, share)]
    ordered = []
    for spot in range(share):
        chosen = kv_parts[spot]
        for m in range(1, share):
            chosen = jnp.where(member == m, kv_parts[spot ^ m], chosen)
        ordered.append(chosen)
    kv_raw = jnp.concatenate(ordered, axis=1) if share > 1 else ordered[0]
    k_raw, v_raw = kv_raw[:, :HD], kv_raw[:, HD:]
    attn = attn_forward(q_raw, k_raw, v_raw, cos, sin, gain_query, gain_key, heads)
    branch = mm(attn, w_out).astype(BF)
    inputs = own_tokens.astype(F32)
    residual = inputs + lax.psum_scatter(
        branch, "ctx", scatter_dimension=0, tiled=True
    ).astype(F32)
    inv_res = inv_rms(residual)
    normed_res = residual * inv_res
    ffn_in = (normed_res * gain_ffn).astype(BF)

    def gates_of(values, ids):
        logits = mm(values, router)
        chosen = jnp.any(ids[:, :, None] == lax.iota(jnp.int32, experts)[None, None, :], axis=1)
        top = jnp.max(jnp.where(chosen, logits, -jnp.inf), axis=-1, keepdims=True)
        raised = jnp.where(chosen, jnp.exp(jnp.where(chosen, logits - top, 0.0)), 0.0)
        return raised / jnp.sum(raised, axis=-1, keepdims=True)

    w_gate, w_up, w_down = gate_weight[0], up_weight[0], down_weight[0]
    ffn_chain = ring(ffn_in)
    gates_home = None
    gate_sends = []
    for step, values in enumerate(ffn_chain):
        ids = lax.dynamic_index_in_dim(ids_ctx, (ei - step) % ne, 0, keepdims=False)
        gates = gates_of(values, ids)
        if step == 0:
            gates_home = gates
        plane = lax.dynamic_index_in_dim(gates.reshape(rows, nc, ne), ei, 2, keepdims=False)
        gate_sends.append(
            jnp.sum(
                picks[step].reshape(nc, cap, rows).astype(F32) * plane.T[:, None, :], axis=-1
            )
        )
    ffn_rows = [dispatch(step, values) for step, values in enumerate(ffn_chain)]
    gate_rows = spread(jnp.stack(gate_sends, axis=1))

    hidden_g, act_gate, act_up, back_rows, mix_rows, score_rows = [], [], [], [], [], []
    for step in range(ne):
        gate_vec = gate_rows[:, step].reshape(slots, 1)
        gate_act = mm(ffn_rows[step], w_gate)
        up_act = mm(ffn_rows[step], w_up)
        sig = jax.nn.sigmoid(gate_act)
        silu = gate_act * sig
        hidden = silu * up_act
        hidden_low = hidden.astype(BF)
        upstream = nt_dot(cot_rows[step], w_down)
        score_rows.append(jnp.sum(upstream * hidden_low.astype(F32), axis=-1).reshape(nc, cap))
        grad_hidden = upstream * gate_vec
        grad_gate_low = (grad_hidden * up_act * sig * (1.0 + gate_act * (1.0 - sig))).astype(BF)
        grad_up_low = (grad_hidden * silu).astype(BF)
        back_rows.append((nt_dot(grad_gate_low, w_gate) + nt_dot(grad_up_low, w_up)).astype(BF))
        mix_rows.append((mm(hidden_low, w_down) * gate_vec).astype(BF))
        hidden_g.append((hidden_low.astype(F32) * gate_vec).astype(BF))
        act_gate.append(grad_gate_low)
        act_up.append(grad_up_low)

    score_back = spread(jnp.stack(score_rows, axis=1))
    order = list(range(1, ne)) + [0]

    def collect(chunks):
        total = None
        for step in order:
            home = spread(chunks[step].reshape(nc, cap, D)).reshape(slots, D)
            part_sum = tn_dot(picks[step], home)
            total = part_sum if total is None else part_sum + along(total.astype(BF)).astype(F32)
        return total

    grad_ffn_experts = collect(back_rows)
    mixture = collect(mix_rows)
    layer_out = (residual + mixture).astype(BF)[None]

    def tokens_of(step):
        return jnp.sum(
            picks[step].reshape(nc, cap, rows).astype(F32)
            * score_back[:, step].reshape(nc, cap, 1),
            axis=1,
        )

    scores = [tokens_of(step) for step in range(ne)]
    planes = [scores[0]]
    for step in range(1, ne):
        planes.append(
            lax.ppermute(scores[step], "exp", [(i, (i - step) % ne) for i in range(ne)])
        )
    grad_gates = jnp.zeros((ne, nc, rows), F32)
    for step in range(ne):
        grad_gates = lax.dynamic_update_slice_in_dim(
            grad_gates, planes[step][None], (ei + step) % ne, 0
        )
    grad_gates = grad_gates.transpose(2, 1, 0).reshape(rows, experts)
    grad_logits = gates_home * (
        grad_gates - jnp.sum(gates_home * grad_gates, axis=-1, keepdims=True)
    )
    grad_logits_low = grad_logits.astype(BF)
    grad_router = tn_dot(ffn_in, grad_logits_low)
    grad_ffn_in = grad_ffn_experts + nt_dot(grad_logits_low, router)
    grad_gain_ffn = jnp.sum(grad_ffn_in * normed_res, axis=0)
    scaled = grad_ffn_in * gain_ffn
    grad_residual = cotangent[0].astype(F32) + inv_res * (
        scaled - normed_res * jnp.mean(scaled * normed_res, axis=-1, keepdims=True)
    )

    grad_branch = lax.all_gather(grad_residual.astype(BF), "ctx", axis=0, tiled=True)
    grad_attn = nt_dot(grad_branch, w_out).astype(BF)
    grad_q_low, grad_k, grad_v, grad_gain_query = attn_backward(
        q_raw, k_raw, v_raw, cos, sin, gain_query, gain_key, grad_attn, heads
    )
    gks = [grad_k] + [mate(grad_k, bit) for bit in range(1, share)]
    gvs = [grad_v] + [mate(grad_v, bit) for bit in range(1, share)]
    grad_k_low, grad_v_low, grad_gain_key = key_backward(k_raw, cos, sin, gain_key, gks, gvs)
    grad_gain_key = jnp.where(member == 0, grad_gain_key, 0.0)
    grad_kv = jnp.concatenate([grad_k_low, grad_v_low], axis=1)
    if share > 1:
        grad_kv = lax.dynamic_slice_in_dim(grad_kv, member * piece, piece, 1)
    grad_in = jnp.concatenate([grad_q_low, grad_kv], axis=1)
    grad_xa = lax.psum_scatter(
        nt_dot(grad_in, w_in).astype(BF), "ctx", scatter_dimension=0, tiled=True
    ).astype(F32)
    inv_in = inv_rms(inputs)
    normed_in = inputs * inv_in
    scaled_in = grad_xa * gain_attn
    grad_tokens = (
        grad_residual
        + inv_in
        * (scaled_in - normed_in * jnp.mean(scaled_in * normed_in, axis=-1, keepdims=True))
    )[None]

    all_rows = jnp.concatenate(ffn_rows)
    grad_gate = tn_dot(all_rows, jnp.concatenate(act_gate))
    grad_up = tn_dot(all_rows, jnp.concatenate(act_up))
    grad_down = tn_dot(jnp.concatenate(hidden_g), jnp.concatenate(cot_rows))

    grad_output = lax.psum_scatter(
        tn_dot(attn, grad_branch).astype(BF), "exp", scatter_dimension=0, tiled=True
    ).astype(F32)
    grad_w = tn_dot(xa, grad_in).astype(BF).reshape(nc, ne, wrows, width + piece)
    grad_w = lax.psum_scatter(
        grad_w.transpose(1, 0, 2, 3), "exp", scatter_dimension=0, tiled=True
    )[0]
    grad_w = spread(grad_w).astype(F32)
    sum_query = grad_w[:, :, :width].transpose(1, 0, 2).reshape(wrows, H * HD)
    sum_kv = grad_w[:, :, width:].transpose(1, 0, 2).reshape(wrows, KVH, 2 * HD)
    sum_key = sum_kv[:, :, :HD].reshape(wrows, KVH * HD)
    sum_value = sum_kv[:, :, HD:].reshape(wrows, KVH * HD)
    sum_attn_gain = (
        jnp.sum(sum_query * query_weight.astype(F32), axis=1)
        + jnp.sum(sum_key * key_weight.astype(F32), axis=1)
        + jnp.sum(sum_value * value_weight.astype(F32), axis=1)
    ) / attn_gain.astype(F32)

    small = jnp.concatenate(
        [
            grad_router.reshape(count, wrows * experts),
            grad_gain_ffn.reshape(count, gain_rows),
            grad_gain_query.reshape(count, head_rows),
            grad_gain_key.reshape(count, head_rows),
        ],
        axis=1,
    )
    small = jnp.sum(
        lax.all_to_all(small, both, split_axis=0, concat_axis=0, tiled=True), axis=0
    )
    ends = np.cumsum([wrows * experts, gain_rows, head_rows, head_rows]).tolist()
    return (
        layer_out,
        grad_tokens,
        sum_attn_gain,
        small[ends[0] : ends[1]],
        small[ends[1] : ends[2]],
        small[ends[2] : ends[3]],
        sum_query,
        sum_key,
        sum_value,
        grad_output,
        small[: ends[0]].reshape(wrows, experts),
        grad_gate[None],
        grad_up[None],
        grad_down[None],
    )


def solution(mesh):
    shard = ("ctx", "exp")
    rows = P("exp", "ctx", None)
    vector, matrix, stack = P(shard), P(shard, None), P(shard, None, None)
    return jax.shard_map(
        on_device,
        mesh=mesh,
        in_specs=(rows,) * 3 + (vector,) * 4 + (matrix,) * 5 + (stack,) * 3,
        out_specs=(rows,) * 2 + (vector,) * 4 + (matrix,) * 5 + (stack,) * 3,
        check_vma=False,
    )
```

time: 3160 us -> 923 us (0.29)
  waiting for transfers between devices: 2410 us -> 433 us
  blocking collectives: 281 us -> 7.07 us
  starting transfers between devices: 23.1 us -> 115 us
  local copies, waits for them, and re-layouts: 118 us -> 47.3 us
  Pallas kernels: 0 us -> 38.2 us
  matrix products: 239 us -> 201 us
    reduce_scatter x4, waiting for transfers between devices: 1670 us -> 15.4 us  [the longest x1 10 us: on_device(): lax.psum_scatter(branch, 'ctx', scatter_dimension=0, tiled=True).astype(F32)]
    all_to_all x4 -> x20, waiting for transfers between devices: 365 us -> 143 us  [the longest x19 143 us: spread(): lax.all_to_all(values, 'ctx', split_axis=0, concat_axis=0, tiled=True)]
    all_gather x6 -> x4, waiting for transfers between devices: 249 us -> 34.8 us  [the longest x1 34.8 us: on_device(): lax.all_gather(grad_residual.astype(BF), 'ctx', axis=0, tiled=True)]
    all_gather x1 -> x0, blocking collectives: 201 us -> none  [on_device(): lax.all_gather(router_weight, ('ctx', 'exp'), axis=0, tiled=True)]
    unnamed x2 -> x0, blocking collectives: 80.3 us -> none
    all_to_all x4 -> x20, starting transfers between devices: 22.1 us -> 91.3 us  [the longest x19 85 us: spread(): lax.all_to_all(values, 'ctx', split_axis=0, concat_axis=0, tiled=True)]
    unnamed x16 -> x10, waiting for transfers between devices: 126 us -> 185 us
    ppermute x0 -> x18, waiting for transfers between devices: none -> 54.7 us  [the longest x12 40.1 us: along(): return lax.ppermute(values, 'exp', [(i, (i + 1) % ne) for i in range(ne)])]
  transfers between devices with their start and end apart: 17 -> 47, of which waited for: 15 -> 28; matrix products, arithmetic and copies ran while one was open for 9% -> 26% of each run, Pallas kernels for 0% -> 1%
where the time goes in v1:
time: 923 us; the launch traced here: 911 us
  waiting for transfers between devices  433 us (47%)
  matrix products  201 us (22%)
  starting transfers between devices  115 us (12%)
  other arithmetic  51.3 us (6%)
  local copies, waits for them, and re-layouts  47.3 us (5%)
  Pallas kernels  38.2 us (4%)
  between operations  17.3 us (2%)
    unnamed x10, waiting for transfers between devices  185 us
    all_to_all x19, waiting for transfers between devices, spread(): lax.all_to_all(values, 'ctx', split_axis=0, concat_axis=0, tiled=True)  143 us
    dot_general x30, matrix products, mm(): return jnp.dot(a, b, preferred_element_type=F32)  88.6 us
    all_to_all x19, starting transfers between devices, spread(): lax.all_to_all(values, 'ctx', split_axis=0, concat_axis=0, tiled=True)  85 us
    dot_general x14, matrix products, tn_dot(): lax.dot_general(a, b, (((0,), (0,)), ((), ())), preferred_element_type=F32)  65.7 us
    dot_general x15, matrix products, nt_dot(): lax.dot_general(a, b, (((1,), (1,)), ((), ())), preferred_element_type=F32)  47.1 us
    ppermute x12, waiting for transfers between devices, along(): return lax.ppermute(values, 'exp', [(i, (i + 1) % ne) for i in range(ne)])  40.1 us
    all_gather x1, waiting for transfers between devices, on_device(): lax.all_gather(grad_residual.astype(BF), 'ctx', axis=0, tiled=True)  34.8 us
  transfers between devices with their start and end apart: 47, of which 28 were waited for; matrix products, arithmetic and copies ran while one was open for 26% of the time, Pallas kernels for 1%

profile of v1, /device:TPU:0, one launch (start us, length us, event | category | flops | bytes accessed | tf_op | source)
XLA Modules:
  0.0 910.8 jit_solution(4857844556607651114)
XLA Ops:
  19.2 9.5 %all-to-all-done = bf16[8,64,640]{2,1,0:T(8,128)(2,1)} async-done(((bf16[8,64,640]{2,1,0:T(8,128)(2,1)}), bf16[8,64,640]{2,1,0:T(8,128)(2,1)}, u32[]{:S(2)}, u32[]{:S(2)}) %all-to-all-start) | async-done | bytes 655392 | tf_op jit(solution)/shard_map/all_to_all | solution.py:252
  30.0 183.9 %all-reduce.3.cloned.1.call-done = bf16[102656]{0:T(1024)(128)(2,1)} async-done(((bf16[102656]{0:T(1024)(128)(2,1)}), bf16[102656]{0:T(1024)(128)(2,1)}) %all-reduce.3.cloned.1.call-update) | async-done | bytes 205328
  234.2 12.9 %attn_fw.1 = bf16[1024,512]{1,0:T(8,128)(2,1)S(1)} custom-call(f32[1024,512]{1,0:T(8,128)S(1)} %slice.97.refs_0_, f32[1024,128]{1,0:T(8,128)S(1)} %get-tuple-element.173.refs_1_.refs_0_, f32[1024,128]{1,0:T(8,128)S(1)} %get-tuple-element.172.refs_2_, f32[1024,128]{1,0:T(8,128)S(1)} %copy-done.5, f32[1024,128]{1,0:T(8,128)S(1)} %copy-done.2, ...), custom_call_target="tpu_custom_call" | custom-call | tf_op jit(solution)/shard_map/attn_fw/pallas_call | solution.py:160
  279.7 11.8 %collective-permute-done.8 = bf16[128,2048]{1,0:T(8,128)(2,1)} collective-permute-done((bf16[128,2048]{1,0:T(8,128)(2,1)}, bf16[128,2048]{1,0:T(8,128)(2,1)}, u32[]{:S(2)}, u32[]{:S(2)}) %collective-permute-start.8) | collective-permute-done | bytes 524320 | tf_op jit(solution)/shard_map/ppermute | solution.py:249
  297.1 9.6 %all-to-all-done.10 = bf16[8,48,2048]{2,1,0:T(8,128)(2,1)} async-done(((bf16[8,48,2048]{2,1,0:T(8,128)(2,1)}), bf16[8,48,2048]{2,1,0:T(8,128)(2,1)}, u32[]{:S(2)}, u32[]{:S(2)}) %all-to-all-start.10) | async-done | bytes 1572896 | tf_op jit(solution)/shard_map/all_to_all | solution.py:252
  313.8 10.0 %reduce-scatter.5.cloned.1.call-done = bf16[128,2048]{1,0:T(8,128)(2,1)} async-done(((bf16[1024,2048]{1,0:T(8,128)(2,1)}), bf16[128,2048]{1,0:T(8,128)(2,1)}) %reduce-scatter.5.cloned.1.call-update) | async-done | bytes 524304 | tf_op jit(solution)/shard_map/reduce_scatter | solution.py:335
  353.0 12.2 %all-to-all-done.1 = bf16[8,48,2048]{2,1,0:T(8,128)(2,1)} async-done(((bf16[8,48,2048]{2,1,0:T(8,128)(2,1)}), bf16[8,48,2048]{2,1,0:T(8,128)(2,1)}, u32[]{:S(2)}, u32[]{:S(2)}) %all-to-all-start.1) | async-done | bytes 1572896 | tf_op jit(solution)/shard_map/all_to_all | solution.py:252
  379.3 11.2 %all-to-all-done.14 = bf16[8,48,2048]{2,1,0:T(8,128)(2,1)} async-done(((bf16[8,48,2048]{2,1,0:T(8,128)(2,1)}), bf16[8,48,2048]{2,1,0:T(8,128)(2,1)}, u32[]{:S(2)}, u32[]{:S(2)}) %all-to-all-start.14) | async-done | bytes 1572896 | tf_op jit(solution)/shard_map/all_to_all | solution.py:252
  405.0 10.9 %all-to-all-done.8 = bf16[8,48,2048]{2,1,0:T(8,128)(2,1)} async-done(((bf16[8,48,2048]{2,1,0:T(8,128)(2,1)}), bf16[8,48,2048]{2,1,0:T(8,128)(2,1)}, u32[]{:S(2)}, u32[]{:S(2)}) %all-to-all-start.8) | async-done | bytes 1572896 | tf_op jit(solution)/shard_map/all_to_all | solution.py:252
  432.0 9.4 %all-to-all-done.6 = bf16[8,48,2048]{2,1,0:T(8,128)(2,1)} async-done(((bf16[8,48,2048]{2,1,0:T(8,128)(2,1)}), bf16[8,48,2048]{2,1,0:T(8,128)(2,1)}, u32[]{:S(2)}, u32[]{:S(2)}) %all-to-all-start.6) | async-done | bytes 1572896 | tf_op jit(solution)/shard_map/all_to_all | solution.py:252
  459.3 7.5 all-to-all-done.4
  537.8 12.3 %all-to-all-done.13 = bf16[8,48,2048]{2,1,0:T(8,128)(2,1)} async-done(((bf16[8,48,2048]{2,1,0:T(8,128)(2,1)}), bf16[8,48,2048]{2,1,0:T(8,128)(2,1)}, u32[]{:S(2)}, u32[]{:S(2)}) %all-to-all-start.13) | async-done | bytes 1572896 | tf_op jit(solution)/shard_map/all_to_all | solution.py:252
  563.3 12.1 %all-to-all-done.17 = bf16[8,48,2048]{2,1,0:T(8,128)(2,1)} async-done(((bf16[8,48,2048]{2,1,0:T(8,128)(2,1)}), bf16[8,48,2048]{2,1,0:T(8,128)(2,1)}, u32[]{:S(2)}, u32[]{:S(2)}) %all-to-all-start.17) | async-done | bytes 1572896 | tf_op jit(solution)/shard_map/all_to_all | solution.py:252
  593.0 7.8 all-to-all-done.15
  612.4 9.2 %collective-permute-done.13 = f32[8,128]{1,0:T(8,128)S(1)} collective-permute-done((f32[8,128]{1,0:T(8,128)S(1)}, f32[8,128]{1,0:T(8,128)S(1)}, u32[]{:S(2)}, u32[]{:S(2)}) %collective-permute-start.13) | collective-permute-done | bytes 4128 | tf_op jit(solution)/shard_map/ppermute | solution.py:413
  631.0 12.9 %collective-permute-done.12 = bf16[128,2048]{1,0:T(8,128)(2,1)} collective-permute-done((bf16[128,2048]{1,0:T(8,128)(2,1)}, bf16[128,2048]{1,0:T(8,128)(2,1)}, u32[]{:S(2)}, u32[]{:S(2)}) %collective-permute-start.12) | collective-permute-done | bytes 524320 | tf_op jit(solution)/shard_map/ppermute | solution.py:249
  647.9 34.8 %all-gather.10.cloned.1.call-done = bf16[1024,2048]{1,0:T(8,128)(2,1)} async-done(((bf16[128,2048]{1,0:T(8,128)(2,1)}), bf16[1024,2048]{1,0:T(8,128)(2,1)}) %all-gather.10.cloned.1.call-update) | async-done | bytes 4194320 | tf_op jit(solution)/shard_map/all_gather | solution.py:433
  688.1 23.2 %attn_bw.1 = (bf16[1024,512]{1,0:T(8,128)(2,1)S(1)}, f32[1024,128]{1,0:T(8,128)}, f32[1024,128]{1,0:T(8,128)}, f32[1,128]{1,0:T(1,128)S(1)}) custom-call(f32[1024,512]{1,0:T(8,128)} %copy-done.1, f32[1024,128]{1,0:T(8,128)S(1)} %copy-done.9, f32[1024,128]{1,0:T(8,128)S(1)} %copy-done.12, f32[1024,128]{1,0:T(8,128)S(1)} %copy-done.6, ...), custom_call_target="tpu_custom_call" | custom-call | tf_op jit(solution)/shard_map/attn_bw/pallas_call | solution.py:175
  746.8 10.9 %all-to-all-done.3 = bf16[8,48,2048]{2,1,0:T(8,128)(2,1)} async-done(((bf16[8,48,2048]{2,1,0:T(8,128)(2,1)}), bf16[8,48,2048]{2,1,0:T(8,128)(2,1)}, u32[]{:S(2)}, u32[]{:S(2)}) %all-to-all-start.3) | async-done | bytes 1572896 | tf_op jit(solution)/shard_map/all_to_all | solution.py:252
  770.3 12.7 %all-to-all-done.9 = bf16[8,48,2048]{2,1,0:T(8,128)(2,1)} async-done(((bf16[8,48,2048]{2,1,0:T(8,128)(2,1)}), bf16[8,48,2048]{2,1,0:T(8,128)(2,1)}, u32[]{:S(2)}, u32[]{:S(2)}) %all-to-all-start.9) | async-done | bytes 1572896 | tf_op jit(solution)/shard_map/all_to_all | solution.py:252
  787.4 10.2 %convolution_bitcast_fusion.1 = f32[1,2048,768]{2,1,0:T(8,128)} fusion(bf16[384,768]{1,0:T(8,128)(2,1)} %copy-done.31, bf16[384,768]{1,0:T(8,128)(2,1)} %copy-done.35, bf16[384,768]{1,0:T(8,128)(2,1)} %copy-done.33, bf16[384,768]{1,0:T(8,128)(2,1)} %copy-done.36, bf16[384,2048]{1,0:T(8,128)(2,1)} %bitcast.41, bf16[384,2048]{1,0:T(8,128)(2,1)} %bitcast.46, ...), kind=kOutput, calls=%fused_computation.16 | convolution fusion | flops 4866441216 | bytes 14942208 | tf_op jit(solution)/shard_map/dot_general | solution.py:44
  814.9 9.6 %convolution_bitcast_fusion = f32[1,2048,768]{2,1,0:T(8,128)} fusion(bf16[384,768]{1,0:T(8,128)(2,1)} %copy-done.29, bf16[384,768]{1,0:T(8,128)(2,1)} %copy-done.32, bf16[384,768]{1,0:T(8,128)(2,1)} %copy-done.30, bf16[384,768]{1,0:T(8,128)(2,1)} %copy-done.34, bf16[384,2048]{1,0:T(8,128)(2,1)} %bitcast.41, bf16[384,2048]{1,0:T(8,128)(2,1)} %bitcast.46, ...), kind=kOutput, calls=%fused_computation.15 | convolution fusion | flops 4866441216 | bytes 14942208 | tf_op jit(solution)/shard_map/dot_general | solution.py:44
  824.6 12.4 %collective-permute-done.4 = bf16[128,2048]{1,0:T(8,128)(2,1)} collective-permute-done((bf16[128,2048]{1,0:T(8,128)(2,1)}, bf16[128,2048]{1,0:T(8,128)(2,1)}, u32[]{:S(2)}, u32[]{:S(2)}) %collective-permute-start.4) | collective-permute-done | bytes 524320 | tf_op jit(solution)/shard_map/ppermute | solution.py:249
  849.6 10.1 %fusion.11 = f32[1,768,2048]{2,1,0:T(8,128)} fusion(bf16[384,2048]{1,0:T(8,128)(2,1)} %bitcast.62, bf16[384,2048]{1,0:T(8,128)(2,1)} %bitcast.66, bf16[384,2048]{1,0:T(8,128)(2,1)} %bitcast.70, bf16[384,2048]{1,0:T(8,128)(2,1)} %bitcast.58, bf16[384,768]{1,0:T(8,128)(2,1)} %get-tuple-element.203, bf16[384,768]{1,0:T(8,128)(2,1)} %get-tuple-element.202, ...), kind=kOutput, calls=%fused_computation.14 | convolution fusion | flops 4866441216 | bytes 14942208 | tf_op jit(solution)/shard_map/dot_general | solution.py:44
  (402 shorter events, 426.4 us)
Async XLA Ops:
  17.5 196.4 %all-reduce.3.cloned.1.call-start = ((), (), s32[]{:S(2)}) async-start(), calls=%async_computation.33 | async-start | bytes 413696
  19.2 196.2 %all-gather.14.cloned.1.call-start = ((), (), s32[]{:S(2)}) async-start(), calls=%async_computation.32 | async-start | bytes 3276800 | tf_op jit(solution)/shard_map/all_gather | solution.py:283
  28.8 190.1 %all-gather.12.cloned.1.call-start = ((), (), s32[]{:S(2)}) async-start(), calls=%async_computation.31 | async-start | bytes 4718592 | tf_op jit(solution)/shard_map/all_gather | solution.py:276
  29.3 220.3 %all-gather.8.cloned.1.call-start = ((), (), s32[]{:S(2)}) async-start(), calls=%async_computation.25 | async-start | bytes 2621440 | tf_op jit(solution)/shard_map/all_gather | solution.py:287
  29.9 293.9 %reduce-scatter.5.cloned.1.call-start = ((), (), s32[]{:S(2)}) async-start(), calls=%async_computation.26 | async-start | bytes 4718592 | tf_op jit(solution)/shard_map/reduce_scatter | solution.py:335
  270.2 36.5 %all-to-all-start.10 = ((bf16[8,48,2048]{2,1,0:T(8,128)(2,1)}), bf16[8,48,2048]{2,1,0:T(8,128)(2,1)}, u32[]{:S(2)}, u32[]{:S(2)}) async-start(bf16[8,48,2048]{2,1,0:T(8,128)(2,1)} %bitcast.317), calls=%async_computation.11 | async-start | bytes 3145728 | tf_op jit(solution)/shard_map/all_to_all | solution.py:252
  306.7 30.3 %all-to-all-start.16 = ((bf16[8,48,2048]{2,1,0:T(8,128)(2,1)}), bf16[8,48,2048]{2,1,0:T(8,128)(2,1)}, u32[]{:S(2)}, u32[]{:S(2)}) async-start(bf16[8,48,2048]{2,1,0:T(8,128)(2,1)} %bitcast.320), calls=%async_computation.17 | async-start | bytes 3145728 | tf_op jit(solution)/shard_map/all_to_all | solution.py:252
  337.0 28.2 %all-to-all-start.1 = ((bf16[8,48,2048]{2,1,0:T(8,128)(2,1)}), bf16[8,48,2048]{2,1,0:T(8,128)(2,1)}, u32[]{:S(2)}, u32[]{:S(2)}) async-start(bf16[8,48,2048]{2,1,0:T(8,128)(2,1)} %bitcast.319), calls=%async_computation.2 | async-start | bytes 3145728 | tf_op jit(solution)/shard_map/all_to_all | solution.py:252
  369.5 33.9 %collective-permute-start.3 = (bf16[128,2048]{1,0:T(8,128)(2,1)}, bf16[128,2048]{1,0:T(8,128)(2,1)}, u32[]{:S(2)}, u32[]{:S(2)}) collective-permute-start(bf16[128,2048]{1,0:T(8,128)(2,1)} %collective-permute-done.2), channel_id=1, source_target_pairs={{0,1},{1,2},{2,3},{3,0},{4,5},{5,6},{6,7},{7,4},{8,9},{9,10},{10,1... | collective-permute-start | bytes 1572872 | tf_op jit(solution)/shard_map/ppermute | solution.py:249
  415.9 25.5 %all-to-all-start.6 = ((bf16[8,48,2048]{2,1,0:T(8,128)(2,1)}), bf16[8,48,2048]{2,1,0:T(8,128)(2,1)}, u32[]{:S(2)}, u32[]{:S(2)}) async-start(bf16[8,48,2048]{2,1,0:T(8,128)(2,1)} %bitcast.318), calls=%async_computation.7 | async-start | bytes 3145728 | tf_op jit(solution)/shard_map/all_to_all | solution.py:252
  466.7 25.4 %all-to-all-start.12 = ((bf16[8,48,2048]{2,1,0:T(8,128)(2,1)}), bf16[8,48,2048]{2,1,0:T(8,128)(2,1)}, u32[]{:S(2)}, u32[]{:S(2)}) async-start(bf16[8,48,2048]{2,1,0:T(8,128)(2,1)} %bitcast.314), calls=%async_computation.13 | async-start | bytes 3145728 | tf_op jit(solution)/shard_map/all_to_all | solution.py:252
  550.1 25.4 %all-to-all-start.17 = ((bf16[8,48,2048]{2,1,0:T(8,128)(2,1)}), bf16[8,48,2048]{2,1,0:T(8,128)(2,1)}, u32[]{:S(2)}, u32[]{:S(2)}) async-start(bf16[8,48,2048]{2,1,0:T(8,128)(2,1)} %bitcast.335), calls=%async_computation.18 | async-start | bytes 3145728 | tf_op jit(solution)/shard_map/all_to_all | solution.py:252
  600.7 28.2 %all-to-all-start.11 = ((bf16[8,48,2048]{2,1,0:T(8,128)(2,1)}), bf16[8,48,2048]{2,1,0:T(8,128)(2,1)}, u32[]{:S(2)}, u32[]{:S(2)}) async-start(bf16[8,48,2048]{2,1,0:T(8,128)(2,1)} %bitcast.331), calls=%async_computation.12 | async-start | bytes 3145728 | tf_op jit(solution)/shard_map/all_to_all | solution.py:252
  605.1 77.6 %all-gather.10.cloned.1.call-start = ((), (), s32[]{:S(2)}) async-start(), calls=%async_computation.27 | async-start | bytes 4718592 | tf_op jit(solution)/shard_map/all_gather | solution.py:433
  647.9 217.6 %reduce-scatter.9.cloned.1.call-start = ((), (), s32[]{:S(2)}) async-start(), calls=%async_computation.29 | async-start | bytes 3276800 | tf_op jit(solution)/shard_map/reduce_scatter | solution.py:467
  732.2 25.4 %all-to-all-start.3 = ((bf16[8,48,2048]{2,1,0:T(8,128)(2,1)}), bf16[8,48,2048]{2,1,0:T(8,128)(2,1)}, u32[]{:S(2)}, u32[]{:S(2)}) async-start(bf16[8,48,2048]{2,1,0:T(8,128)(2,1)} %bitcast.336), calls=%async_computation.4 | async-start | bytes 3145728 | tf_op jit(solution)/shard_map/all_to_all | solution.py:252
  736.6 139.8 %reduce-scatter.11.cloned.1.call-start = ((), (), s32[]{:S(2)}) async-start(), calls=%async_computation.30 | async-start | bytes 2621440 | tf_op jit(solution)/shard_map/reduce_scatter | solution.py:463
  757.6 25.4 %all-to-all-start.9 = ((bf16[8,48,2048]{2,1,0:T(8,128)(2,1)}), bf16[8,48,2048]{2,1,0:T(8,128)(2,1)}, u32[]{:S(2)}, u32[]{:S(2)}) async-start(bf16[8,48,2048]{2,1,0:T(8,128)(2,1)} %bitcast.337), calls=%async_computation.10 | async-start | bytes 3145728 | tf_op jit(solution)/shard_map/all_to_all | solution.py:252
  783.0 27.4 %all-to-all-start.7 = ((bf16[8,48,2048]{2,1,0:T(8,128)(2,1)}), bf16[8,48,2048]{2,1,0:T(8,128)(2,1)}, u32[]{:S(2)}, u32[]{:S(2)}) async-start(bf16[8,48,2048]{2,1,0:T(8,128)(2,1)} %bitcast.333), calls=%async_computation.8 | async-start | bytes 3145728 | tf_op jit(solution)/shard_map/all_to_all | solution.py:252
  787.3 109.9 %reduce-scatter.7.cloned.1.call-start = ((), (), s32[]{:S(2)}) async-start(), calls=%async_computation.28 | async-start | bytes 4718592 | tf_op jit(solution)/shard_map/reduce_scatter | solution.py:446
  809.0 28.0 %collective-permute-start.4 = (bf16[128,2048]{1,0:T(8,128)(2,1)}, bf16[128,2048]{1,0:T(8,128)(2,1)}, u32[]{:S(2)}, u32[]{:S(2)}) collective-permute-start(bf16[128,2048]{1,0:T(8,128)(2,1)} %fusion.78), channel_id=1, source_target_pairs={{0,1},{1,2},{2,3},{3,0},{4,5},{5,6},{6,7},{7,4},{8,9},{9,10},{10,1... | collective-permute-start | bytes 1572872 | tf_op jit(solution)/shard_map/ppermute | solution.py:249
  810.4 32.9 %all-to-all-start.5 = ((bf16[8,48,2048]{2,1,0:T(8,128)(2,1)}), bf16[8,48,2048]{2,1,0:T(8,128)(2,1)}, u32[]{:S(2)}, u32[]{:S(2)}) async-start(bf16[8,48,2048]{2,1,0:T(8,128)(2,1)} %bitcast.332), calls=%async_computation.6 | async-start | bytes 3145728 | tf_op jit(solution)/shard_map/all_to_all | solution.py:252
  839.8 30.0 %collective-permute-start.5 = (bf16[128,2048]{1,0:T(8,128)(2,1)}, bf16[128,2048]{1,0:T(8,128)(2,1)}, u32[]{:S(2)}, u32[]{:S(2)}) collective-permute-start(bf16[128,2048]{1,0:T(8,128)(2,1)} %add_convert_fusion.8), channel_id=1, source_target_pairs={{0,1},{1,2},{2,3},{3,0},{4,5},{5,6},{6,7},{7,4},{8,9},{9,10},{10,1... | collective-permute-start | bytes 1572872 | tf_op jit(solution)/shard_map/ppermute | solution.py:249
  872.0 26.8 %collective-permute-start.6 = (bf16[128,2048]{1,0:T(8,128)(2,1)}, bf16[128,2048]{1,0:T(8,128)(2,1)}, u32[]{:S(2)}, u32[]{:S(2)}) collective-permute-start(bf16[128,2048]{1,0:T(8,128)(2,1)} %add_convert_fusion.7), channel_id=1, source_target_pairs={{0,1},{1,2},{2,3},{3,0},{4,5},{5,6},{6,7},{7,4},{8,9},{9,10},{10,1... | collective-permute-start | bytes 1572872 | tf_op jit(solution)/shard_map/ppermute | solution.py:249
  (87 other events, 1367.7 us)
Sparse Core Ops, SparseCore 0:
  24.4 189.4 all-reduce.2
Sparse Core Ops, SparseCore 1:
  28.8 54.8 all-gather.13
  85.4 35.6 all-gather.11
  122.5 45.8 all-gather.7
  256.1 67.7 reduce-scatter.4
  648.0 34.7 all-gather.9
  728.7 52.1 reduce-scatter.8
  783.1 54.0 reduce-scatter.10
  840.4 56.8 reduce-scatter.6

commit v2 on v1

v2 whole, which is shorter than its diff:
```python
import jax
import jax.numpy as jnp
import numpy as np
from jax import lax
from jax.experimental import pallas as pl
from jax.experimental.pallas import tpu as pltpu
from jax.sharding import PartitionSpec as P

D = 2048
H = 32
KVH = 4
HD = 128
TOP = 8
BLK = 256

EPSILON = 1e-06
ROPE_BASE = 1000000.0
SCALE = HD**-0.5
BF = jnp.bfloat16
F32 = jnp.float32
MASKED = -1e30
VMEM_LIMIT = 48 * 1024 * 1024
ATTN_LIMIT = 24 * 1024 * 1024
SMALL = pl.CostEstimate(flops=1000, bytes_accessed=1000, transcendentals=0)
TILE = 512


def cost(micros):
    return pl.CostEstimate(flops=int(1.1e9 * micros), bytes_accessed=1000, transcendentals=0)


def rope_tables(rows):
    half = HD // 2
    freq = np.power(ROPE_BASE, np.arange(half) * (-2.0 / HD))
    angles = np.arange(rows)[:, None] * freq[None, :]
    cos, sin = np.cos(angles), np.sin(angles)
    return (
        np.concatenate([cos, cos], axis=1).astype(np.float32),
        np.concatenate([-sin, sin], axis=1).astype(np.float32),
    )


def inv_rms(values):
    return lax.rsqrt(jnp.mean(values * values, axis=-1, keepdims=True) + EPSILON)


def nt_dot(a, b):
    return lax.dot_general(a, b, (((1,), (1,)), ((), ())), preferred_element_type=F32)


def tn_dot(a, b):
    return lax.dot_general(a, b, (((0,), (0,)), ((), ())), preferred_element_type=F32)


def mm(a, b):
    return jnp.dot(a, b, preferred_element_type=F32)


def spin(values, cos, sin):
    return values * cos + pltpu.roll(values, HD // 2, 1) * sin


def unspin(values, cos, sin):
    return values * cos - pltpu.roll(values, HD // 2, 1) * sin


def attn_forward_kernel(blocks, raw, kraw, vraw, cos_all, sin_all, cos, sin, qgain, kgain, out, keys, vals):
    head, block = pl.program_id(0), pl.program_id(1)

    @pl.when((head == 0) & (block == 0))
    def _():
        rows = kraw[...]
        keys[...] = spin(rows * inv_rms(rows) * kgain[...], cos_all[...], sin_all[...]).astype(BF)
        vals[...] = vraw[...].astype(BF)

    rows = raw[...]
    query = spin(rows * inv_rms(rows) * qgain[...], cos[...], sin[...]).astype(BF)
    for n in range(blocks):

        @pl.when(block == n)
        def _(n=n):
            span = (n + 1) * BLK
            weights = jnp.exp(nt_dot(query, keys[:span, :]) * SCALE)
            total = jnp.sum(weights, axis=-1, keepdims=True)
            probs = (weights * (1.0 / total)).astype(BF)
            out[...] = mm(probs, vals[:span, :]).astype(BF)


def attn_backward_kernel(
    blocks, raw, kraw, vraw, cos_all, sin_all, cos, sin, qgain, kgain, gout, *rest
):
    *start, gq, gk, gv, gqgain, keys, vals = rest
    head, block = pl.program_id(0), pl.program_id(1)

    @pl.when((head == 0) & (block == 0))
    def _():
        rows = kraw[...]
        keys[...] = spin(rows * inv_rms(rows) * kgain[...], cos_all[...], sin_all[...]).astype(BF)
        vals[...] = vraw[...].astype(BF)
        for ref, first in zip((gk, gv, gqgain), start or (None,) * 3):
            ref[...] = jnp.zeros_like(ref) if first is None else first[...]

    rows = raw[...]
    inverse = inv_rms(rows)
    normed = rows * inverse
    query = spin(normed * qgain[...], cos[...], sin[...]).astype(BF)
    grad_out = gout[...]

    def finish(grad_query):
        turned = unspin(grad_query, cos[...], sin[...])
        gqgain[...] += jnp.sum(turned * normed, axis=0, keepdims=True)
        scaled = turned * qgain[...]
        mean = jnp.mean(scaled * normed, axis=-1, keepdims=True)
        gq[...] = (inverse * (scaled - normed * mean)).astype(BF)

    for n in range(blocks):

        @pl.when(block == n)
        def _(n=n):
            span = (n + 1) * BLK
            seen, values = keys[:span, :], vals[:span, :]
            weights = jnp.exp(nt_dot(query, seen) * SCALE)
            total = jnp.sum(weights, axis=-1, keepdims=True)
            probs = weights * (1.0 / total)
            grad_probs = nt_dot(grad_out, values)
            delta = jnp.sum(probs * grad_probs, axis=-1, keepdims=True)
            grad_scores = (probs * (grad_probs - delta)).astype(BF)
            gv[:span, :] += tn_dot(probs.astype(BF), grad_out)
            gk[:span, :] += tn_dot(grad_scores, query) * SCALE
            finish(mm(grad_scores, seen) * SCALE)


def key_backward_kernel(count, kraw, cos, sin, kgain, *rest):
    gks, gvs, (gk_low, gv_low, gkgain) = rest[:count], rest[count : 2 * count], rest[2 * count :]
    grad_keys, grad_vals = gks[0][...], gvs[0][...]
    for n in range(1, count):
        grad_keys = grad_keys + gks[n][...]
        grad_vals = grad_vals + gvs[n][...]
    rows = kraw[...]
    inverse = inv_rms(rows)
    normed = rows * inverse
    turned = unspin(grad_keys, cos[...], sin[...])
    gkgain[...] = jnp.sum(turned * normed, axis=0, keepdims=True)
    scaled = turned * kgain[...]
    mean = jnp.mean(scaled * normed, axis=-1, keepdims=True)
    gk_low[...] = (inverse * (scaled - normed * mean)).astype(BF)
    gv_low[...] = grad_vals.astype(BF)


def attn_specs(rows, first=0):
    return [
        pl.BlockSpec((BLK, HD), lambda h, i: (i, h + first)),
        pl.BlockSpec((rows, HD), lambda h, i: (0, 0)),
        pl.BlockSpec((rows, HD), lambda h, i: (0, 0)),
        pl.BlockSpec((rows, HD), lambda h, i: (0, 0)),
        pl.BlockSpec((rows, HD), lambda h, i: (0, 0)),
        pl.BlockSpec((BLK, HD), lambda h, i: (i, 0)),
        pl.BlockSpec((BLK, HD), lambda h, i: (i, 0)),
        pl.BlockSpec((1, HD), lambda h, i: (0, 0)),
        pl.BlockSpec((1, HD), lambda h, i: (0, 0)),
    ]


def attn_forward(raw, kraw, vraw, cos, sin, qgain, kgain, first, heads):
    rows = raw.shape[0]
    blocks = rows // BLK
    return pl.pallas_call(
        lambda *refs: attn_forward_kernel(blocks, *refs),
        grid=(heads, blocks),
        in_specs=attn_specs(rows, first),
        out_specs=pl.BlockSpec((BLK, HD), lambda h, i: (i, h)),
        out_shape=jax.ShapeDtypeStruct((rows, heads * HD), BF),
        scratch_shapes=[pltpu.VMEM((rows, HD), BF), pltpu.VMEM((rows, HD), BF)],
        compiler_params=pltpu.CompilerParams(vmem_limit_bytes=ATTN_LIMIT),
        cost_estimate=cost(7),
        name="attn_fw",
    )(raw, kraw, vraw, cos, sin, cos, sin, qgain, kgain)


def attn_backward(raw, kraw, vraw, cos, sin, qgain, kgain, gout, first, heads, start):
    rows = raw.shape[0]
    blocks = rows // BLK
    return pl.pallas_call(
        lambda *refs: attn_backward_kernel(blocks, *refs),
        grid=(heads, blocks),
        in_specs=attn_specs(rows, first)
        + [pl.BlockSpec((BLK, HD), lambda h, i: (i, h + first))]
        + [pl.BlockSpec(v.shape, lambda h, i: (0, 0)) for v in start],
        out_specs=[
            pl.BlockSpec((BLK, HD), lambda h, i: (i, h)),
            pl.BlockSpec((rows, HD), lambda h, i: (0, 0)),
            pl.BlockSpec((rows, HD), lambda h, i: (0, 0)),
            pl.BlockSpec((1, HD), lambda h, i: (0, 0)),
        ],
        out_shape=[
            jax.ShapeDtypeStruct((rows, heads * HD), BF),
            jax.ShapeDtypeStruct((rows, HD), F32),
            jax.ShapeDtypeStruct((rows, HD), F32),
            jax.ShapeDtypeStruct((1, HD), F32),
        ],
        scratch_shapes=[pltpu.VMEM((rows, HD), BF), pltpu.VMEM((rows, HD), BF)],
        compiler_params=pltpu.CompilerParams(vmem_limit_bytes=ATTN_LIMIT),
        cost_estimate=cost(12),
        name="attn_bw",
    )(raw, kraw, vraw, cos, sin, cos, sin, qgain, kgain, gout, *start)


def key_backward(kraw, cos, sin, kgain, gks, gvs):
    rows = kraw.shape[0]
    return pl.pallas_call(
        lambda *refs: key_backward_kernel(len(gks), *refs),
        out_shape=[
            jax.ShapeDtypeStruct((rows, HD), BF),
            jax.ShapeDtypeStruct((rows, HD), BF),
            jax.ShapeDtypeStruct((1, HD), F32),
        ],
        compiler_params=pltpu.CompilerParams(vmem_limit_bytes=ATTN_LIMIT),
        cost_estimate=cost(2),
        name="key_bw",
    )(kraw, cos, sin, kgain, *gks, *gvs)


def call(kernel, name, out_shape, micros=0, **kw):
    return pl.pallas_call(
        kernel,
        out_shape=out_shape,
        compiler_params=pltpu.CompilerParams(vmem_limit_bytes=VMEM_LIMIT),
        cost_estimate=cost(micros) if micros else SMALL,
        name=name,
        **kw,
    )


def whole(values):
    return pl.BlockSpec(values.shape, lambda *_: (0,) * values.ndim)


def column_tile(height):
    return pl.BlockSpec((height, TILE), lambda j: (0, j))


def routing(ids, place, ne, experts, cap):
    nc, _, rows = ids.shape
    nchip = nc // 2
    block = 2 * cap

    def kernel(at, ids_ref, send, direct, chosen, spots, named):
        chip, core, ci, ei = at[0], at[1], at[2], at[3]
        number = lax.broadcasted_iota(jnp.int32, (experts, rows), 0)
        slot = lax.broadcasted_iota(jnp.int32, (cap, rows), 0).astype(F32)
        lower = (
            lax.broadcasted_iota(jnp.int32, (rows, rows), 0)
            < lax.broadcasted_iota(jnp.int32, (rows, rows), 1)
        ).astype(BF)
        for dev in range(nc):
            got = ids_ref[dev]
            hits = jnp.zeros((experts, rows), F32)
            for k in range(TOP):
                hits = hits + (got[k : k + 1, :] == number).astype(F32)
            named[dev] = hits.astype(BF)
            spots[dev] = jnp.where(hits > 0.5, mm(hits.astype(BF), lower), -1.0)

        def slots_of(dev, expert):
            line = jnp.sum(jnp.where(number == expert, spots[dev], 0.0), axis=0, keepdims=True)
            return (line == slot).astype(BF)

        for m in range(nchip):
            expert = ((chip ^ m) * 2 + core) * ne + ei
            send[m] = jnp.zeros((block, 2 * rows), BF)
            send[m, :cap, :rows] = slots_of(ci, expert)
            send[m, cap:, rows:] = slots_of(ci ^ 1, expert)
            for src in range(2):
                dev = (chip ^ m) * 2 + (core ^ src)
                taken = slots_of(dev, ci * ne + ei)
                first = (m * 2 + src) * cap
                chosen[first : first + cap, :] = nt_dot(taken, named[dev])
        for dev in range(nc):
            direct[dev] = slots_of(ci, dev * ne + ei)

    return pl.pallas_call(
        kernel,
        out_shape=[
            jax.ShapeDtypeStruct((nchip, block, 2 * rows), BF),
            jax.ShapeDtypeStruct((nc, cap, rows), BF),
            jax.ShapeDtypeStruct((nc * cap, experts), F32),
        ],
        in_specs=[pl.BlockSpec(memory_space=pltpu.SMEM), pl.BlockSpec(memory_space=pltpu.VMEM)],
        scratch_shapes=[
            pltpu.VMEM((nc, experts, rows), F32),
            pltpu.VMEM((nc, experts, rows), BF),
        ],
        compiler_params=pltpu.CompilerParams(vmem_limit_bytes=ATTN_LIMIT),
        cost_estimate=SMALL,
        name="routing",
    )(place, ids)


def select_direct(direct, planes, values):
    steps, (nc, cap, rows) = len(direct), direct[0].shape

    def kernel(at, *refs):
        tokens, out = refs[steps], refs[steps + 1]
        for n in range(steps):
            part = tokens[at[n]]
            for dev in range(nc):
                out[dev, n * cap : (n + 1) * cap, :] = mm(refs[n][dev], part).astype(BF)

    return call(
        kernel,
        "select_direct",
        micros=3,
        out_shape=jax.ShapeDtypeStruct((nc, steps * cap, D), BF),
        grid=(D // TILE,),
        in_specs=[pl.BlockSpec(memory_space=pltpu.SMEM)]
        + [whole(v) for v in direct]
        + [pl.BlockSpec((values.shape[0], rows, TILE), lambda j: (0, 0, j))],
        out_specs=pl.BlockSpec((nc, steps * cap, TILE), lambda j: (0, 0, j)),
    )(planes, *direct, values)


def select_rows(send, values, mates):
    nchip, block, _ = send.shape
    rows, count = values[0].shape[0], len(values)

    def kernel(picks, *refs):
        outs = refs[2 * count :]
        for n in range(count):
            pair = jnp.concatenate([refs[n][...], refs[count + n][...]], axis=0)
            for m in range(nchip):
                outs[m][n] = mm(picks[m], pair).astype(BF)

    return call(
        kernel,
        "select_rows",
        micros=3,
        out_shape=[jax.ShapeDtypeStruct((count, block, D), BF)] * nchip,
        grid=(D // TILE,),
        in_specs=[whole(send)] + [column_tile(rows)] * (2 * count),
        out_specs=[pl.BlockSpec((count, block, TILE), lambda j: (0, 0, j))] * nchip,
    )(send, *values, *mates)


def combine_rows(send, home):
    nchip, block, _ = send.shape
    rows, wide = send.shape[2] // 2, home[0].shape[1]

    def kernel(picks, *refs):
        blocks, mine, theirs = refs[:nchip], refs[nchip], refs[nchip + 1]
        got = jnp.concatenate([b[...] for b in blocks], axis=0)
        chosen = jnp.concatenate([picks[m] for m in range(nchip)], axis=0)
        both = tn_dot(chosen, got)
        mine[...] = both[:rows]
        theirs[...] = both[rows:].astype(BF)

    return call(
        kernel,
        "combine_rows",
        micros=3,
        out_shape=[jax.ShapeDtypeStruct((rows, wide), F32), jax.ShapeDtypeStruct((rows, wide), BF)],
    )(send, *home)


def combine_all(send, planes, home):
    ne, (nchip, block, wide) = len(send), send[0].shape
    rows = wide // 2

    def kernel(at, *refs):
        mine, theirs = refs[-2:]
        for step in range(ne):
            blocks = refs[ne + step * nchip : ne + (step + 1) * nchip]
            got = jnp.concatenate([b[...] for b in blocks], axis=0)
            chosen = jnp.concatenate([refs[step][m] for m in range(nchip)], axis=0)
            both = tn_dot(chosen, got).astype(BF)
            mine[at[step]] = both[:rows]
            theirs[at[step]] = both[rows:]

    return call(
        kernel,
        "combine_all",
        micros=6,
        out_shape=[jax.ShapeDtypeStruct((ne, rows, D), BF)] * 2,
        grid=(D // TILE,),
        in_specs=[pl.BlockSpec(memory_space=pltpu.SMEM)]
        + [whole(v) for v in send]
        + [column_tile(block)] * (ne * nchip),
        out_specs=[pl.BlockSpec((ne, rows, TILE), lambda j: (0, 0, j))] * 2,
    )(planes, *send, *(v for blocks in home for v in blocks))


def expert_rows(rows_in, cot_in, devices, row_chosen, router, column, lane, weights):
    nchip, (both, block, _) = len(rows_in), rows_in[0].shape
    nc, cap = 2 * nchip, block // 2
    cots = 0 if both > 1 else nc
    slots, lanes, hidden_size = nchip * block, lane.shape[1], weights[0].shape[1]

    def kernel(_, *refs):
        ffn_in, cot_refs = refs[:nchip], refs[nchip : nchip + cots]
        chosen_ref, router_ref, column_ref, lane_ref, w_gate, w_up, w_down = refs[
            nchip + cots : nchip + cots + 7
        ]
        outs = refs[nchip + cots + 7 :]
        backs, mixes, kept = outs[:nchip], outs[nchip : 2 * nchip], outs[2 * nchip :]
        all_out, hidden_out, gate_out, up_out = kept
        rows = jnp.concatenate([r[0] for r in ffn_in], axis=0)
        cot = jnp.concatenate([r[0] for r in cot_refs] or [r[1] for r in ffn_in], axis=0)
        all_out[...] = rows
        gates = gates_of(mm(rows, router_ref[...]), chosen_ref[...] > 0.5, True)
        gate_vec = jnp.sum(gates * column_ref[...], axis=-1, keepdims=True)
        gate_act = mm(rows, w_gate[...])
        up_act = mm(rows, w_up[...])
        upstream = nt_dot(cot, w_down[...])
        sig = 1.0 / (1.0 + jnp.exp(-gate_act))
        silu = gate_act * sig
        hidden = (silu * up_act).astype(BF).astype(F32)
        score = jnp.sum(upstream * hidden, axis=-1, keepdims=True)
        gated = (hidden * gate_vec).astype(BF)
        hidden_out[...] = gated
        grad_hidden = upstream * gate_vec
        grad_gate = (grad_hidden * up_act * sig * (1.0 + gate_act * (1.0 - sig))).astype(BF)
        grad_up = (grad_hidden * silu).astype(BF)
        gate_out[...] = grad_gate
        up_out[...] = grad_up
        back = (nt_dot(grad_gate, w_gate[...]) + nt_dot(grad_up, w_up[...])).astype(BF)
        scores = (score * lane_ref[...]).astype(BF)
        for m in range(nchip):
            part = slice(m * block, (m + 1) * block)
            backs[m][:, :D] = back[part]
            backs[m][:, D:] = scores[part]
            mixes[m][...] = mm(gated[part], w_down[...]).astype(BF)

    narrow = jax.ShapeDtypeStruct((slots, hidden_size), BF)
    out_shape = [jax.ShapeDtypeStruct((block, D + lanes), BF)] * nchip
    out_shape += [jax.ShapeDtypeStruct((block, D), BF)] * nchip + [
        jax.ShapeDtypeStruct((slots, D), BF),
        narrow,
        narrow,
        narrow,
    ]
    fixed = [row_chosen, router, column, lane, *weights]
    outs = call(
        kernel,
        "expert_rows",
        micros=14,
        out_shape=out_shape,
        grid_spec=pltpu.PrefetchScalarGridSpec(
            num_scalar_prefetch=1,
            grid=(1,),
            in_specs=[whole(r) for r in rows_in]
            + [
                pl.BlockSpec((1, cap, D), lambda i, at, n=n: (at[n], 0, 0))
                for n in range(cots)
            ]
            + [whole(v) for v in fixed],
            out_specs=[whole(v) for v in out_shape],
        ),
    )(devices, *rows_in, *([cot_in] * cots), *fixed)
    return outs[:nchip], outs[nchip : 2 * nchip], outs[2 * nchip :]


def grad_in_weight(rows, grads):
    chunks, slots, size = len(rows), rows[0].shape[0], grads[0].shape[1]

    def kernel(*refs):
        total = tn_dot(refs[0][...], refs[chunks][...])
        for n in range(1, chunks):
            total += tn_dot(refs[n][...], refs[chunks + n][...])
        refs[2 * chunks][...] = total

    return call(
        kernel,
        "grad_in_weight",
        micros=10,
        out_shape=jax.ShapeDtypeStruct((D, size), F32),
        grid=(D // TILE,),
        in_specs=[column_tile(slots)] * chunks + [whole(v) for v in grads],
        out_specs=pl.BlockSpec((TILE, size), lambda i: (i, 0)),
    )(*rows, *grads)


def grad_down_weight(hidden, devices, cot_first, later):
    chunks = len(hidden)
    (nc, cap, _), size = cot_first.shape, hidden[0].shape[1]
    nchip = nc // 2

    def kernel(at, *refs):
        hid, early, late, out = refs[:chunks], refs[chunks], refs[chunks + 1 : -1], refs[-1]
        total = None
        for n in range(chunks):
            if n:
                rows = [r[0] for r in late[(n - 1) * nchip : n * nchip]]
            else:
                rows = [early[at[i]] for i in range(nc)]
            part = tn_dot(hid[n][...], jnp.concatenate(rows, axis=0))
            total = part if total is None else total + part
        out[...] = total

    late = [v for blocks in later for v in blocks]
    return call(
        kernel,
        "grad_down_weight",
        micros=10,
        out_shape=jax.ShapeDtypeStruct((size, D), F32),
        grid=(D // TILE,),
        in_specs=[pl.BlockSpec(memory_space=pltpu.SMEM)]
        + [whole(v) for v in hidden]
        + [pl.BlockSpec((nc, cap, TILE), lambda j: (0, 0, j))]
        + [pl.BlockSpec((1, 2 * cap, TILE), lambda j: (1, 0, j))] * len(late),
        out_specs=column_tile(size),
    )(devices, *hidden, cot_first, *late)


def project(x_all, gain, weight, wrows):
    rows, size = x_all.shape[0], weight.shape[3]

    def kernel(x, gain_ref, w, normed, raw):
        values = x[...].astype(F32)
        low = (values * inv_rms(values) * gain_ref[...]).astype(BF)
        normed[...] = low
        raw[...] = mm(low, w[:, :, :wrows, :].reshape(D, size))

    band = pl.BlockSpec((BLK, D), lambda i: (i, 0))
    return call(
        kernel,
        "project",
        micros=6,
        out_shape=[jax.ShapeDtypeStruct((rows, D), BF), jax.ShapeDtypeStruct((rows, size), F32)],
        grid=(rows // BLK,),
        in_specs=[band, whole(gain), whole(weight)],
        out_specs=[band, pl.BlockSpec((BLK, size), lambda i: (i, 0))],
    )(x_all, gain, weight)


def part_product(values, index, rows, weight, wrows, theirs, dtype):
    size = values.shape[1]
    extra = [] if theirs is None else [theirs]

    def kernel(_, part, w, *refs):
        if wrows:
            out = nt_dot(part[...], w[:, :, :wrows, :].reshape(TILE, size))
        else:
            out = mm(part[...], w[...])
        if theirs is not None:
            out = out + refs[0][...].astype(F32)
        refs[-1][...] = out.astype(dtype)

    if wrows:
        shape = (TILE // (weight.shape[1] * wrows),) + weight.shape[1:]
        weight_spec = pl.BlockSpec(shape, lambda j, at: (j, 0, 0, 0))
    else:
        weight_spec = pl.BlockSpec((size, TILE), lambda j, at: (0, j))
    column = pl.BlockSpec((rows, TILE), lambda j, at: (0, j))
    return call(
        kernel,
        "part_product",
        micros=2,
        out_shape=jax.ShapeDtypeStruct((rows, D), dtype),
        grid_spec=pltpu.PrefetchScalarGridSpec(
            num_scalar_prefetch=1,
            grid=(D // TILE,),
            in_specs=[pl.BlockSpec((rows, size), lambda j, at: (at[0], 0)), weight_spec]
            + [column] * len(extra),
            out_specs=column,
        ),
    )(index.reshape(1), values, weight, *extra)


def output_grads(attn, grad_branch):
    rows, size = attn.shape

    def kernel(a, g, out):
        out[...] = tn_dot(a[...], g[...]).astype(BF)

    return call(
        kernel,
        "output_grads",
        micros=5,
        out_shape=jax.ShapeDtypeStruct((size, D), BF),
        grid=(D // TILE,),
        in_specs=[whole(attn), column_tile(rows)],
        out_specs=column_tile(size),
    )(attn, grad_branch)


def attn_grads(grad_branch, weight):
    rows, size = grad_branch.shape[0], weight.shape[0]

    def kernel(g, w, out):
        out[...] = nt_dot(g[...], w[...]).astype(BF)

    return call(
        kernel,
        "attn_grads",
        micros=5,
        out_shape=jax.ShapeDtypeStruct((rows, size), BF),
        grid=(rows // BLK,),
        in_specs=[pl.BlockSpec((BLK, D), lambda i: (i, 0)), whole(weight)],
        out_specs=pl.BlockSpec((BLK, size), lambda i: (i, 0)),
    )(grad_branch, weight)


def projection_grads(xa, grads, nc, ne, small=None):
    rows, wrows, size = xa.shape[0], D // (nc * ne), grads.shape[1]
    more = [] if small is None else list(small)
    high = wrows + sum(v.shape[2] for v in more)

    def kernel(x, g, *refs):
        out = refs[-1]
        out[:, :, :wrows, :] = tn_dot(x[...], g[...]).astype(BF).reshape(ne, 1, wrows, size)
        if small is not None:
            out[:, :, wrows:, :] = jnp.concatenate([refs[0][...], refs[1][...]], axis=2)

    return call(
        kernel,
        "projection_grads",
        micros=3,
        out_shape=jax.ShapeDtypeStruct((ne, nc, high, size), BF),
        grid=(nc,),
        in_specs=[pl.BlockSpec((rows, ne * wrows), lambda i: (0, i)), whole(grads)]
        + [pl.BlockSpec((ne, 1) + v.shape[2:], lambda i: (0, i, 0, 0)) for v in more],
        out_specs=pl.BlockSpec((ne, 1, high, size), lambda i: (0, i, 0, 0)),
    )(xa, grads, *more)


def gates_of(logits, chosen, empty):
    top = jnp.max(jnp.where(chosen, logits, MASKED), axis=-1, keepdims=True)
    raised = jnp.where(chosen, jnp.exp(jnp.where(chosen, logits - top, 0.0)), 0.0)
    total = jnp.sum(raised, axis=-1, keepdims=True)
    return raised / (jnp.where(total > 0.0, total, 1.0) if empty else total)


def on_device(
    tokens,
    expert_ids,
    cotangent,
    attn_gain,
    ffn_gain,
    query_gain,
    key_gain,
    query_weight,
    key_weight,
    value_weight,
    output_weight,
    router_weight,
    gate_weight,
    up_weight,
    down_weight,
):
    both = ("ctx", "exp")
    nc, ne = lax.axis_size("ctx"), lax.axis_size("exp")
    ci, ei = lax.axis_index("ctx"), lax.axis_index("exp")
    chip, core = ci // 2, ci % 2
    nchip = nc // 2
    count = nc * ne
    rows = tokens.shape[1]
    seq = rows * nc
    heads = H // nc
    width = heads * HD
    share = nc // KVH
    piece = 2 * HD // share
    member = ci % share
    experts = router_weight.shape[1]
    lanes = -(-experts // 128) * 128
    cap = -(-max(2, rows * TOP * 3 // (2 * experts)) // 8) * 8
    block = 2 * cap
    slots = nchip * block
    wrows = query_weight.shape[0]
    gain_rows, head_rows = attn_gain.shape[0], query_gain.shape[0]

    def mate(values, bit=1):
        return lax.ppermute(values, "ctx", [(i, i ^ bit) for i in range(nc)])

    def peer(values, step):
        return mate(values, 2 * step) if step else values

    def along(values):
        return lax.ppermute(values, "exp", [(i, (i + 1) % ne) for i in range(ne)])

    def after(values, *others):
        return lax.optimization_barrier((values,) + others)[0]

    def place(step, other):
        return (chip ^ step) * 2 + (1 - core if other else core)

    def gather_ctx(values, out):
        got = [values] + [None] * (nchip - 1)
        for step in range(nchip - 1, 0, -1):
            got[step] = peer(values, step)
        for step in range(nchip):
            out = lax.dynamic_update_slice_in_dim(out, got[step], place(step, False) * rows, 0)
            out = lax.dynamic_update_slice_in_dim(
                out, mate(got[step]), place(step, True) * rows, 0
            )
        return out

    def scatter_ctx(values, weight, height):
        def part(step, other, theirs, dtype):
            return part_product(values, place(step, other), rows, weight, height, theirs, dtype)

        arrived, sent = [], []
        for step in list(range(nchip - 1, 0, -1)) + [0]:
            theirs = mate(part(step, True, None, BF))
            mine = part(step, False, theirs, BF if step else F32)
            sent.append(mine)
            if step:
                arrived.append(peer(mine, step))
        total = mine
        for values in arrived:
            total = total + values.astype(F32)
        return total, sent

    own_tokens = tokens[0]
    x_all = lax.all_gather(own_tokens, "ctx", axis=0, tiled=True)
    w_out = lax.all_gather(after(output_weight, x_all), "exp", axis=0, tiled=True)
    total_width = width + piece
    packed = jnp.concatenate(
        [
            expert_ids[0].T.astype(BF).reshape(-1),
            attn_gain,
            ffn_gain,
            query_gain,
            key_gain,
            router_weight.reshape(-1),
        ]
    )
    more = -(-packed.shape[0] // (8 * total_width)) * 8
    packed = jnp.pad(packed, (0, more * total_width - packed.shape[0]))
    kv = jnp.concatenate(
        [key_weight.reshape(wrows, KVH, HD), value_weight.reshape(wrows, KVH, HD)], axis=2
    ).reshape(wrows, nc, piece)
    part = jnp.concatenate([query_weight.reshape(wrows, nc, width), kv], axis=2)
    part = jnp.concatenate(
        [
            part.transpose(1, 0, 2),
            jnp.broadcast_to(packed.reshape(1, more, total_width), (nc, more, total_width)),
        ],
        axis=1,
    )
    part = lax.all_to_all(part, "ctx", split_axis=0, concat_axis=0, tiled=True)

    spot = jnp.stack([chip, core, ci, ei]).astype(jnp.int32)
    index = lax.iota(jnp.int32, nc)
    devices = (chip ^ (index // 2)) * 2 + (core ^ (index % 2))
    planes = (ei - lax.iota(jnp.int32, ne)) % ne
    moving, send, direct, row_chosen = part, [], [], []
    w_in = jnp.zeros((nc, ne, wrows + more, total_width), BF)
    for step in range(ne):
        if step:
            moving = along(moving)
        w_in = lax.dynamic_update_slice(w_in, moving[:, None], (0, (ei - step) % ne, 0, 0))
        ids = moving[:, wrows:].reshape(nc, more * total_width)[:, : TOP * rows]
        ids = ids.reshape(nc, TOP, rows).astype(jnp.int32)
        if step:
            ids = after(ids, row_chosen[-1])
        else:
            own_ids = ids
        for into, values in zip(
            (send, direct, row_chosen), routing(ids, spot, ne, experts, cap)
        ):
            into.append(values)
        if step == 0:
            cot_first = select_direct(direct, jnp.zeros((1,), jnp.int32), cotangent)
            cot_first = lax.all_to_all(
                cot_first, "ctx", split_axis=0, concat_axis=0, tiled=True
            )
    table = w_in[:, :, wrows:].reshape(count, more * total_width)
    cuts = np.cumsum(
        [TOP * rows, gain_rows, gain_rows, head_rows, head_rows, wrows * experts]
    ).tolist()
    gain_attn = table[:, cuts[0] : cuts[1]].reshape(1, D).astype(F32)
    gain_ffn = table[:, cuts[1] : cuts[2]].reshape(1, D).astype(F32)
    gain_query = table[:, cuts[2] : cuts[3]].reshape(1, HD).astype(F32)
    gain_key = table[:, cuts[3] : cuts[4]].reshape(1, HD).astype(F32)
    router = table[:, cuts[4] : cuts[5]].reshape(D, experts)
    own_ids = lax.dynamic_index_in_dim(own_ids, ci, 0, keepdims=False)
    chosen_home = jnp.any(
        own_ids.T[:, :, None] == lax.iota(jnp.int32, experts)[None, None, :], axis=1
    )
    cot_all = lax.all_gather(
        after(cotangent[0], moving, w_out), "exp", axis=0, tiled=False
    )

    def to_experts(picked):
        return [peer(picked[m], m) for m in range(nchip - 1, -1, -1)][::-1]

    cos, sin = (jnp.asarray(v) for v in rope_tables(seq))
    x_all = after(x_all, cot_first)
    xa, raw = project(x_all, gain_attn, w_in, wrows)
    q_raw = raw[:, :width]
    kv_own = raw[:, width:]
    kv_parts = [kv_own] + [mate(kv_own, bit) for bit in range(1, share)]
    ordered = []
    for spot in range(share):
        chosen = kv_parts[spot]
        for m in range(1, share):
            chosen = jnp.where(member == m, kv_parts[spot ^ m], chosen)
        ordered.append(chosen)
    kv_raw = jnp.concatenate(ordered, axis=1) if share > 1 else ordered[0]
    k_raw, v_raw = kv_raw[:, :HD], kv_raw[:, HD:]
    near = heads // 2
    attn_near = attn_forward(q_raw, k_raw, v_raw, cos, sin, gain_query, gain_key, 0, near)
    k_far = after(k_raw, attn_near, w_out)
    attn_far = attn_forward(
        q_raw, k_far, v_raw, cos, sin, gain_query, gain_key, near, heads - near
    )
    attn = jnp.concatenate([attn_near, attn_far], axis=1)
    w_gate, w_up, w_down = gate_weight[0], up_weight[0], down_weight[0]
    cot_all = after(cot_all, attn_far)
    cot_moving = [
        lax.dynamic_index_in_dim(cot_all, (ei - step) % ne, 0, keepdims=False)
        for step in range(ne)
    ]
    cot_mates = [mate(v) for v in cot_moving]
    inputs = own_tokens.astype(F32)
    residual = inputs + scatter_ctx(attn, w_out, 0)[0]
    inv_res = inv_rms(residual)
    normed_res = residual * inv_res
    ffn_in = (normed_res * gain_ffn).astype(BF)

    lane = (lax.iota(jnp.int32, lanes)[None, :] == ci * ne + ei).astype(F32)
    column = lane[:, :experts]
    ffn_moving = [ffn_in]
    for _ in range(1, ne):
        ffn_moving.append(along(ffn_moving[-1]))
    arrived, done, mixed, back_home = [None] * ne, [], [], {}

    def send_chunk(step, *others):
        values = [after(ffn_moving[step], *others)]
        mates = [mate(values[0])]
        if step:
            values.append(cot_moving[step])
            mates.append(cot_mates[step])
        picked = select_rows(send[step], values, mates)
        arrived[step] = to_experts(picked)
        return picked[0]

    def run_chunk(step, *others):
        rows_in = [after(v, *others) for v in arrived[step]]
        backs, mixes, kept = expert_rows(
            rows_in, cot_first, devices, row_chosen[step], router, column, lane,
            (w_gate, w_up, w_down),
        )
        done.append((backs, kept))
        mixed.append(mixes)
        return kept[0]

    def give_back(step, *others):
        backs = [after(v, *others) for v in done[step][0]] if others else done[step][0]
        back_home[step] = to_experts(backs)

    order = list(range(1, ne)) + [0]
    tick = send_chunk(0)
    for step in range(ne):
        if step + 1 < ne:
            tick = send_chunk(step + 1, tick, *arrived[step])
        tick = run_chunk(step, tick)
    waits = arrived[-1]
    for step in order:
        give_back(step, *waits)
        waits = back_home[step]

    all_rows, hidden_g, act_gate, act_up = ([d[1][n] for d in done] for n in range(4))
    work = [
        lambda t: grad_in_weight(all_rows, [after(v, t) for v in act_gate]),
        lambda t: grad_in_weight(all_rows, [after(v, t) for v in act_up]),
        lambda t: grad_down_weight(
            [after(v, t) for v in hidden_g], devices, cot_first, arrived[1:]
        ),
    ]
    grads, travelling = [], None
    for at, step in enumerate(order):
        waits = (tick,) if travelling is None else (tick, travelling)
        mine, theirs = combine_rows(send[step], [after(v, *waits) for v in back_home[step]])
        back_total = mine + mate(theirs).astype(F32)
        if travelling is not None:
            back_total = back_total + travelling.astype(F32)
        if at < ne - 1:
            tick = back_total.astype(BF)
            travelling = along(tick)
            if work:
                tick = work.pop(0)(tick)
                grads.append(tick)
    grad_gate, grad_up, grad_down = grads

    gates_home = gates_of(mm(ffn_in, router), chosen_home, False)
    grad_gates = back_total[:, D : D + experts]
    grad_logits = gates_home * (
        grad_gates - jnp.sum(gates_home * grad_gates, axis=-1, keepdims=True)
    )
    grad_logits_low = grad_logits.astype(BF)
    grad_ffn_in = back_total[:, :D] + nt_dot(grad_logits_low, router)
    scaled = grad_ffn_in * gain_ffn
    grad_residual = cotangent[0].astype(F32) + inv_res * (
        scaled - normed_res * jnp.mean(scaled * normed_res, axis=-1, keepdims=True)
    )
    grad_router = tn_dot(ffn_in, grad_logits_low)
    grad_gain_ffn = jnp.sum(grad_ffn_in * normed_res, axis=0)

    grad_branch = gather_ctx(grad_residual.astype(BF), x_all)
    far_width = (heads - heads // 2) * HD + piece
    small = jnp.concatenate(
        [grad_router.reshape(nc, ne, wrows * experts), grad_gain_ffn.reshape(nc, ne, gain_rows)],
        axis=2,
    )
    ends = small.shape[2]
    extra = -(-(-(-ends // far_width) + 1) // 8) * 8
    small = jnp.pad(small, ((0, 0), (0, 0), (0, (extra - 1) * far_width - ends)))
    small = small.transpose(1, 0, 2).astype(BF).reshape(ne, nc, extra - 1, far_width)
    grad_branch = after(grad_branch, small)
    grad_output = output_grads(attn, grad_branch)
    grad_branch_late = after(grad_branch, grad_output)
    orows = output_weight.shape[0]

    def output_part(step):
        return lax.dynamic_slice_in_dim(grad_output, ((ei - step) % ne) * orows, orows, 0)

    output_ring = [output_part(1 % ne)]
    for step in range(2, ne):
        output_ring.append(output_part(step) + along(output_ring[-1]))
    output_sum = output_part(0).astype(F32)
    if ne > 1:
        output_sum = output_sum + along(output_ring[-1]).astype(F32)
    grad_attn = attn_grads(grad_branch_late, w_out)

    mix_home, waits = [], (grad_branch,)
    for blocks in mixed:
        waits = to_experts([after(v, *waits) for v in blocks])
        mix_home.append(waits)
    grad_attn = after(grad_attn, *mix_home[0], output_ring[1 % len(output_ring)])

    def weight_grad(earlier, grads, *small):
        local = projection_grads(xa, grads, nc, ne, *small)
        late = after(local, earlier)
        return local, lax.psum_scatter(late, "exp", scatter_dimension=0, tiled=True)[0]

    grad_q_near, *start = attn_backward(
        q_raw, k_raw, v_raw, cos, sin, gain_query, gain_key, grad_attn, 0, near, ()
    )
    local_near, grad_w_near = weight_grad(grad_output, grad_q_near)
    grad_attn = after(grad_attn, local_near, *mix_home[1], output_ring[-1])
    grad_q_far, grad_k, grad_v, grad_gain_query = attn_backward(
        q_raw, k_raw, v_raw, cos, sin, gain_query, gain_key, grad_attn, near, heads - near, start
    )
    grad_k = after(grad_k, *mix_home[2], output_sum)
    gks = [grad_k] + [mate(grad_k, bit) for bit in range(1, share)]
    gvs = [grad_v] + [mate(grad_v, bit) for bit in range(1, share)]
    grad_k_low, grad_v_low, grad_gain_key = key_backward(k_raw, cos, sin, gain_key, gks, gvs)
    grad_gain_key = jnp.where(member == 0, grad_gain_key, 0.0)
    grad_kv = jnp.concatenate([grad_k_low, grad_v_low], axis=1)
    if share > 1:
        grad_kv = lax.dynamic_slice_in_dim(grad_kv, member * piece, piece, 1)
    grad_far = jnp.concatenate([grad_q_far, grad_kv], axis=1)
    grad_in = jnp.concatenate([grad_q_near, grad_far], axis=1)
    gains = jnp.concatenate(
        [
            grad_gain_query.reshape(nc, ne, head_rows),
            grad_gain_key.reshape(nc, ne, head_rows),
        ],
        axis=2,
    )
    gains = jnp.pad(gains, ((0, 0), (0, 0), (0, far_width - 2 * head_rows)))
    gains = gains.transpose(1, 0, 2).astype(BF).reshape(ne, nc, 1, far_width)
    local_far, grad_w_far = weight_grad(grad_w_near, grad_far, (small, gains))
    grad_in = after(grad_in, local_far, *(v for blocks in mix_home[3:] for v in blocks))
    grad_w_near = jnp.pad(grad_w_near, ((0, 0), (0, extra), (0, 0)))
    grad_w = lax.all_to_all(
        jnp.concatenate([grad_w_near, grad_w_far], axis=2),
        "ctx",
        split_axis=0,
        concat_axis=0,
        tiled=True,
    ).astype(F32)
    small = jnp.sum(grad_w[:, wrows:, near * HD :], axis=0)
    gains, small = small[-1], small[:-1].reshape(-1)
    grad_w = grad_w[:, :wrows]
    sum_query = grad_w[:, :, :width].transpose(1, 0, 2).reshape(wrows, H * HD)
    sum_kv = grad_w[:, :, width:].transpose(1, 0, 2).reshape(wrows, KVH, 2 * HD)
    sum_key = sum_kv[:, :, :HD].reshape(wrows, KVH * HD)
    sum_value = sum_kv[:, :, HD:].reshape(wrows, KVH * HD)
    sum_attn_gain = (
        jnp.sum(sum_query * query_weight.astype(F32), axis=1)
        + jnp.sum(sum_key * key_weight.astype(F32), axis=1)
        + jnp.sum(sum_value * value_weight.astype(F32), axis=1)
    ) / attn_gain.astype(F32)

    grad_xa, sent = scatter_ctx(grad_in, w_in, wrows)
    mix_home[0][0] = after(mix_home[0][0], *sent)
    mine, theirs = combine_all(send, planes, mix_home)
    mixture = (mine.astype(F32) + mate(theirs).astype(F32)).astype(BF)
    mixture = after(mixture, grad_w_far)
    mixture = lax.psum_scatter(mixture, "exp", scatter_dimension=0, tiled=True)[0].astype(F32)
    inv_in = inv_rms(inputs)
    normed_in = inputs * inv_in
    scaled_in = grad_xa * gain_attn
    grad_tokens = (
        grad_residual
        + inv_in
        * (scaled_in - normed_in * jnp.mean(scaled_in * normed_in, axis=-1, keepdims=True))
    )[None]

    layer_out = (residual + mixture).astype(BF)[None]

    router_size = wrows * experts
    return (
        layer_out,
        grad_tokens,
        sum_attn_gain,
        small[router_size : router_size + gain_rows],
        gains[:head_rows],
        gains[head_rows : 2 * head_rows],
        sum_query,
        sum_key,
        sum_value,
        output_sum,
        small[:router_size].reshape(wrows, experts),
        grad_gate[None],
        grad_up[None],
        grad_down[None],
    )


def solution(mesh):
    shard = ("ctx", "exp")
    rows = P("exp", "ctx", None)
    vector, matrix, stack = P(shard), P(shard, None), P(shard, None, None)
    return jax.shard_map(
        on_device,
        mesh=mesh,
        in_specs=(rows,) * 3 + (vector,) * 4 + (matrix,) * 5 + (stack,) * 3,
        out_specs=(rows,) * 2 + (vector,) * 4 + (matrix,) * 5 + (stack,) * 3,
        check_vma=False,
    )
```

time: 923 us -> 705 us (0.76)
  waiting for transfers between devices: 433 us -> 226 us
  matrix products: 201 us -> 2.05 us
  Pallas kernels: 38.2 us -> 219 us
  local copies, waits for them, and re-layouts: 47.3 us -> 101 us
  starting transfers between devices: 115 us -> 78 us
  other arithmetic: 51.3 us -> 29.9 us
  blocking collectives: 7.07 us -> 21.8 us
    unnamed x10 -> x6, waiting for transfers between devices: 185 us -> 0.76 us
    pallas_call x0 -> x42, Pallas kernels: none -> 181 us  [the longest x4 58.2 us: expert_rows(): call(kernel, 'expert_rows', micros=14, out_shape=out_shape, grid_spec=plt...]
    ppermute x3 -> x72, waiting for transfers between devices: 2.64 us -> 143 us  [mate(): return lax.ppermute(values, 'ctx', [(i, i ^ bit) for i in range(nc)])]
    all_to_all x20 -> x2, waiting for transfers between devices: 143 us -> 9.15 us  [the longest x1 9.14 us: on_device(): lax.all_to_all(jnp.concatenate([grad_w_near, grad_w_far], axis=2), 'ctx',...]
    dot_general x30 -> x1, matrix products: 88.6 us -> 0.33 us  [mm(): return jnp.dot(a, b, preferred_element_type=F32)]
    all_to_all x20 -> x2, starting transfers between devices: 91.3 us -> 7.87 us  [the longest x1 4.32 us: on_device(): lax.all_to_all(cot_first, 'ctx', split_axis=0, concat_axis=0, tiled=True)]
    dot_general x14 -> x1, matrix products: 65.7 us -> 1.17 us  [tn_dot(): lax.dot_general(a, b, (((0,), (0,)), ((), ())), preferred_element_type=F32)]
    ppermute x3 -> x72, starting transfers between devices: 0.51 us -> 57.2 us  [mate(): return lax.ppermute(values, 'ctx', [(i, i ^ bit) for i in range(nc)])]
  transfers between devices with their start and end apart: 47 -> 92, of which waited for: 28 -> 32; matrix products, arithmetic and copies ran while one was open for 26% -> 9% of each run, Pallas kernels for 1% -> 30%
where the time goes in v2:
time: 705 us; the launch traced here: 694 us
  waiting for transfers between devices  226 us (32%)
  Pallas kernels  219 us (31%)
  local copies, waits for them, and re-layouts  101 us (14%)
  starting transfers between devices  78 us (11%)
  other arithmetic  29.9 us (4%)
  blocking collectives  21.8 us (3%)
  between operations  16.4 us (2%)
    ppermute x72, waiting for transfers between devices, mate(): return lax.ppermute(values, 'ctx', [(i, i ^ bit) for i in range(nc)])  143 us
    unnamed x374, local copies, waits for them, and re-layouts  68 us
    ppermute x12, waiting for transfers between devices, along(): return lax.ppermute(values, 'exp', [(i, (i + 1) % ne) for i in range(ne)])  61.9 us
    pallas_call x4, Pallas kernels, expert_rows(): call(kernel, 'expert_rows', micros=14, out_shape=out_shape, grid_spec=plt...  58.2 us
    ppermute x72, starting transfers between devices, mate(): return lax.ppermute(values, 'ctx', [(i, i ^ bit) for i in range(nc)])  57.2 us
    pallas_call x16, Pallas kernels, part_product(): call(kernel, 'part_product', micros=2, out_shape=jax.ShapeDtypeStruct((ro...  35.4 us
    pallas_call x2, Pallas kernels, attn_backward(): pl.pallas_call(lambda *refs: attn_backward_kernel(blocks, *refs), grid=(h...  23.1 us
    all_to_all x1, blocking collectives, on_device(): part = lax.all_to_all(part, 'ctx', split_axis=0, concat_axis=0, tiled=True)  21.8 us
  transfers between devices with their start and end apart: 92, of which 32 were waited for; matrix products, arithmetic and copies ran while one was open for 9% of the time, Pallas kernels for 30%

profile of v2, /device:TPU:0, one launch (start us, length us, event | category | flops | bytes accessed | tf_op | source)
XLA Modules:
  0.0 693.9 jit_solution(8804841956536140160)
XLA Ops:
  15.4 21.8 %all_to_all.15 = bf16[8,72,640]{2,1,0:T(8,128)(2,1)S(1)} all-to-all(bf16[8,72,640]{2,1,0:T(8,128)(2,1)S(1)} %pad_maximum_fusion.3), channel_id=1, replica_groups=mesh['ctx'=8,'exp'=4] {'ctx'}, dimensions={0} | all-to-all | bytes 1474560 | tf_op jit(solution)/shard_map/all_to_all | solution.py:738
  38.8 17.5 %collective-permute-done = bf16[8,72,640]{2,1,0:T(8,128)(2,1)S(1)} collective-permute-done((bf16[8,72,640]{2,1,0:T(8,128)(2,1)S(1)}, bf16[8,72,640]{2,1,0:T(8,128)(2,1)S(1)}, u32[]{:S(2)}, u32[]{:S(2)}) %collective-permute-start) | collective-permute-done | bytes 737312 | tf_op jit(solution)/shard_map/ppermute | solution.py:676
  65.6 9.0 %collective-permute-done.1 = bf16[8,72,640]{2,1,0:T(8,128)(2,1)} collective-permute-done((bf16[8,72,640]{2,1,0:T(8,128)(2,1)S(1)}, bf16[8,72,640]{2,1,0:T(8,128)(2,1)}, u32[]{:S(2)}, u32[]{:S(2)}) %collective-permute-start.1) | collective-permute-done | bytes 737312 | tf_op jit(solution)/shard_map/ppermute | solution.py:676
  77.5 22.8 %collective-permute-done.2 = bf16[8,72,640]{2,1,0:T(8,128)(2,1)} collective-permute-done((bf16[8,72,640]{2,1,0:T(8,128)(2,1)}, bf16[8,72,640]{2,1,0:T(8,128)(2,1)}, u32[]{:S(2)}, u32[]{:S(2)}) %collective-permute-start.2) | collective-permute-done | bytes 737312 | tf_op jit(solution)/shard_map/ppermute | solution.py:676
  162.7 10.3 %collective-permute-done.8 = bf16[128,2048]{1,0:T(8,128)(2,1)} collective-permute-done((bf16[128,2048]{1,0:T(8,128)(2,1)}, bf16[128,2048]{1,0:T(8,128)(2,1)}, u32[]{:S(2)}, u32[]{:S(2)}) %collective-permute-start.8) | collective-permute-done | bytes 524320 | tf_op jit(solution)/shard_map/ppermute | solution.py:670
  193.7 8.0 %collective-permute-done.14.refs_2_ = bf16[1,96,2048]{2,1,0:T(8,128)(2,1)S(1)} collective-permute-done((bf16[1,96,2048]{2,1,0:T(8,128)(2,1)S(1)}, bf16[1,96,2048]{2,1,0:T(8,128)(2,1)S(1)}, u32[]{:S(2)}, u32[]{:S(2)}) %collective-permute-start.14) | collective-permute-done | bytes 393248 | tf_op jit(solution)/shard_map/ppermute | solution.py:670
  220.8 13.9 %expert_rows.4 = (bf16[96,2176]{1,0:T(8,128)(2,1)S(1)}, bf16[96,2176]{1,0:T(8,128)(2,1)S(1)}, bf16[96,2176]{1,0:T(8,128)(2,1)S(1)}, bf16[96,2176]{1,0:T(8,128)(2...) custom-call(s32[8]{0:T(128)S(1)} %fusion.26._.at, ...), custom_call_target="tpu_custom_call" | custom-call | flops 15399999488 | bytes 1000 | tf_op jit(solution)/shard_map/expert_rows/pallas_call | solution.py:440
  238.7 16.4 %collective-permute-done.21.refs_2_.refs_7_ = bf16[2,96,2048]{2,1,0:T(8,128)(2,1)S(1)} collective-permute-done((bf16[2,96,2048]{2,1,0:T(8,128)(2,1)S(1)}, bf16[2,96,2048]{2,1,0:T(8,128)(2,1)S(1)}, u32[]{:S(2)}, u32[]{:S(2)}) %collective-permute-start.21) | collective-permute-done | bytes 786464 | tf_op jit(solution)/shard_map/ppermute | solution.py:670
  266.4 14.9 %expert_rows.5 = (bf16[96,2176]{1,0:T(8,128)(2,1)S(1)}, bf16[96,2176]{1,0:T(8,128)(2,1)S(1)}, bf16[96,2176]{1,0:T(8,128)(2,1)S(1)}, bf16[96,2176]{1,0:T(8,128)(2...) custom-call(s32[8]{0:T(128)S(1)} %fusion.26._.at, ...), custom_call_target="tpu_custom_call" | custom-call | flops 15399999488 | bytes 1000 | tf_op jit(solution)/shard_map/expert_rows/pallas_call | solution.py:440
  283.2 16.8 %collective-permute-done.26.refs_2_.refs_11_ = bf16[2,96,2048]{2,1,0:T(8,128)(2,1)S(1)} collective-permute-done((bf16[2,96,2048]{2,1,0:T(8,128)(2,1)S(1)}, bf16[2,96,2048]{2,1,0:T(8,128)(2,1)S(1)}, u32[]{:S(2)}, u32[]{:S(2)}) %collective-permute-start.26) | collective-permute-done | bytes 786464 | tf_op jit(solution)/shard_map/ppermute | solution.py:670
  309.7 14.9 %expert_rows.6 = (bf16[96,2176]{1,0:T(8,128)(2,1)S(1)}, bf16[96,2176]{1,0:T(8,128)(2,1)S(1)}, bf16[96,2176]{1,0:T(8,128)(2,1)S(1)}, bf16[96,2176]{1,0:T(8,128)(2...) custom-call(s32[8]{0:T(128)S(1)} %fusion.26._.at, ...), custom_call_target="tpu_custom_call" | custom-call | flops 15399999488 | bytes 1000 | tf_op jit(solution)/shard_map/expert_rows/pallas_call | solution.py:440
  327.8 16.0 %collective-permute-done.31.refs_2_.refs_15_ = bf16[2,96,2048]{2,1,0:T(8,128)(2,1)S(1)} collective-permute-done((bf16[2,96,2048]{2,1,0:T(8,128)(2,1)S(1)}, bf16[2,96,2048]{2,1,0:T(8,128)(2,1)S(1)}, u32[]{:S(2)}, u32[]{:S(2)}) %collective-permute-start.31) | collective-permute-done | bytes 786464 | tf_op jit(solution)/shard_map/ppermute | solution.py:670
  347.4 14.5 %expert_rows.7 = (bf16[96,2176]{1,0:T(8,128)(2,1)S(1)}, bf16[96,2176]{1,0:T(8,128)(2,1)S(1)}, bf16[96,2176]{1,0:T(8,128)(2,1)S(1)}, bf16[96,2176]{1,0:T(8,128)(2...) custom-call(s32[8]{0:T(128)S(1)} %fusion.26._.at, ...), custom_call_target="tpu_custom_call" | custom-call | flops 15399999488 | bytes 1000 | tf_op jit(solution)/shard_map/expert_rows/pallas_call | solution.py:440
  374.8 9.9 %grad_in_weight.2 = f32[2048,768]{1,0:T(8,128)} custom-call(bf16[384,2048]{1,0:T(8,128)(2,1)S(1)} %copy-done.113, bf16[384,2048]{1,0:T(8,128)(2,1)S(1)} %copy-done.114, bf16[384,2048]{1,0:T(8,128)(2,1)} %get-tuple-element.256.refs_2_, bf16[384,2048]{1,0:T(8,128)(2,1)} %get-tuple-element.291.refs_3_, bf16[384,768]{1,0:T(8,128)(2,1)S(1)} %copy-done.133, ...), custom_call_target="tpu_custom_call" | custom-call | flops 11000000512 | bytes 1000 | tf_op jit(solution)/shard_map/grad_in_weight/pallas_call | solution.py:469
  394.3 9.9 %grad_in_weight.3 = f32[2048,768]{1,0:T(8,128)} custom-call(bf16[384,2048]{1,0:T(8,128)(2,1)S(1)} %copy-done.113, bf16[384,2048]{1,0:T(8,128)(2,1)S(1)} %copy-done.115, bf16[384,2048]{1,0:T(8,128)(2,1)} %get-tuple-element.256.refs_2_, bf16[384,2048]{1,0:T(8,128)(2,1)} %get-tuple-element.291.refs_3_, bf16[384,768]{1,0:T(8,128)(2,1)S(1)} %copy-done.132, ...), custom_call_target="tpu_custom_call" | custom-call | flops 11000000512 | bytes 1000 | tf_op jit(solution)/shard_map/grad_in_weight/pallas_call | solution.py:469
  424.5 10.3 %grad_down_weight.1 = f32[768,2048]{1,0:T(8,128)} custom-call(s32[8]{0:T(128)S(1)} %fusion.26._.at, bf16[384,768]{1,0:T(8,128)(2,1)S(1)} %copy-done.117, bf16[384,768]{1,0:T(8,128)(2,1)S(1)} %copy-done.119, bf16[384,768]{1,0:T(8,128)(2,1)S(1)} %copy-done.121, bf16[384,768]{1,0:T(8,128)(2,1)S(1)} %copy-done.123, ...), custom_call_target="tpu_custom_call" | custom-call | flops 11000000512 | bytes 1000 | tf_op jit(solution)/shard_map/grad_down_weight/pallas_call | solution.py:498
  449.5 9.2 %collective-permute-done.53 = bf16[128,2048]{1,0:T(8,128)(2,1)S(1)} collective-permute-done((bf16[128,2048]{1,0:T(8,128)(2,1)S(1)}, bf16[128,2048]{1,0:T(8,128)(2,1)S(1)}, u32[]{:S(2)}, u32[]{:S(2)}) %collective-permute-start.53) | collective-permute-done | bytes 524320 | tf_op jit(solution)/shard_map/ppermute | solution.py:670
  459.4 10.6 %collective-permute-done.55 = bf16[128,2048]{1,0:T(8,128)(2,1)} collective-permute-done((bf16[128,2048]{1,0:T(8,128)(2,1)S(1)}, bf16[128,2048]{1,0:T(8,128)(2,1)}, u32[]{:S(2)}, u32[]{:S(2)}) %collective-permute-start.55) | collective-permute-done | bytes 524320 | tf_op jit(solution)/shard_map/ppermute | solution.py:670
  513.6 11.2 %attn_bw.2 = (bf16[1024,256]{1,0:T(8,128)(2,1)S(1)}, f32[1024,128]{1,0:T(8,128)S(1)}, f32[1024,128]{1,0:T(8,128)S(1)}, f32[1,128]{1,0:T(1,128)S(1)}) custom-call(f32[1024,512]{1,0:T(8,128)S(1)} %copy-done.8, f32[1024,128]{1,0:T(8,128)S(1)} %copy-done.16, f32[1024,128]{1,0:T(8,128)S(1)} %copy-done.20, f32[1024,128]{1,0:T(8,128)S(1)} %copy-done.97, ...), custom_call_target="tpu_custom_call" | custom-call | flops 13200000000 | bytes 1000 | tf_op jit(solution)/shard_map/attn_bw/pallas_call | solution.py:183
  546.0 11.9 %attn_bw.3 = (bf16[1024,256]{1,0:T(8,128)(2,1)S(1)}, f32[1024,128]{1,0:T(8,128)}, f32[1024,128]{1,0:T(8,128)}, f32[1,128]{1,0:T(1,128)S(1)}) custom-call(f32[1024,512]{1,0:T(8,128)S(1)} %copy-done.9, f32[1024,128]{1,0:T(8,128)S(1)} %copy-done.17, f32[1024,128]{1,0:T(8,128)S(1)} %copy-done.21, f32[1024,128]{1,0:T(8,128)S(1)} %copy-done.98, ...), custom_call_target="tpu_custom_call" | custom-call | flops 13200000000 | bytes 1000 | tf_op jit(solution)/shard_map/attn_bw/pallas_call | solution.py:183
  625.6 8.6 %reduce-scatter.6.cloned.1.call-done = bf16[1,8,72,384]{3,2,1,0:T(8,128)(2,1)} async-done(((bf16[4,8,72,384]{3,2,1,0:T(8,128)(2,1)}), bf16[1,8,72,384]{3,2,1,0:T(8,128)(2,1)}) %reduce-scatter.6.cloned.1.call-update) | async-done | bytes 442384 | tf_op jit(solution)/shard_map/reduce_scatter | solution.py:933
  637.9 12.3 %collective-permute-done.81 = bf16[128,2048]{1,0:T(8,128)(2,1)} collective-permute-done((bf16[128,2048]{1,0:T(8,128)(2,1)S(1)}, bf16[128,2048]{1,0:T(8,128)(2,1)}, u32[]{:S(2)}, u32[]{:S(2)}) %collective-permute-start.81) | collective-permute-done | bytes 524320 | tf_op jit(solution)/shard_map/ppermute | solution.py:670
  650.2 9.9 %collective-permute-done.82 = bf16[128,2048]{1,0:T(8,128)(2,1)} collective-permute-done((bf16[128,2048]{1,0:T(8,128)(2,1)S(1)}, bf16[128,2048]{1,0:T(8,128)(2,1)}, u32[]{:S(2)}, u32[]{:S(2)}) %collective-permute-start.82) | collective-permute-done | bytes 524320 | tf_op jit(solution)/shard_map/ppermute | solution.py:670
  669.3 9.1 %all-to-all-done.2 = bf16[8,72,640]{2,1,0:T(8,128)(2,1)S(1)} async-done(((bf16[8,72,640]{2,1,0:T(8,128)(2,1)}), bf16[8,72,640]{2,1,0:T(8,128)(2,1)S(1)}, u32[]{:S(2)}, u32[]{:S(2)}) %all-to-all-start.2) | async-done | bytes 737312 | tf_op jit(solution)/shard_map/all_to_all | solution.py:965
  (696 shorter events, 367.8 us)
Async XLA Ops:
  7.2 67.8 %all-gather.8.cloned.1.call-start = ((), (), s32[]{:S(2)}) async-start(), calls=%async_computation.10 | async-start | bytes 4718592 | tf_op jit(solution)/shard_map/all_gather | solution.py:712
  61.1 42.3 %all-to-all-start.1 = ((bf16[8,48,2048]{2,1,0:T(8,128)(2,1)}), bf16[8,48,2048]{2,1,0:T(8,128)(2,1)}, u32[]{:S(2)}, u32[]{:S(2)}) async-start(bf16[8,48,2048]{2,1,0:T(8,128)(2,1)} %select_direct.1), calls=%async_computation.1 | async-start | bytes 3145728 | tf_op jit(solution)/shard_map/all_to_all | solution.py:762
  65.4 61.1 %all-gather.6.cloned.1.call-start = ((), (), s32[]{:S(2)}) async-start(), calls=%async_computation.6 | async-start | bytes 2621440 | tf_op jit(solution)/shard_map/all_gather | solution.py:713
  74.6 25.8 %collective-permute-start.2 = (bf16[8,72,640]{2,1,0:T(8,128)(2,1)}, bf16[8,72,640]{2,1,0:T(8,128)(2,1)}, u32[]{:S(2)}, u32[]{:S(2)}) collective-permute-start(bf16[8,72,640]{2,1,0:T(8,128)(2,1)} %collective-permute-done.1), channel_id=1, source_target_pairs={{0,1},{1,2},{2,3},{3,0},{4,5},{5,6},{6,7},{7,4},{8,9},{9,10},{10,1... | collective-permute-start | bytes 2211848 | tf_op jit(solution)/shard_map/ppermute | solution.py:676
  75.0 127.5 %all-gather.10.cloned.1.call-start = ((), (), s32[]{:S(2)}) async-start(), calls=%async_computation.11 | async-start | bytes 2621440 | tf_op jit(solution)/shard_map/all_gather | solution.py:778
  126.5 468.9 %reduce-scatter.4.cloned.1.call-start = ((), (), s32[]{:S(2)}) async-start(), calls=%async_computation.7 | async-start | bytes 1310720 | tf_op jit(solution)/shard_map/reduce_scatter | solution.py:933
  212.2 26.5 %collective-permute-start.18 = (bf16[128,2048]{1,0:T(8,128)(2,1)}, bf16[128,2048]{1,0:T(8,128)(2,1)S(1)}, u32[]{:S(2)}, u32[]{:S(2)}) collective-permute-start(bf16[128,2048]{1,0:T(8,128)(2,1)} %collective-permute-done.12.refs_0_), channel_id=1, source_target_pairs={{0,1},{1,2},{2,3},{3,0},{4,5},{5,6},{6,7},{7,4},{8,9},{9,10},{10,1... | collective-permute-start | bytes 1572872 | tf_op jit(solution)/shard_map/ppermute | solution.py:676
  212.2 47.3 %collective-permute-start.24 = (bf16[128,2048]{1,0:T(8,128)(2,1)S(1)}, bf16[128,2048]{1,0:T(8,128)(2,1)S(1)}, u32[]{:S(2)}, u32[]{:S(2)}) collective-permute-start(bf16[128,2048]{1,0:T(8,128)(2,1)S(1)} %get-tuple-element.442.refs_1_), channel_id=1, source_target_pairs={{0,4},{4,0},{8,12},{12,8},{16,20},{20,16},{24,28},{28,24},{1,5},{5... | collective-permute-start | bytes 1572872 | tf_op jit(solution)/shard_map/ppermute | solution.py:670
  218.6 36.5 %collective-permute-start.21 = (bf16[2,96,2048]{2,1,0:T(8,128)(2,1)S(1)}, bf16[2,96,2048]{2,1,0:T(8,128)(2,1)S(1)}, u32[]{:S(2)}, u32[]{:S(2)}) collective-permute-start(bf16[2,96,2048]{2,1,0:T(8,128)(2,1)S(1)} %get-tuple-element.238), channel_id=1, source_target_pairs={{0,16},{4,20},{8,24},{12,28},{16,0},{20,4},{24,8},{28,12},{1,17},{... | collective-permute-start | bytes 2359304 | tf_op jit(solution)/shard_map/ppermute | solution.py:670
  219.2 35.9 %collective-permute-start.22 = (bf16[2,96,2048]{2,1,0:T(8,128)(2,1)S(1)}, bf16[2,96,2048]{2,1,0:T(8,128)(2,1)S(1)}, u32[]{:S(2)}, u32[]{:S(2)}) collective-permute-start(bf16[2,96,2048]{2,1,0:T(8,128)(2,1)S(1)} %get-tuple-element.239), channel_id=1, source_target_pairs={{0,24},{4,28},{8,16},{12,20},{16,8},{20,12},{24,0},{28,4},{1,25},{... | collective-permute-start | bytes 2359304 | tf_op jit(solution)/shard_map/ppermute | solution.py:670
  259.4 43.3 %collective-permute-start.29 = (bf16[128,2048]{1,0:T(8,128)(2,1)S(1)}, bf16[128,2048]{1,0:T(8,128)(2,1)S(1)}, u32[]{:S(2)}, u32[]{:S(2)}) collective-permute-start(bf16[128,2048]{1,0:T(8,128)(2,1)S(1)} %get-tuple-element.441.refs_1_), channel_id=1, source_target_pairs={{0,4},{4,0},{8,12},{12,8},{16,20},{20,16},{24,28},{28,24},{1,5},{5... | collective-permute-start | bytes 1572872 | tf_op jit(solution)/shard_map/ppermute | solution.py:670
  263.6 36.5 %collective-permute-start.26 = (bf16[2,96,2048]{2,1,0:T(8,128)(2,1)S(1)}, bf16[2,96,2048]{2,1,0:T(8,128)(2,1)S(1)}, u32[]{:S(2)}, u32[]{:S(2)}) collective-permute-start(bf16[2,96,2048]{2,1,0:T(8,128)(2,1)S(1)} %get-tuple-element.248), channel_id=1, source_target_pairs={{0,16},{4,20},{8,24},{12,28},{16,0},{20,4},{24,8},{28,12},{1,17},{... | collective-permute-start | bytes 2359304 | tf_op jit(solution)/shard_map/ppermute | solution.py:670
  265.0 35.0 %collective-permute-start.27 = (bf16[2,96,2048]{2,1,0:T(8,128)(2,1)S(1)}, bf16[2,96,2048]{2,1,0:T(8,128)(2,1)S(1)}, u32[]{:S(2)}, u32[]{:S(2)}) collective-permute-start(bf16[2,96,2048]{2,1,0:T(8,128)(2,1)S(1)} %get-tuple-element.249), channel_id=1, source_target_pairs={{0,24},{4,28},{8,16},{12,20},{16,8},{20,12},{24,0},{28,4},{1,25},{... | collective-permute-start | bytes 2359304 | tf_op jit(solution)/shard_map/ppermute | solution.py:670
  307.4 36.4 %collective-permute-start.31 = (bf16[2,96,2048]{2,1,0:T(8,128)(2,1)S(1)}, bf16[2,96,2048]{2,1,0:T(8,128)(2,1)S(1)}, u32[]{:S(2)}, u32[]{:S(2)}) collective-permute-start(bf16[2,96,2048]{2,1,0:T(8,128)(2,1)S(1)} %get-tuple-element.260), channel_id=1, source_target_pairs={{0,16},{4,20},{8,24},{12,28},{16,0},{20,4},{24,8},{28,12},{1,17},{... | collective-permute-start | bytes 2359304 | tf_op jit(solution)/shard_map/ppermute | solution.py:670
  308.1 35.9 %collective-permute-start.32 = (bf16[2,96,2048]{2,1,0:T(8,128)(2,1)S(1)}, bf16[2,96,2048]{2,1,0:T(8,128)(2,1)}, u32[]{:S(2)}, u32[]{:S(2)}) collective-permute-start(bf16[2,96,2048]{2,1,0:T(8,128)(2,1)S(1)} %get-tuple-element.262), channel_id=1, source_target_pairs={{0,24},{4,28},{8,16},{12,20},{16,8},{20,12},{24,0},{28,4},{1,25},{... | collective-permute-start | bytes 2359304 | tf_op jit(solution)/shard_map/ppermute | solution.py:670
  445.0 25.0 %collective-permute-start.55 = (bf16[128,2048]{1,0:T(8,128)(2,1)S(1)}, bf16[128,2048]{1,0:T(8,128)(2,1)}, u32[]{:S(2)}, u32[]{:S(2)}) collective-permute-start(bf16[128,2048]{1,0:T(8,128)(2,1)S(1)} %get-tuple-element.435), channel_id=1, source_target_pairs={{0,16},{4,20},{8,24},{12,28},{16,0},{20,4},{24,8},{28,12},{1,17},{... | collective-permute-start | bytes 1572872 | tf_op jit(solution)/shard_map/ppermute | solution.py:670
  485.3 25.4 %collective-permute-start.62 = (bf16[128,2048]{1,0:T(8,128)(2,1)}, bf16[128,2048]{1,0:T(8,128)(2,1)}, u32[]{:S(2)}, u32[]{:S(2)}) collective-permute-start(bf16[128,2048]{1,0:T(8,128)(2,1)} %constant_dynamic-slice_fusion), channel_id=1, source_target_pairs={{0,1},{1,2},{2,3},{3,0},{4,5},{5,6},{6,7},{7,4},{8,9},{9,10},{10,1... | collective-permute-start | bytes 1572872 | tf_op jit(solution)/shard_map/ppermute | solution.py:676
  507.1 25.6 %collective-permute-start.63 = (bf16[96,2048]{1,0:T(8,128)(2,1)}, bf16[96,2048]{1,0:T(8,128)(2,1)S(1)}, u32[]{:S(2)}, u32[]{:S(2)}) collective-permute-start(bf16[96,2048]{1,0:T(8,128)(2,1)} %get-tuple-element.360), channel_id=1, source_target_pairs={{0,8},{4,12},{8,0},{12,4},{16,24},{20,28},{24,16},{28,20},{1,9},{5... | collective-permute-start | bytes 1179656 | tf_op jit(solution)/shard_map/ppermute | solution.py:670
  508.2 24.5 %collective-permute-start.64 = (bf16[96,2048]{1,0:T(8,128)(2,1)}, bf16[96,2048]{1,0:T(8,128)(2,1)}, u32[]{:S(2)}, u32[]{:S(2)}) collective-permute-start(bf16[96,2048]{1,0:T(8,128)(2,1)} %get-tuple-element.362), channel_id=1, source_target_pairs={{0,16},{4,20},{8,24},{12,28},{16,0},{20,4},{24,8},{28,12},{1,17},{... | collective-permute-start | bytes 1179656 | tf_op jit(solution)/shard_map/ppermute | solution.py:670
  532.7 26.3 %collective-permute-start.67 = (bf16[96,2048]{1,0:T(8,128)(2,1)}, bf16[96,2048]{1,0:T(8,128)(2,1)S(1)}, u32[]{:S(2)}, u32[]{:S(2)}) collective-permute-start(bf16[96,2048]{1,0:T(8,128)(2,1)} %get-tuple-element.374), channel_id=1, source_target_pairs={{0,8},{4,12},{8,0},{12,4},{16,24},{20,28},{24,16},{28,20},{1,9},{5... | collective-permute-start | bytes 1179656 | tf_op jit(solution)/shard_map/ppermute | solution.py:670
  533.9 25.9 %collective-permute-start.68 = (bf16[96,2048]{1,0:T(8,128)(2,1)}, bf16[96,2048]{1,0:T(8,128)(2,1)S(1)}, u32[]{:S(2)}, u32[]{:S(2)}) collective-permute-start(bf16[96,2048]{1,0:T(8,128)(2,1)} %get-tuple-element.376), channel_id=1, source_target_pairs={{0,16},{4,20},{8,24},{12,28},{16,0},{20,4},{24,8},{28,12},{1,17},{... | collective-permute-start | bytes 1179656 | tf_op jit(solution)/shard_map/ppermute | solution.py:670
  534.9 25.7 %collective-permute-start.69 = (bf16[96,2048]{1,0:T(8,128)(2,1)}, bf16[96,2048]{1,0:T(8,128)(2,1)S(1)}, u32[]{:S(2)}, u32[]{:S(2)}) collective-permute-start(bf16[96,2048]{1,0:T(8,128)(2,1)} %get-tuple-element.378), channel_id=1, source_target_pairs={{0,24},{4,28},{8,16},{12,20},{16,8},{20,12},{24,0},{28,4},{1,25},{... | collective-permute-start | bytes 1179656 | tf_op jit(solution)/shard_map/ppermute | solution.py:670
  561.8 72.3 %reduce-scatter.6.cloned.1.call-start = ((), (), s32[]{:S(2)}) async-start(), calls=%async_computation.8 | async-start | bytes 2211840 | tf_op jit(solution)/shard_map/reduce_scatter | solution.py:933
  595.5 89.4 %reduce-scatter.8.cloned.1.call-start = ((), (), s32[]{:S(2)}) async-start(), calls=%async_computation.9 | async-start | bytes 2621440 | tf_op jit(solution)/shard_map/reduce_scatter | solution.py:990
  (247 other events, 2659.6 us)
Sparse Core Ops, SparseCore 0:
  9.9 47.3 all-gather.7
  75.1 51.3 all-gather.5
  128.1 43.5 all-gather.9
  562.0 27.2 reduce-scatter.3
  595.6 38.5 reduce-scatter.5
  636.3 42.9 reduce-scatter.7

commit v3 on v2

--- a/solution.py
+++ b/solution.py
@@ -172,7 +172,7 @@
         out_shape=jax.ShapeDtypeStruct((rows, heads * HD), BF),
         scratch_shapes=[pltpu.VMEM((rows, HD), BF), pltpu.VMEM((rows, HD), BF)],
         compiler_params=pltpu.CompilerParams(vmem_limit_bytes=ATTN_LIMIT),
-        cost_estimate=cost(7),
+        cost_estimate=cost(13),
         name="attn_fw",
     )(raw, kraw, vraw, cos, sin, cos, sin, qgain, kgain)
 
@@ -200,7 +200,7 @@
         ],
         scratch_shapes=[pltpu.VMEM((rows, HD), BF), pltpu.VMEM((rows, HD), BF)],
         compiler_params=pltpu.CompilerParams(vmem_limit_bytes=ATTN_LIMIT),
-        cost_estimate=cost(12),
+        cost_estimate=cost(22),
         name="attn_bw",
     )(raw, kraw, vraw, cos, sin, cos, sin, qgain, kgain, gout, *start)
 
@@ -332,7 +332,6 @@
     return call(
         kernel,
         "select_rows",
-        micros=3,
         out_shape=[jax.ShapeDtypeStruct((count, block, D), BF)] * nchip,
         grid=(D // TILE,),
         in_specs=[whole(send)] + [column_tile(rows)] * (2 * count),
@@ -440,7 +439,7 @@
     outs = call(
         kernel,
         "expert_rows",
-        micros=14,
+        micros=2,
         out_shape=out_shape,
         grid_spec=pltpu.PrefetchScalarGridSpec(
             num_scalar_prefetch=1,
@@ -564,38 +563,31 @@
     )(index.reshape(1), values, weight, *extra)
 
 
-def output_grads(attn, grad_branch):
-    rows, size = attn.shape
-
-    def kernel(a, g, out):
-        out[...] = tn_dot(a[...], g[...]).astype(BF)
-
+def branch_grads(attn, pieces, devices, weight):
+    (rows, size), height = attn.shape, pieces[0].shape[0]
+
+    def kernel(at, a, w, *refs):
+        parts, (to_weight, to_attn, whole_g) = refs[: len(pieces)], refs[len(pieces) :]
+        for n, part in enumerate(parts):
+            first = pl.multiple_of(at[n] * height, height)
+            whole_g[pl.ds(first, height), :] = part[...]
+        for n in range(0, D, TILE):
+            to_weight[:, n : n + TILE] = tn_dot(a[...], whole_g[:, n : n + TILE]).astype(BF)
+        for n in range(0, rows, BLK):
+            to_attn[n : n + BLK, :] = nt_dot(whole_g[n : n + BLK, :], w[...]).astype(BF)
+
+    outs = [jax.ShapeDtypeStruct((size, D), BF), jax.ShapeDtypeStruct((rows, size), BF)]
     return call(
         kernel,
-        "output_grads",
-        micros=5,
-        out_shape=jax.ShapeDtypeStruct((size, D), BF),
-        grid=(D // TILE,),
-        in_specs=[whole(attn), column_tile(rows)],
-        out_specs=column_tile(size),
-    )(attn, grad_branch)
-
-
-def attn_grads(grad_branch, weight):
-    rows, size = grad_branch.shape[0], weight.shape[0]
-
-    def kernel(g, w, out):
-        out[...] = nt_dot(g[...], w[...]).astype(BF)
-
-    return call(
-        kernel,
-        "attn_grads",
-        micros=5,
-        out_shape=jax.ShapeDtypeStruct((rows, size), BF),
-        grid=(rows // BLK,),
-        in_specs=[pl.BlockSpec((BLK, D), lambda i: (i, 0)), whole(weight)],
-        out_specs=pl.BlockSpec((BLK, size), lambda i: (i, 0)),
-    )(grad_branch, weight)
+        "branch_grads",
+        micros=12,
+        out_shape=outs,
+        grid=(1,),
+        in_specs=[pl.BlockSpec(memory_space=pltpu.SMEM)]
+        + [whole(v) for v in (attn, weight, *pieces)],
+        out_specs=[whole(v) for v in outs],
+        scratch_shapes=[pltpu.VMEM((rows, D), BF)],
+    )(devices, attn, weight, *pieces)
 
 
 def projection_grads(xa, grads, nc, ne, small=None):
@@ -612,7 +604,7 @@
     return call(
         kernel,
         "projection_grads",
-        micros=3,
+        micros=8,
         out_shape=jax.ShapeDtypeStruct((ne, nc, high, size), BF),
         grid=(nc,),
         in_specs=[pl.BlockSpec((rows, ne * wrows), lambda i: (0, i)), whole(grads)]
@@ -681,24 +673,19 @@
     def place(step, other):
         return (chip ^ step) * 2 + (1 - core if other else core)
 
-    def gather_ctx(values, out):
+    def gather_ctx(values):
         got = [values] + [None] * (nchip - 1)
         for step in range(nchip - 1, 0, -1):
             got[step] = peer(values, step)
-        for step in range(nchip):
-            out = lax.dynamic_update_slice_in_dim(out, got[step], place(step, False) * rows, 0)
-            out = lax.dynamic_update_slice_in_dim(
-                out, mate(got[step]), place(step, True) * rows, 0
-            )
-        return out
-
-    def scatter_ctx(values, weight, height):
+        return [v for part in got for v in (part, mate(part))]
+
+    def scatter_ctx(values, weight, height, *late):
         def part(step, other, theirs, dtype):
             return part_product(values, place(step, other), rows, weight, height, theirs, dtype)
 
         arrived, sent = [], []
         for step in list(range(nchip - 1, 0, -1)) + [0]:
-            theirs = mate(part(step, True, None, BF))
+            theirs = after(mate(part(step, True, None, BF)), *late)
             mine = part(step, False, theirs, BF if step else F32)
             sent.append(mine)
             if step:
@@ -783,7 +770,7 @@
         return [peer(picked[m], m) for m in range(nchip - 1, -1, -1)][::-1]
 
     cos, sin = (jnp.asarray(v) for v in rope_tables(seq))
-    x_all = after(x_all, cot_first)
+    x_all = after(x_all, cot_first, send[max(0, ne - 2)], row_chosen[max(0, ne - 2)])
     xa, raw = project(x_all, gain_attn, w_in, wrows)
     q_raw = raw[:, :width]
     kv_own = raw[:, width:]
@@ -796,15 +783,9 @@
         ordered.append(chosen)
     kv_raw = jnp.concatenate(ordered, axis=1) if share > 1 else ordered[0]
     k_raw, v_raw = kv_raw[:, :HD], kv_raw[:, HD:]
-    near = heads // 2
-    attn_near = attn_forward(q_raw, k_raw, v_raw, cos, sin, gain_query, gain_key, 0, near)
-    k_far = after(k_raw, attn_near, w_out)
-    attn_far = attn_forward(
-        q_raw, k_far, v_raw, cos, sin, gain_query, gain_key, near, heads - near
-    )
-    attn = jnp.concatenate([attn_near, attn_far], axis=1)
+    attn = attn_forward(q_raw, k_raw, v_raw, cos, sin, gain_query, gain_key, 0, heads)
     w_gate, w_up, w_down = gate_weight[0], up_weight[0], down_weight[0]
-    cot_all = after(cot_all, attn_far)
+    cot_all = after(cot_all, attn)
     cot_moving = [
         lax.dynamic_index_in_dim(cot_all, (ei - step) % ne, 0, keepdims=False)
         for step in range(ne)
@@ -819,19 +800,17 @@
     lane = (lax.iota(jnp.int32, lanes)[None, :] == ci * ne + ei).astype(F32)
     column = lane[:, :experts]
     ffn_moving = [ffn_in]
-    for _ in range(1, ne):
+    for _ in range(1, min(ne, 2)):
         ffn_moving.append(along(ffn_moving[-1]))
     arrived, done, mixed, back_home = [None] * ne, [], [], {}
 
-    def send_chunk(step, *others):
+    def pick_chunk(step, *others):
         values = [after(ffn_moving[step], *others)]
         mates = [mate(values[0])]
         if step:
             values.append(cot_moving[step])
             mates.append(cot_mates[step])
-        picked = select_rows(send[step], values, mates)
-        arrived[step] = to_experts(picked)
-        return picked[0]
+        return select_rows(send[step], values, mates)
 
     def run_chunk(step, *others):
         rows_in = [after(v, *others) for v in arrived[step]]
@@ -848,12 +827,24 @@
         back_home[step] = to_experts(backs)
 
     order = list(range(1, ne)) + [0]
-    tick = send_chunk(0)
+    picked = {0: pick_chunk(0)}
+    arrived[0] = to_experts(picked[0])
+    if ne > 1:
+        picked[1] = pick_chunk(1, picked[0][0])
+    for _ in range(2, ne):
+        ffn_moving.append(along(after(ffn_moving[-1], *arrived[0])))
+    tick, outs = picked[0][0], []
     for step in range(ne):
         if step + 1 < ne:
-            tick = send_chunk(step + 1, tick, *arrived[step])
+            ready = picked[step + 1]
+            arrived[step + 1] = to_experts([after(v, tick, *arrived[step]) for v in ready])
+            tick = ready[0]
+        if step + 2 < ne:
+            picked[step + 2] = pick_chunk(step + 2, tick, *arrived[step])
+            tick = picked[step + 2][0]
         tick = run_chunk(step, tick)
-    waits = arrived[-1]
+        outs.append(tick)
+    waits = arrived[-1] + outs[-2:-1]
     for step in order:
         give_back(step, *waits)
         waits = back_home[step]
@@ -895,19 +886,17 @@
     grad_router = tn_dot(ffn_in, grad_logits_low)
     grad_gain_ffn = jnp.sum(grad_ffn_in * normed_res, axis=0)
 
-    grad_branch = gather_ctx(grad_residual.astype(BF), x_all)
-    far_width = (heads - heads // 2) * HD + piece
+    pieces = gather_ctx(grad_residual.astype(BF))
     small = jnp.concatenate(
         [grad_router.reshape(nc, ne, wrows * experts), grad_gain_ffn.reshape(nc, ne, gain_rows)],
         axis=2,
     )
     ends = small.shape[2]
-    extra = -(-(-(-ends // far_width) + 1) // 8) * 8
-    small = jnp.pad(small, ((0, 0), (0, 0), (0, (extra - 1) * far_width - ends)))
-    small = small.transpose(1, 0, 2).astype(BF).reshape(ne, nc, extra - 1, far_width)
-    grad_branch = after(grad_branch, small)
-    grad_output = output_grads(attn, grad_branch)
-    grad_branch_late = after(grad_branch, grad_output)
+    extra = -(-(-(-ends // total_width) + 1) // 8) * 8
+    small = jnp.pad(small, ((0, 0), (0, 0), (0, (extra - 1) * total_width - ends)))
+    small = small.transpose(1, 0, 2).astype(BF).reshape(ne, nc, extra - 1, total_width)
+    pieces[0] = after(pieces[0], small)
+    grad_output, grad_attn = branch_grads(attn, pieces, devices, w_out)
     orows = output_weight.shape[0]
 
     def output_part(step):
@@ -919,28 +908,18 @@
     output_sum = output_part(0).astype(F32)
     if ne > 1:
         output_sum = output_sum + along(output_ring[-1]).astype(F32)
-    grad_attn = attn_grads(grad_branch_late, w_out)
-
-    mix_home, waits = [], (grad_branch,)
-    for blocks in mixed:
+
+    mix_home, waits = [], pieces[1:]
+    for blocks in mixed[:2]:
         waits = to_experts([after(v, *waits) for v in blocks])
         mix_home.append(waits)
-    grad_attn = after(grad_attn, *mix_home[0], output_ring[1 % len(output_ring)])
-
-    def weight_grad(earlier, grads, *small):
-        local = projection_grads(xa, grads, nc, ne, *small)
-        late = after(local, earlier)
-        return local, lax.psum_scatter(late, "exp", scatter_dimension=0, tiled=True)[0]
-
-    grad_q_near, *start = attn_backward(
-        q_raw, k_raw, v_raw, cos, sin, gain_query, gain_key, grad_attn, 0, near, ()
-    )
-    local_near, grad_w_near = weight_grad(grad_output, grad_q_near)
-    grad_attn = after(grad_attn, local_near, *mix_home[1], output_ring[-1])
-    grad_q_far, grad_k, grad_v, grad_gain_query = attn_backward(
-        q_raw, k_raw, v_raw, cos, sin, gain_query, gain_key, grad_attn, near, heads - near, start
-    )
-    grad_k = after(grad_k, *mix_home[2], output_sum)
+
+    grad_q_low, grad_k, grad_v, grad_gain_query = attn_backward(
+        q_raw, k_raw, v_raw, cos, sin, gain_query, gain_key, grad_attn, 0, heads, ()
+    )
+    grad_q_low, grad_k, grad_v, grad_gain_query, *_ = lax.optimization_barrier(
+        (grad_q_low, grad_k, grad_v, grad_gain_query) + tuple(mix_home[0])
+    )
     gks = [grad_k] + [mate(grad_k, bit) for bit in range(1, share)]
     gvs = [grad_v] + [mate(grad_v, bit) for bit in range(1, share)]
     grad_k_low, grad_v_low, grad_gain_key = key_backward(k_raw, cos, sin, gain_key, gks, gvs)
@@ -948,8 +927,7 @@
     grad_kv = jnp.concatenate([grad_k_low, grad_v_low], axis=1)
     if share > 1:
         grad_kv = lax.dynamic_slice_in_dim(grad_kv, member * piece, piece, 1)
-    grad_far = jnp.concatenate([grad_q_far, grad_kv], axis=1)
-    grad_in = jnp.concatenate([grad_q_near, grad_far], axis=1)
+    grad_in = jnp.concatenate([grad_q_low, grad_kv], axis=1)
     gains = jnp.concatenate(
         [
             grad_gain_query.reshape(nc, ne, head_rows),
@@ -957,19 +935,19 @@
         ],
         axis=2,
     )
-    gains = jnp.pad(gains, ((0, 0), (0, 0), (0, far_width - 2 * head_rows)))
-    gains = gains.transpose(1, 0, 2).astype(BF).reshape(ne, nc, 1, far_width)
-    local_far, grad_w_far = weight_grad(grad_w_near, grad_far, (small, gains))
-    grad_in = after(grad_in, local_far, *(v for blocks in mix_home[3:] for v in blocks))
-    grad_w_near = jnp.pad(grad_w_near, ((0, 0), (0, extra), (0, 0)))
+    gains = jnp.pad(gains, ((0, 0), (0, 0), (0, total_width - 2 * head_rows)))
+    gains = gains.transpose(1, 0, 2).astype(BF).reshape(ne, nc, 1, total_width)
+    local = projection_grads(xa, grad_in, nc, ne, (small, gains))
+    grad_in = after(grad_in, local, output_ring[-1], *mix_home[1 % ne])
+    waits = [grad_in]
+    for blocks in mixed[2:]:
+        waits = to_experts([after(v, *waits) for v in blocks])
+        mix_home.append(waits)
+    grad_w_sum = lax.psum_scatter(local, "exp", scatter_dimension=0, tiled=True)[0]
     grad_w = lax.all_to_all(
-        jnp.concatenate([grad_w_near, grad_w_far], axis=2),
-        "ctx",
-        split_axis=0,
-        concat_axis=0,
-        tiled=True,
+        grad_w_sum, "ctx", split_axis=0, concat_axis=0, tiled=True
     ).astype(F32)
-    small = jnp.sum(grad_w[:, wrows:, near * HD :], axis=0)
+    small = jnp.sum(grad_w[:, wrows:], axis=0)
     gains, small = small[-1], small[:-1].reshape(-1)
     grad_w = grad_w[:, :wrows]
     sum_query = grad_w[:, :, :width].transpose(1, 0, 2).reshape(wrows, H * HD)
@@ -982,11 +960,11 @@
         + jnp.sum(sum_value * value_weight.astype(F32), axis=1)
     ) / attn_gain.astype(F32)
 
-    grad_xa, sent = scatter_ctx(grad_in, w_in, wrows)
+    grad_xa, sent = scatter_ctx(grad_in, w_in, wrows, *mix_home[2 % ne], output_sum)
     mix_home[0][0] = after(mix_home[0][0], *sent)
     mine, theirs = combine_all(send, planes, mix_home)
     mixture = (mine.astype(F32) + mate(theirs).astype(F32)).astype(BF)
-    mixture = after(mixture, grad_w_far)
+    mixture = after(mixture, grad_w_sum)
     mixture = lax.psum_scatter(mixture, "exp", scatter_dimension=0, tiled=True)[0].astype(F32)
     inv_in = inv_rms(inputs)
     normed_in = inputs * inv_in

time: 705 us -> 636 us (0.902)
  local copies, waits for them, and re-layouts: 101 us -> 73.9 us
  blocking collectives: 21.8 us -> 0 us
  waiting for transfers between devices: 226 us -> 207 us
    ppermute x72, waiting for transfers between devices: 143 us -> 115 us  [mate(): return lax.ppermute(values, 'ctx', [(i, i ^ bit) for i in range(nc)])]
    all_to_all x1 -> x0, blocking collectives: 21.8 us -> none  [on_device(): part = lax.all_to_all(part, 'ctx', split_axis=0, concat_axis=0, tiled=True)]
    all_to_all x1 -> x2, waiting for transfers between devices: 9.14 us -> 25.6 us  [the longest x1 16.8 us: on_device(): part = lax.all_to_all(part, 'ctx', split_axis=0, concat_axis=0, tiled=True)]
    unnamed x374 -> x304, local copies, waits for them, and re-layouts: 68 us -> 54.3 us
    ppermute x12, waiting for transfers between devices: 61.9 us -> 50.8 us  [along(): return lax.ppermute(values, 'exp', [(i, (i + 1) % ne) for i in range(ne)])]
    all_gather x1, waiting for transfers between devices: 3.05 us -> 12.6 us  [on_device(): lax.all_gather(after(output_weight, x_all), 'exp', axis=0, tiled=True)]
    dynamic_update_slice x7 -> x0, local copies, waits for them, and re-layouts: 9.02 us -> none  [the longest x3 4.64 us: gather_ctx(): lax.dynamic_update_slice_in_dim(out, got[step], place(step, False) * rows...]
    pallas_call x12 -> x10, Pallas kernels: 89.8 us -> 87.7 us  [the longest x4 58.8 us: expert_rows(): call(kernel, 'expert_rows', micros=2, out_shape=out_shape, grid_spec=pltp...]
  transfers between devices with their start and end apart: 92 -> 92, of which waited for: 32 -> 35; matrix products, arithmetic and copies ran while one was open for 9% -> 8% of each run, Pallas kernels for 30% -> 33%
where the time goes in v3:
time: 636 us; the launch traced here: 625 us
  Pallas kernels  212 us (33%)
  waiting for transfers between devices  207 us (33%)
  starting transfers between devices  81.8 us (13%)
  local copies, waits for them, and re-layouts  73.9 us (12%)
  other arithmetic  32.3 us (5%)
  between operations  15.7 us (2%)
    ppermute x72, waiting for transfers between devices, mate(): return lax.ppermute(values, 'ctx', [(i, i ^ bit) for i in range(nc)])  115 us
    pallas_call x4, Pallas kernels, expert_rows(): call(kernel, 'expert_rows', micros=2, out_shape=out_shape, grid_spec=pltp...  58.8 us
    ppermute x72, starting transfers between devices, mate(): return lax.ppermute(values, 'ctx', [(i, i ^ bit) for i in range(nc)])  57.6 us
    unnamed x304, local copies, waits for them, and re-layouts  54.3 us
    ppermute x12, waiting for transfers between devices, along(): return lax.ppermute(values, 'exp', [(i, (i + 1) % ne) for i in range(ne)])  50.8 us
    pallas_call x16, Pallas kernels, part_product(): call(kernel, 'part_product', micros=2, out_shape=jax.ShapeDtypeStruct((ro...  33.9 us
    pallas_call x1, Pallas kernels, attn_backward(): pl.pallas_call(lambda *refs: attn_backward_kernel(blocks, *refs), grid=(h...  21.7 us
    pallas_call x2, Pallas kernels, grad_in_weight(): call(kernel, 'grad_in_weight', micros=10, out_shape=jax.ShapeDtypeStruct(...  20.1 us
  transfers between devices with their start and end apart: 92, of which 35 were waited for; matrix products, arithmetic and copies ran while one was open for 8% of the time, Pallas kernels for 33%

profile of v3, /device:TPU:0, one launch (start us, length us, event | category | flops | bytes accessed | tf_op | source)
XLA Modules:
  0.0 624.8 jit_solution(17690805994347499039)
XLA Ops:
  20.5 16.8 %all-to-all-done = bf16[8,72,640]{2,1,0:T(8,128)(2,1)S(1)} async-done(((bf16[8,72,640]{2,1,0:T(8,128)(2,1)}), bf16[8,72,640]{2,1,0:T(8,128)(2,1)S(1)}, u32[]{:S(2)}, u32[]{:S(2)}) %all-to-all-start) | async-done | bytes 737312 | tf_op jit(solution)/shard_map/all_to_all | solution.py:725
  57.6 13.9 %collective-permute-done.1 = bf16[8,72,640]{2,1,0:T(8,128)(2,1)} collective-permute-done((bf16[8,72,640]{2,1,0:T(8,128)(2,1)}, bf16[8,72,640]{2,1,0:T(8,128)(2,1)}, u32[]{:S(2)}, u32[]{:S(2)}) %collective-permute-start.1) | collective-permute-done | bytes 737312 | tf_op jit(solution)/shard_map/ppermute | solution.py:668
  78.9 8.3 %collective-permute-done.2 = bf16[8,72,640]{2,1,0:T(8,128)(2,1)} collective-permute-done((bf16[8,72,640]{2,1,0:T(8,128)(2,1)}, bf16[8,72,640]{2,1,0:T(8,128)(2,1)}, u32[]{:S(2)}, u32[]{:S(2)}) %collective-permute-start.2) | collective-permute-done | bytes 737312 | tf_op jit(solution)/shard_map/ppermute | solution.py:668
  103.2 12.9 %attn_fw.1.part.a = bf16[1024,512]{1,0:T(8,128)(2,1)S(1)} custom-call(f32[1024,512]{1,0:T(8,128)S(1)} %slice.110.refs_0_, f32[1024,128]{1,0:T(8,128)S(1)} %get-tuple-element.465.refs_1_.refs_0_, f32[1024,128]{1,0:T(8,128)S(1)} %get-tuple-element.464.refs_2_, f32[1024,128]{1,0:T(8,128)S(1)} %copy-done.110, f32[1024,128]{1,0:T(8,128)S(1)} %copy-done.107, ...), custom_call_target="tpu_custom_call" | custom-call | flops 14300000256 | bytes 1000 | tf_op jit(solution)/shard_map/attn_fw/pallas_call | solution.py:167
  116.9 12.6 %all-gather.6.cloned.1.call-done.w = bf16[512,2048]{1,0:T(8,128)(2,1)} async-done(((bf16[128,2048]{1,0:T(8,128)(2,1)}), bf16[512,2048]{1,0:T(8,128)(2,1)}) %all-gather.6.cloned.1.call-update) | async-done | bytes 2097168 | tf_op jit(solution)/shard_map/all_gather | solution.py:700
  156.3 10.3 %collective-permute-done.8 = bf16[128,2048]{1,0:T(8,128)(2,1)} collective-permute-done((bf16[128,2048]{1,0:T(8,128)(2,1)}, bf16[128,2048]{1,0:T(8,128)(2,1)}, u32[]{:S(2)}, u32[]{:S(2)}) %collective-permute-start.8) | collective-permute-done | bytes 524320 | tf_op jit(solution)/shard_map/ppermute | solution.py:662
  178.8 8.4 %collective-permute-done.12.refs_0_ = bf16[128,2048]{1,0:T(8,128)(2,1)} collective-permute-done((bf16[128,2048]{1,0:T(8,128)(2,1)S(1)}, bf16[128,2048]{1,0:T(8,128)(2,1)}, u32[]{:S(2)}, u32[]{:S(2)}) %collective-permute-start.12) | collective-permute-done | bytes 524320 | tf_op jit(solution)/shard_map/ppermute | solution.py:668
  189.3 7.3 %collective-permute-done.14.refs_2_ = bf16[1,96,2048]{2,1,0:T(8,128)(2,1)} collective-permute-done((bf16[1,96,2048]{2,1,0:T(8,128)(2,1)}, bf16[1,96,2048]{2,1,0:T(8,128)(2,1)}, u32[]{:S(2)}, u32[]{:S(2)}) %collective-permute-start.14) | collective-permute-done | bytes 393248 | tf_op jit(solution)/shard_map/ppermute | solution.py:662
  221.9 14.9 %expert_rows.4 = (bf16[96,2176]{1,0:T(8,128)(2,1)S(1)}, bf16[96,2176]{1,0:T(8,128)(2,1)S(1)}, bf16[96,2176]{1,0:T(8,128)(2,1)S(1)}, bf16[96,2176]{1,0:T(8,128)(2...) custom-call(s32[8]{0:T(128)S(1)} %fusion.23._.at, ...), custom_call_target="tpu_custom_call" | custom-call | flops 2200000000 | bytes 1000 | tf_op jit(solution)/shard_map/expert_rows/pallas_call | solution.py:439
  251.6 14.3 %expert_rows.5 = (bf16[96,2176]{1,0:T(8,128)(2,1)S(1)}, bf16[96,2176]{1,0:T(8,128)(2,1)S(1)}, bf16[96,2176]{1,0:T(8,128)(2,1)S(1)}, bf16[96,2176]{1,0:T(8,128)(2...) custom-call(s32[8]{0:T(128)S(1)} %fusion.23._.at, ...), custom_call_target="tpu_custom_call" | custom-call | flops 2200000000 | bytes 1000 | tf_op jit(solution)/shard_map/expert_rows/pallas_call | solution.py:439
  269.7 7.6 %collective-permute-done.29.refs_3_.refs_12_ = bf16[2,96,2048]{2,1,0:T(8,128)(2,1)} collective-permute-done((bf16[2,96,2048]{2,1,0:T(8,128)(2,1)S(1)}, bf16[2,96,2048]{2,1,0:T(8,128)(2,1)}, u32[]{:S(2)}, u32[]{:S(2)}) %collective-permute-start.29) | collective-permute-done | bytes 786464 | tf_op jit(solution)/shard_map/ppermute | solution.py:662
  280.9 15.2 %expert_rows.6 = (bf16[96,2176]{1,0:T(8,128)(2,1)S(1)}, bf16[96,2176]{1,0:T(8,128)(2,1)S(1)}, bf16[96,2176]{1,0:T(8,128)(2,1)S(1)}, bf16[96,2176]{1,0:T(8,128)(2...) custom-call(s32[8]{0:T(128)S(1)} %fusion.23._.at, ...), custom_call_target="tpu_custom_call" | custom-call | flops 2200000000 | bytes 1000 | tf_op jit(solution)/shard_map/expert_rows/pallas_call | solution.py:439
  299.2 14.1 %collective-permute-done.32.refs_3_.refs_16_ = bf16[2,96,2048]{2,1,0:T(8,128)(2,1)} collective-permute-done((bf16[2,96,2048]{2,1,0:T(8,128)(2,1)S(1)}, bf16[2,96,2048]{2,1,0:T(8,128)(2,1)}, u32[]{:S(2)}, u32[]{:S(2)}) %collective-permute-start.32) | collective-permute-done | bytes 786464 | tf_op jit(solution)/shard_map/ppermute | solution.py:662
  316.9 14.5 %expert_rows.7 = (bf16[96,2176]{1,0:T(8,128)(2,1)S(1)}, bf16[96,2176]{1,0:T(8,128)(2,1)S(1)}, bf16[96,2176]{1,0:T(8,128)(2,1)S(1)}, bf16[96,2176]{1,0:T(8,128)(2...) custom-call(s32[8]{0:T(128)S(1)} %fusion.23._.at, ...), custom_call_target="tpu_custom_call" | custom-call | flops 2200000000 | bytes 1000 | tf_op jit(solution)/shard_map/expert_rows/pallas_call | solution.py:439
  341.6 10.3 %grad_in_weight.2 = f32[2048,768]{1,0:T(8,128)} custom-call(bf16[384,2048]{1,0:T(8,128)(2,1)S(1)} %copy-done.46, bf16[384,2048]{1,0:T(8,128)(2,1)S(1)} %copy-done.47, bf16[384,2048]{1,0:T(8,128)(2,1)} %get-tuple-element.279.refs_2_, bf16[384,2048]{1,0:T(8,128)(2,1)} %get-tuple-element.317.refs_3_, bf16[384,768]{1,0:T(8,128)(2,1)S(1)} %copy-done.55, ...), custom_call_target="tpu_custom_call" | custom-call | flops 11000000512 | bytes 1000 | tf_op jit(solution)/shard_map/grad_in_weight/pallas_call | solution.py:468
  364.4 9.8 %grad_in_weight.3 = f32[2048,768]{1,0:T(8,128)} custom-call(bf16[384,2048]{1,0:T(8,128)(2,1)S(1)} %copy-done.46, bf16[384,2048]{1,0:T(8,128)(2,1)S(1)} %copy-done.47, bf16[384,2048]{1,0:T(8,128)(2,1)} %get-tuple-element.279.refs_2_, bf16[384,2048]{1,0:T(8,128)(2,1)} %get-tuple-element.317.refs_3_, bf16[384,768]{1,0:T(8,128)(2,1)S(1)} %copy-done.50, ...), custom_call_target="tpu_custom_call" | custom-call | flops 11000000512 | bytes 1000 | tf_op jit(solution)/shard_map/grad_in_weight/pallas_call | solution.py:468
  391.3 10.0 %grad_down_weight.1 = f32[768,2048]{1,0:T(8,128)} custom-call(s32[8]{0:T(128)S(1)} %fusion.23._.at, bf16[384,768]{1,0:T(8,128)(2,1)S(1)} %copy-done.49, bf16[384,768]{1,0:T(8,128)(2,1)S(1)} %copy-done.52, bf16[384,768]{1,0:T(8,128)(2,1)S(1)} %copy-done.54, bf16[384,768]{1,0:T(8,128)(2,1)S(1)} %copy-done.57, ...), custom_call_target="tpu_custom_call" | custom-call | flops 11000000512 | bytes 1000 | tf_op jit(solution)/shard_map/grad_down_weight/pallas_call | solution.py:497
  418.3 9.4 %collective-permute-done.57.refs_6_ = bf16[128,2048]{1,0:T(8,128)(2,1)S(1)} collective-permute-done((bf16[128,2048]{1,0:T(8,128)(2,1)S(1)}, bf16[128,2048]{1,0:T(8,128)(2,1)S(1)}, u32[]{:S(2)}, u32[]{:S(2)}) %collective-permute-start.57) | collective-permute-done | bytes 524320 | tf_op jit(solution)/shard_map/ppermute | solution.py:662
  427.7 10.4 %collective-permute-done.55.refs_4_ = bf16[128,2048]{1,0:T(8,128)(2,1)S(1)} collective-permute-done((bf16[128,2048]{1,0:T(8,128)(2,1)S(1)}, bf16[128,2048]{1,0:T(8,128)(2,1)S(1)}, u32[]{:S(2)}, u32[]{:S(2)}) %collective-permute-start.55) | collective-permute-done | bytes 524320 | tf_op jit(solution)/shard_map/ppermute | solution.py:662
  456.0 21.7 %attn_bw.1 = (bf16[1024,512]{1,0:T(8,128)(2,1)S(1)}, f32[1024,128]{1,0:T(8,128)S(1)}, f32[1024,128]{1,0:T(8,128)S(1)}, f32[1,128]{1,0:T(1,128)S(1)}) custom-call(f32[1024,512]{1,0:T(8,128)S(1)} %copy-done.8, f32[1024,128]{1,0:T(8,128)S(1)} %get-tuple-element.465.refs_1_.refs_0_, f32[1024,128]{1,0:T(8,128)S(1)} %copy-done.19, f32[1024,128]{1,0:T(8,128)S(1)} %copy-done.111, ...), custom_call_target="tpu_custom_call" | custom-call | flops 24199999488 | bytes 1000 | tf_op jit(solution)/shard_map/attn_bw/pallas_call | solution.py:183
  491.5 7.5 %projection_grads.1 = bf16[4,8,72,640]{3,2,1,0:T(8,128)(2,1)S(1)} custom-call(bf16[1024,2048]{1,0:T(8,128)(2,1)} %get-tuple-element.389.x, bf16[1024,640]{1,0:T(8,128)(2,1)S(1)} %pad_maximum_fusion.g.part, bf16[4,8,7,640]{3,2,1,0:T(8,128)(2,1)S(1)} %copy.67.refs_0_, bf16[4,8,1,640]{3,2,1,0:T(2,128)(2,1)S(1)} %copy.68.refs_1_), custom_call_target="tpu_custom_call" | custom-call | flops 8800000000 | bytes 1000 | tf_op jit(solution)/shard_map/projection_grads/pallas_call | solution.py:604
  571.2 12.2 %collective-permute-done.81 = bf16[128,2048]{1,0:T(8,128)(2,1)} collective-permute-done((bf16[128,2048]{1,0:T(8,128)(2,1)S(1)}, bf16[128,2048]{1,0:T(8,128)(2,1)}, u32[]{:S(2)}, u32[]{:S(2)}) %collective-permute-start.81) | collective-permute-done | bytes 524320 | tf_op jit(solution)/shard_map/ppermute | solution.py:662
  583.4 10.4 %collective-permute-done.82 = bf16[128,2048]{1,0:T(8,128)(2,1)} collective-permute-done((bf16[128,2048]{1,0:T(8,128)(2,1)S(1)}, bf16[128,2048]{1,0:T(8,128)(2,1)}, u32[]{:S(2)}, u32[]{:S(2)}) %collective-permute-start.82) | collective-permute-done | bytes 524320 | tf_op jit(solution)/shard_map/ppermute | solution.py:662
  602.3 8.8 %all-to-all-done.2 = bf16[8,72,640]{2,1,0:T(8,128)(2,1)S(1)} async-done(((bf16[8,72,640]{2,1,0:T(8,128)(2,1)}), bf16[8,72,640]{2,1,0:T(8,128)(2,1)S(1)}, u32[]{:S(2)}, u32[]{:S(2)}) %all-to-all-start.2) | async-done | bytes 737312 | tf_op jit(solution)/shard_map/all_to_all | solution.py:947
  (610 shorter events, 327.6 us)
Async XLA Ops:
  7.2 71.7 %all-gather.8.cloned.1.call-start = ((), (), s32[]{:S(2)}) async-start(), calls=%async_computation.8 | async-start | bytes 4718592 | tf_op jit(solution)/shard_map/all_gather | solution.py:699
  43.6 47.4 %all-to-all-start.1 = ((bf16[8,48,2048]{2,1,0:T(8,128)(2,1)}), bf16[8,48,2048]{2,1,0:T(8,128)(2,1)}, u32[]{:S(2)}, u32[]{:S(2)}) async-start(bf16[8,48,2048]{2,1,0:T(8,128)(2,1)} %select_direct.1), calls=%async_computation.1 | async-start | bytes 3145728 | tf_op jit(solution)/shard_map/all_to_all | solution.py:749
  47.9 81.6 %all-gather.6.cloned.1.call-start = ((), (), s32[]{:S(2)}) async-start(), calls=%async_computation.5 | async-start | bytes 2621440 | tf_op jit(solution)/shard_map/all_gather | solution.py:700
  78.9 108.3 %all-gather.10.cloned.1.call-start = ((), (), s32[]{:S(2)}) async-start(), calls=%async_computation.9 | async-start | bytes 2621440 | tf_op jit(solution)/shard_map/all_gather | solution.py:765
  129.5 438.0 %reduce-scatter.3.cloned.1.call-start = ((), (), s32[]{:S(2)}) async-start(), calls=%async_computation.6 | async-start | bytes 3686400 | tf_op jit(solution)/shard_map/reduce_scatter | solution.py:946
  202.2 37.0 %collective-permute-start.24 = (bf16[2,96,2048]{2,1,0:T(8,128)(2,1)}, bf16[2,96,2048]{2,1,0:T(8,128)(2,1)S(1)}, u32[]{:S(2)}, u32[]{:S(2)}) collective-permute-start(bf16[2,96,2048]{2,1,0:T(8,128)(2,1)} %get-tuple-element.258), channel_id=1, source_target_pairs={{0,24},{4,28},{8,16},{12,20},{16,8},{20,12},{24,0},{28,4},{1,25},{... | collective-permute-start | bytes 2359304 | tf_op jit(solution)/shard_map/ppermute | solution.py:662
  203.4 36.8 %collective-permute-start.23 = (bf16[2,96,2048]{2,1,0:T(8,128)(2,1)}, bf16[2,96,2048]{2,1,0:T(8,128)(2,1)}, u32[]{:S(2)}, u32[]{:S(2)}) collective-permute-start(bf16[2,96,2048]{2,1,0:T(8,128)(2,1)} %get-tuple-element.256), channel_id=1, source_target_pairs={{0,16},{4,20},{8,24},{12,28},{16,0},{20,4},{24,8},{28,12},{1,17},{... | collective-permute-start | bytes 2359304 | tf_op jit(solution)/shard_map/ppermute | solution.py:662
  204.6 35.6 %collective-permute-start.22 = (bf16[2,96,2048]{2,1,0:T(8,128)(2,1)}, bf16[2,96,2048]{2,1,0:T(8,128)(2,1)}, u32[]{:S(2)}, u32[]{:S(2)}) collective-permute-start(bf16[2,96,2048]{2,1,0:T(8,128)(2,1)} %get-tuple-element.254), channel_id=1, source_target_pairs={{0,8},{4,12},{8,0},{12,4},{16,24},{20,28},{24,16},{28,20},{1,9},{5... | collective-permute-start | bytes 2359304 | tf_op jit(solution)/shard_map/ppermute | solution.py:662
  212.4 31.4 %collective-permute-start.21 = (bf16[128,2048]{1,0:T(8,128)(2,1)}, bf16[128,2048]{1,0:T(8,128)(2,1)}, u32[]{:S(2)}, u32[]{:S(2)}) collective-permute-start(bf16[128,2048]{1,0:T(8,128)(2,1)} %collective-permute-done.16.refs_0_), channel_id=1, source_target_pairs={{0,1},{1,2},{2,3},{3,0},{4,5},{5,6},{6,7},{7,4},{8,9},{9,10},{10,1... | collective-permute-start | bytes 1572872 | tf_op jit(solution)/shard_map/ppermute | solution.py:668
  240.2 29.5 %collective-permute-start.27 = (bf16[2,96,2048]{2,1,0:T(8,128)(2,1)S(1)}, bf16[2,96,2048]{2,1,0:T(8,128)(2,1)}, u32[]{:S(2)}, u32[]{:S(2)}) collective-permute-start(bf16[2,96,2048]{2,1,0:T(8,128)(2,1)S(1)} %get-tuple-element.269), channel_id=1, source_target_pairs={{0,8},{4,12},{8,0},{12,4},{16,24},{20,28},{24,16},{28,20},{1,9},{5... | collective-permute-start | bytes 2359304 | tf_op jit(solution)/shard_map/ppermute | solution.py:662
  241.1 28.6 %collective-permute-start.28 = (bf16[2,96,2048]{2,1,0:T(8,128)(2,1)S(1)}, bf16[2,96,2048]{2,1,0:T(8,128)(2,1)}, u32[]{:S(2)}, u32[]{:S(2)}) collective-permute-start(bf16[2,96,2048]{2,1,0:T(8,128)(2,1)S(1)} %get-tuple-element.271), channel_id=1, source_target_pairs={{0,16},{4,20},{8,24},{12,28},{16,0},{20,4},{24,8},{28,12},{1,17},{... | collective-permute-start | bytes 2359304 | tf_op jit(solution)/shard_map/ppermute | solution.py:662
  242.0 35.4 %collective-permute-start.29 = (bf16[2,96,2048]{2,1,0:T(8,128)(2,1)S(1)}, bf16[2,96,2048]{2,1,0:T(8,128)(2,1)}, u32[]{:S(2)}, u32[]{:S(2)}) collective-permute-start(bf16[2,96,2048]{2,1,0:T(8,128)(2,1)S(1)} %get-tuple-element.273), channel_id=1, source_target_pairs={{0,24},{4,28},{8,16},{12,20},{16,8},{20,12},{24,0},{28,4},{1,25},{... | collective-permute-start | bytes 2359304 | tf_op jit(solution)/shard_map/ppermute | solution.py:662
  279.6 33.7 %collective-permute-start.32 = (bf16[2,96,2048]{2,1,0:T(8,128)(2,1)S(1)}, bf16[2,96,2048]{2,1,0:T(8,128)(2,1)}, u32[]{:S(2)}, u32[]{:S(2)}) collective-permute-start(bf16[2,96,2048]{2,1,0:T(8,128)(2,1)S(1)} %get-tuple-element.288), channel_id=1, source_target_pairs={{0,24},{4,28},{8,16},{12,20},{16,8},{20,12},{24,0},{28,4},{1,25},{... | collective-permute-start | bytes 2359304 | tf_op jit(solution)/shard_map/ppermute | solution.py:662
  413.4 24.7 %collective-permute-start.55 = (bf16[128,2048]{1,0:T(8,128)(2,1)S(1)}, bf16[128,2048]{1,0:T(8,128)(2,1)S(1)}, u32[]{:S(2)}, u32[]{:S(2)}) collective-permute-start(bf16[128,2048]{1,0:T(8,128)(2,1)S(1)} %get-tuple-element.372.refs_0_), channel_id=1, source_target_pairs={{0,16},{4,20},{8,24},{12,28},{16,0},{20,4},{24,8},{28,12},{1,17},{... | collective-permute-start | bytes 1572872 | tf_op jit(solution)/shard_map/ppermute | solution.py:662
  415.5 24.2 %collective-permute-start.52 = (bf16[128,2048]{1,0:T(8,128)(2,1)S(1)}, bf16[128,2048]{1,0:T(8,128)(2,1)}, u32[]{:S(2)}, u32[]{:S(2)}) collective-permute-start(bf16[128,2048]{1,0:T(8,128)(2,1)S(1)} %get-tuple-element.372.refs_0_), channel_id=1, source_target_pairs={{0,4},{4,0},{8,12},{12,8},{16,20},{20,16},{24,28},{28,24},{1,5},{5... | collective-permute-start | bytes 1572872 | tf_op jit(solution)/shard_map/ppermute | solution.py:662
  440.8 37.0 %collective-permute-start.59 = (bf16[96,2048]{1,0:T(8,128)(2,1)}, bf16[96,2048]{1,0:T(8,128)(2,1)S(1)}, u32[]{:S(2)}, u32[]{:S(2)}) collective-permute-start(bf16[96,2048]{1,0:T(8,128)(2,1)} %get-tuple-element.379), channel_id=1, source_target_pairs={{0,8},{4,12},{8,0},{12,4},{16,24},{20,28},{24,16},{28,20},{1,9},{5... | collective-permute-start | bytes 1179656 | tf_op jit(solution)/shard_map/ppermute | solution.py:662
  442.2 36.4 %collective-permute-start.60 = (bf16[96,2048]{1,0:T(8,128)(2,1)}, bf16[96,2048]{1,0:T(8,128)(2,1)S(1)}, u32[]{:S(2)}, u32[]{:S(2)}) collective-permute-start(bf16[96,2048]{1,0:T(8,128)(2,1)} %get-tuple-element.381), channel_id=1, source_target_pairs={{0,16},{4,20},{8,24},{12,28},{16,0},{20,4},{24,8},{28,12},{1,17},{... | collective-permute-start | bytes 1179656 | tf_op jit(solution)/shard_map/ppermute | solution.py:662
  442.8 36.5 %collective-permute-start.61 = (bf16[96,2048]{1,0:T(8,128)(2,1)}, bf16[96,2048]{1,0:T(8,128)(2,1)S(1)}, u32[]{:S(2)}, u32[]{:S(2)}) collective-permute-start(bf16[96,2048]{1,0:T(8,128)(2,1)} %get-tuple-element.383), channel_id=1, source_target_pairs={{0,24},{4,28},{8,16},{12,20},{16,8},{20,12},{24,0},{28,4},{1,25},{... | collective-permute-start | bytes 1179656 | tf_op jit(solution)/shard_map/ppermute | solution.py:662
  454.1 28.6 %collective-permute-start.64 = (bf16[128,2048]{1,0:T(8,128)(2,1)}, bf16[128,2048]{1,0:T(8,128)(2,1)}, u32[]{:S(2)}, u32[]{:S(2)}) collective-permute-start(bf16[128,2048]{1,0:T(8,128)(2,1)} %constant_dynamic-slice_fusion), channel_id=1, source_target_pairs={{0,1},{1,2},{2,3},{3,0},{4,5},{5,6},{6,7},{7,4},{8,9},{9,10},{10,1... | collective-permute-start | bytes 1572872 | tf_op jit(solution)/shard_map/ppermute | solution.py:668
  480.7 25.3 %collective-permute-start.66 = (bf16[96,2048]{1,0:T(8,128)(2,1)}, bf16[96,2048]{1,0:T(8,128)(2,1)}, u32[]{:S(2)}, u32[]{:S(2)}) collective-permute-start(bf16[96,2048]{1,0:T(8,128)(2,1)} %copy-done.94), channel_id=1, source_target_pairs={{0,8},{4,12},{8,0},{12,4},{16,24},{20,28},{24,16},{28,20},{1,9},{5... | collective-permute-start | bytes 1179656 | tf_op jit(solution)/shard_map/ppermute | solution.py:662
  481.3 24.7 %collective-permute-start.67 = (bf16[96,2048]{1,0:T(8,128)(2,1)}, bf16[96,2048]{1,0:T(8,128)(2,1)}, u32[]{:S(2)}, u32[]{:S(2)}) collective-permute-start(bf16[96,2048]{1,0:T(8,128)(2,1)} %copy-done.93), channel_id=1, source_target_pairs={{0,16},{4,20},{8,24},{12,28},{16,0},{20,4},{24,8},{28,12},{1,17},{... | collective-permute-start | bytes 1179656 | tf_op jit(solution)/shard_map/ppermute | solution.py:662
  501.8 114.3 %reduce-scatter.5.cloned.1.call-start = ((), (), s32[]{:S(2)}) async-start(), calls=%async_computation.7 | async-start | bytes 2621440 | tf_op jit(solution)/shard_map/reduce_scatter | solution.py:968
  504.6 24.8 %collective-permute-start.73 = (bf16[128,2048]{1,0:T(8,128)(2,1)}, bf16[128,2048]{1,0:T(8,128)(2,1)}, u32[]{:S(2)}, u32[]{:S(2)}) collective-permute-start(bf16[128,2048]{1,0:T(8,128)(2,1)} %dynamic-slice_add_fusion.1), channel_id=1, source_target_pairs={{0,1},{1,2},{2,3},{3,0},{4,5},{5,6},{6,7},{7,4},{8,9},{9,10},{10,1... | collective-permute-start | bytes 1572872 | tf_op jit(solution)/shard_map/ppermute | solution.py:668
  568.9 24.9 %collective-permute-start.82 = (bf16[128,2048]{1,0:T(8,128)(2,1)S(1)}, bf16[128,2048]{1,0:T(8,128)(2,1)}, u32[]{:S(2)}, u32[]{:S(2)}) collective-permute-start(bf16[128,2048]{1,0:T(8,128)(2,1)S(1)} %copy-done.61), channel_id=1, source_target_pairs={{0,16},{4,20},{8,24},{12,28},{16,0},{20,4},{24,8},{28,12},{1,17},{... | collective-permute-start | bytes 1572872 | tf_op jit(solution)/shard_map/ppermute | solution.py:662
  (212 other events, 1880.3 us)
Sparse Core Ops, SparseCore 0:
  9.9 51.8 all-gather.7
  79.0 50.4 all-gather.5
  131.0 44.8 all-gather.9
  502.0 65.5 reduce-scatter.2
  569.8 42.7 reduce-scatter.4

commit v4 on v3

--- a/solution.py
+++ b/solution.py
@@ -604,7 +604,7 @@
     return call(
         kernel,
         "projection_grads",
-        micros=8,
+        micros=2,
         out_shape=jax.ShapeDtypeStruct((ne, nc, high, size), BF),
         grid=(nc,),
         in_specs=[pl.BlockSpec((rows, ne * wrows), lambda i: (0, i)), whole(grads)]
@@ -897,17 +897,7 @@
     small = small.transpose(1, 0, 2).astype(BF).reshape(ne, nc, extra - 1, total_width)
     pieces[0] = after(pieces[0], small)
     grad_output, grad_attn = branch_grads(attn, pieces, devices, w_out)
-    orows = output_weight.shape[0]
-
-    def output_part(step):
-        return lax.dynamic_slice_in_dim(grad_output, ((ei - step) % ne) * orows, orows, 0)
-
-    output_ring = [output_part(1 % ne)]
-    for step in range(2, ne):
-        output_ring.append(output_part(step) + along(output_ring[-1]))
-    output_sum = output_part(0).astype(F32)
-    if ne > 1:
-        output_sum = output_sum + along(output_ring[-1]).astype(F32)
+    output_sum = lax.psum_scatter(grad_output, "exp", scatter_dimension=0, tiled=True)
 
     mix_home, waits = [], pieces[1:]
     for blocks in mixed[:2]:
@@ -938,11 +928,12 @@
     gains = jnp.pad(gains, ((0, 0), (0, 0), (0, total_width - 2 * head_rows)))
     gains = gains.transpose(1, 0, 2).astype(BF).reshape(ne, nc, 1, total_width)
     local = projection_grads(xa, grad_in, nc, ne, (small, gains))
-    grad_in = after(grad_in, local, output_ring[-1], *mix_home[1 % ne])
+    grad_in = after(grad_in, local, *mix_home[1 % ne])
     waits = [grad_in]
     for blocks in mixed[2:]:
         waits = to_experts([after(v, *waits) for v in blocks])
         mix_home.append(waits)
+    local = after(local, output_sum, *mix_home[1 % ne])
     grad_w_sum = lax.psum_scatter(local, "exp", scatter_dimension=0, tiled=True)[0]
     grad_w = lax.all_to_all(
         grad_w_sum, "ctx", split_axis=0, concat_axis=0, tiled=True
@@ -960,7 +951,7 @@
         + jnp.sum(sum_value * value_weight.astype(F32), axis=1)
     ) / attn_gain.astype(F32)
 
-    grad_xa, sent = scatter_ctx(grad_in, w_in, wrows, *mix_home[2 % ne], output_sum)
+    grad_xa, sent = scatter_ctx(grad_in, w_in, wrows, *mix_home[2 % ne])
     mix_home[0][0] = after(mix_home[0][0], *sent)
     mine, theirs = combine_all(send, planes, mix_home)
     mixture = (mine.astype(F32) + mate(theirs).astype(F32)).astype(BF)
@@ -988,7 +979,7 @@
         sum_query,
         sum_key,
         sum_value,
-        output_sum,
+        output_sum.astype(F32),
         small[:router_size].reshape(wrows, experts),
         grad_gate[None],
         grad_up[None],

time: 636 us -> 633 us (level)
  local copies, waits for them, and re-layouts: 73.9 us -> 84.4 us
  Pallas kernels: 212 us -> 203 us
  waiting for transfers between devices: 207 us -> 215 us
  starting transfers between devices: 81.8 us -> 74.8 us
    ppermute x72, waiting for transfers between devices: 115 us -> 128 us  [mate(): return lax.ppermute(values, 'ctx', [(i, i ^ bit) for i in range(nc)])]
    pallas_call x16, Pallas kernels: 33.9 us -> 24.6 us  [part_product(): call(kernel, 'part_product', micros=2, out_shape=jax.ShapeDtypeStruct((ro...]
    ppermute x12 -> x9, starting transfers between devices: 11 us -> 2.97 us  [along(): return lax.ppermute(values, 'exp', [(i, (i + 1) % ne) for i in range(ne)])]
    unnamed x304 -> x322, local copies, waits for them, and re-layouts: 54.3 us -> 62 us
    add x3 -> x0, other arithmetic: 6.78 us -> none  [the longest x2 4.48 us: on_device(): output_ring.append(output_part(step) + along(output_ring[-1]))]
    ppermute x12 -> x9, waiting for transfers between devices: 50.8 us -> 50 us  [along(): return lax.ppermute(values, 'exp', [(i, (i + 1) % ne) for i in range(ne)])]
  transfers between devices with their start and end apart: 92 -> 90, of which waited for: 35 -> 37; matrix products, arithmetic and copies ran while one was open for 8% -> 8% of each run, Pallas kernels for 33% -> 31%
where the time goes in v4:
time: 633 us; the launch traced here: 622 us
  waiting for transfers between devices  215 us (34%)
  Pallas kernels  203 us (32%)
  local copies, waits for them, and re-layouts  84.4 us (13%)
  starting transfers between devices  74.8 us (12%)
  other arithmetic  27.2 us (4%)
  between operations  16 us (3%)
    ppermute x72, waiting for transfers between devices, mate(): return lax.ppermute(values, 'ctx', [(i, i ^ bit) for i in range(nc)])  128 us
    unnamed x322, local copies, waits for them, and re-layouts  62 us
    ppermute x72, starting transfers between devices, mate(): return lax.ppermute(values, 'ctx', [(i, i ^ bit) for i in range(nc)])  57.9 us
    pallas_call x4, Pallas kernels, expert_rows(): call(kernel, 'expert_rows', micros=2, out_shape=out_shape, grid_spec=pltp...  57.8 us
    ppermute x9, waiting for transfers between devices, along(): return lax.ppermute(values, 'exp', [(i, (i + 1) % ne) for i in range(ne)])  50 us
    pallas_call x16, Pallas kernels, part_product(): call(kernel, 'part_product', micros=2, out_shape=jax.ShapeDtypeStruct((ro...  24.6 us
    pallas_call x1, Pallas kernels, attn_backward(): pl.pallas_call(lambda *refs: attn_backward_kernel(blocks, *refs), grid=(h...  22.7 us
    pallas_call x2, Pallas kernels, grad_in_weight(): call(kernel, 'grad_in_weight', micros=10, out_shape=jax.ShapeDtypeStruct(...  20.1 us
  transfers between devices with their start and end apart: 90, of which 37 were waited for; matrix products, arithmetic and copies ran while one was open for 8% of the time, Pallas kernels for 31%

profile of v4, /device:TPU:0, one launch (start us, length us, event | category | flops | bytes accessed | tf_op | source)
XLA Modules:
  0.0 622.5 jit_solution(309325750830957149)
XLA Ops:
  20.5 16.8 %all-to-all-done = bf16[8,72,640]{2,1,0:T(8,128)(2,1)S(1)} async-done(((bf16[8,72,640]{2,1,0:T(8,128)(2,1)}), bf16[8,72,640]{2,1,0:T(8,128)(2,1)S(1)}, u32[]{:S(2)}, u32[]{:S(2)}) %all-to-all-start) | async-done | bytes 737312 | tf_op jit(solution)/shard_map/all_to_all | solution.py:725
  57.6 13.9 %collective-permute-done.1 = bf16[8,72,640]{2,1,0:T(8,128)(2,1)} collective-permute-done((bf16[8,72,640]{2,1,0:T(8,128)(2,1)}, bf16[8,72,640]{2,1,0:T(8,128)(2,1)}, u32[]{:S(2)}, u32[]{:S(2)}) %collective-permute-start.1) | collective-permute-done | bytes 737312 | tf_op jit(solution)/shard_map/ppermute | solution.py:668
  78.9 8.3 %collective-permute-done.2 = bf16[8,72,640]{2,1,0:T(8,128)(2,1)} collective-permute-done((bf16[8,72,640]{2,1,0:T(8,128)(2,1)}, bf16[8,72,640]{2,1,0:T(8,128)(2,1)}, u32[]{:S(2)}, u32[]{:S(2)}) %collective-permute-start.2) | collective-permute-done | bytes 737312 | tf_op jit(solution)/shard_map/ppermute | solution.py:668
  103.6 12.8 %attn_fw.1.part.a = bf16[1024,512]{1,0:T(8,128)(2,1)S(1)} custom-call(f32[1024,512]{1,0:T(8,128)S(1)} %slice.110.refs_0_, f32[1024,128]{1,0:T(8,128)S(1)} %get-tuple-element.467.refs_1_.refs_0_, f32[1024,128]{1,0:T(8,128)S(1)} %get-tuple-element.466.refs_2_, f32[1024,128]{1,0:T(8,128)S(1)} %copy-done.109, f32[1024,128]{1,0:T(8,128)S(1)} %copy-done.106, ...), custom_call_target="tpu_custom_call" | custom-call | flops 14300000256 | bytes 1000 | tf_op jit(solution)/shard_map/attn_fw/pallas_call | solution.py:167
  118.1 11.3 %all-gather.6.cloned.1.call-done.w = bf16[512,2048]{1,0:T(8,128)(2,1)} async-done(((bf16[128,2048]{1,0:T(8,128)(2,1)}), bf16[512,2048]{1,0:T(8,128)(2,1)}) %all-gather.6.cloned.1.call-update) | async-done | bytes 2097168 | tf_op jit(solution)/shard_map/all_gather | solution.py:700
  156.6 10.6 %collective-permute-done.8 = bf16[128,2048]{1,0:T(8,128)(2,1)} collective-permute-done((bf16[128,2048]{1,0:T(8,128)(2,1)}, bf16[128,2048]{1,0:T(8,128)(2,1)}, u32[]{:S(2)}, u32[]{:S(2)}) %collective-permute-start.8) | collective-permute-done | bytes 524320 | tf_op jit(solution)/shard_map/ppermute | solution.py:662
  178.6 9.0 %collective-permute-done.12.refs_0_ = bf16[128,2048]{1,0:T(8,128)(2,1)S(1)} collective-permute-done((bf16[128,2048]{1,0:T(8,128)(2,1)S(1)}, bf16[128,2048]{1,0:T(8,128)(2,1)S(1)}, u32[]{:S(2)}, u32[]{:S(2)}) %collective-permute-start.12) | collective-permute-done | bytes 524320 | tf_op jit(solution)/shard_map/ppermute | solution.py:668
  221.3 14.0 %expert_rows.4 = (bf16[96,2176]{1,0:T(8,128)(2,1)S(1)}, bf16[96,2176]{1,0:T(8,128)(2,1)S(1)}, bf16[96,2176]{1,0:T(8,128)(2,1)S(1)}, bf16[96,2176]{1,0:T(8,128)(2...) custom-call(s32[8]{0:T(128)S(1)} %fusion.23._.at, ...), custom_call_target="tpu_custom_call" | custom-call | flops 2200000000 | bytes 1000 | tf_op jit(solution)/shard_map/expert_rows/pallas_call | solution.py:439
  250.7 14.4 %expert_rows.5 = (bf16[96,2176]{1,0:T(8,128)(2,1)S(1)}, bf16[96,2176]{1,0:T(8,128)(2,1)S(1)}, bf16[96,2176]{1,0:T(8,128)(2,1)S(1)}, bf16[96,2176]{1,0:T(8,128)(2...) custom-call(s32[8]{0:T(128)S(1)} %fusion.23._.at, ...), custom_call_target="tpu_custom_call" | custom-call | flops 2200000000 | bytes 1000 | tf_op jit(solution)/shard_map/expert_rows/pallas_call | solution.py:439
  268.1 8.5 %collective-permute-done.28.refs_2_.refs_11_ = bf16[2,96,2048]{2,1,0:T(8,128)(2,1)} collective-permute-done((bf16[2,96,2048]{2,1,0:T(8,128)(2,1)S(1)}, bf16[2,96,2048]{2,1,0:T(8,128)(2,1)}, u32[]{:S(2)}, u32[]{:S(2)}) %collective-permute-start.28) | collective-permute-done | bytes 786464 | tf_op jit(solution)/shard_map/ppermute | solution.py:662
  280.1 15.1 %expert_rows.6 = (bf16[96,2176]{1,0:T(8,128)(2,1)S(1)}, bf16[96,2176]{1,0:T(8,128)(2,1)S(1)}, bf16[96,2176]{1,0:T(8,128)(2,1)S(1)}, bf16[96,2176]{1,0:T(8,128)(2...) custom-call(s32[8]{0:T(128)S(1)} %fusion.23._.at, ...), custom_call_target="tpu_custom_call" | custom-call | flops 2200000000 | bytes 1000 | tf_op jit(solution)/shard_map/expert_rows/pallas_call | solution.py:439
  299.8 13.1 %collective-permute-done.31.refs_2_.refs_15_ = bf16[2,96,2048]{2,1,0:T(8,128)(2,1)S(1)} collective-permute-done((bf16[2,96,2048]{2,1,0:T(8,128)(2,1)S(1)}, bf16[2,96,2048]{2,1,0:T(8,128)(2,1)S(1)}, u32[]{:S(2)}, u32[]{:S(2)}) %collective-permute-start.31) | collective-permute-done | bytes 786464 | tf_op jit(solution)/shard_map/ppermute | solution.py:662
  317.6 14.4 %expert_rows.7 = (bf16[96,2176]{1,0:T(8,128)(2,1)S(1)}, bf16[96,2176]{1,0:T(8,128)(2,1)S(1)}, bf16[96,2176]{1,0:T(8,128)(2,1)S(1)}, bf16[96,2176]{1,0:T(8,128)(2...) custom-call(s32[8]{0:T(128)S(1)} %fusion.23._.at, ...), custom_call_target="tpu_custom_call" | custom-call | flops 2200000000 | bytes 1000 | tf_op jit(solution)/shard_map/expert_rows/pallas_call | solution.py:439
  341.2 10.3 %grad_in_weight.2 = f32[2048,768]{1,0:T(8,128)} custom-call(bf16[384,2048]{1,0:T(8,128)(2,1)S(1)} %copy-done.47, bf16[384,2048]{1,0:T(8,128)(2,1)S(1)} %copy-done.48, bf16[384,2048]{1,0:T(8,128)(2,1)} %get-tuple-element.280.refs_2_, bf16[384,2048]{1,0:T(8,128)(2,1)} %get-tuple-element.318.refs_3_, bf16[384,768]{1,0:T(8,128)(2,1)S(1)} %copy-done.56, ...), custom_call_target="tpu_custom_call" | custom-call | flops 11000000512 | bytes 1000 | tf_op jit(solution)/shard_map/grad_in_weight/pallas_call | solution.py:468
  362.7 9.8 %grad_in_weight.3 = f32[2048,768]{1,0:T(8,128)} custom-call(bf16[384,2048]{1,0:T(8,128)(2,1)S(1)} %copy-done.47, bf16[384,2048]{1,0:T(8,128)(2,1)S(1)} %copy-done.48, bf16[384,2048]{1,0:T(8,128)(2,1)} %get-tuple-element.280.refs_2_, bf16[384,2048]{1,0:T(8,128)(2,1)} %get-tuple-element.318.refs_3_, bf16[384,768]{1,0:T(8,128)(2,1)S(1)} %copy-done.51, ...), custom_call_target="tpu_custom_call" | custom-call | flops 11000000512 | bytes 1000 | tf_op jit(solution)/shard_map/grad_in_weight/pallas_call | solution.py:468
  389.6 10.0 %grad_down_weight.1 = f32[768,2048]{1,0:T(8,128)} custom-call(s32[8]{0:T(128)S(1)} %fusion.23._.at, bf16[384,768]{1,0:T(8,128)(2,1)S(1)} %copy-done.50, bf16[384,768]{1,0:T(8,128)(2,1)S(1)} %copy-done.53, bf16[384,768]{1,0:T(8,128)(2,1)S(1)} %copy-done.55, bf16[384,768]{1,0:T(8,128)(2,1)S(1)} %copy-done.58, ...), custom_call_target="tpu_custom_call" | custom-call | flops 11000000512 | bytes 1000 | tf_op jit(solution)/shard_map/grad_down_weight/pallas_call | solution.py:497
  418.6 8.1 %collective-permute-done.57.refs_6_ = bf16[128,2048]{1,0:T(8,128)(2,1)S(1)} collective-permute-done((bf16[128,2048]{1,0:T(8,128)(2,1)S(1)}, bf16[128,2048]{1,0:T(8,128)(2,1)S(1)}, u32[]{:S(2)}, u32[]{:S(2)}) %collective-permute-start.57) | collective-permute-done | bytes 524320 | tf_op jit(solution)/shard_map/ppermute | solution.py:662
  426.7 10.4 %collective-permute-done.55.refs_4_ = bf16[128,2048]{1,0:T(8,128)(2,1)S(1)} collective-permute-done((bf16[128,2048]{1,0:T(8,128)(2,1)S(1)}, bf16[128,2048]{1,0:T(8,128)(2,1)S(1)}, u32[]{:S(2)}, u32[]{:S(2)}) %collective-permute-start.55) | collective-permute-done | bytes 524320 | tf_op jit(solution)/shard_map/ppermute | solution.py:662
  456.5 22.7 %attn_bw.1 = (bf16[1024,512]{1,0:T(8,128)(2,1)S(1)}, f32[1024,128]{1,0:T(8,128)}, f32[1024,128]{1,0:T(8,128)}, f32[1,128]{1,0:T(1,128)S(1)}) custom-call(f32[1024,512]{1,0:T(8,128)S(1)} %copy-done.6, f32[1024,128]{1,0:T(8,128)S(1)} %copy-done.14, f32[1024,128]{1,0:T(8,128)S(1)} %copy-done.17, f32[1024,128]{1,0:T(8,128)S(1)} %copy-done.110, ...), custom_call_target="tpu_custom_call" | custom-call | flops 24199999488 | bytes 1000 | tf_op jit(solution)/shard_map/attn_bw/pallas_call | solution.py:183
  492.2 8.6 %projection_grads.1 = bf16[4,8,72,640]{3,2,1,0:T(8,128)(2,1)} custom-call(bf16[1024,2048]{1,0:T(8,128)(2,1)} %get-tuple-element.390.x, bf16[1024,640]{1,0:T(8,128)(2,1)S(1)} %pad_maximum_fusion.g.part, bf16[4,8,7,640]{3,2,1,0:T(8,128)(2,1)S(1)} %copy.67.refs_0_, bf16[4,8,1,640]{3,2,1,0:T(2,128)(2,1)S(1)} %copy.68.refs_1_), custom_call_target="tpu_custom_call" | custom-call | flops 2200000000 | bytes 1000 | tf_op jit(solution)/shard_map/projection_grads/pallas_call | solution.py:604
  516.5 10.6 %collective-permute-done.70.refs_15_ = bf16[96,2048]{1,0:T(8,128)(2,1)S(1)} collective-permute-done((bf16[96,2048]{1,0:T(8,128)(2,1)S(1)}, bf16[96,2048]{1,0:T(8,128)(2,1)S(1)}, u32[]{:S(2)}, u32[]{:S(2)}) %collective-permute-start.70) | collective-permute-done | bytes 393248 | tf_op jit(solution)/shard_map/ppermute | solution.py:662
  566.2 11.8 %collective-permute-done.78 = bf16[128,2048]{1,0:T(8,128)(2,1)} collective-permute-done((bf16[128,2048]{1,0:T(8,128)(2,1)S(1)}, bf16[128,2048]{1,0:T(8,128)(2,1)}, u32[]{:S(2)}, u32[]{:S(2)}) %collective-permute-start.78) | collective-permute-done | bytes 524320 | tf_op jit(solution)/shard_map/ppermute | solution.py:662
  578.0 10.4 %collective-permute-done.79 = bf16[128,2048]{1,0:T(8,128)(2,1)} collective-permute-done((bf16[128,2048]{1,0:T(8,128)(2,1)S(1)}, bf16[128,2048]{1,0:T(8,128)(2,1)}, u32[]{:S(2)}, u32[]{:S(2)}) %collective-permute-start.79) | collective-permute-done | bytes 524320 | tf_op jit(solution)/shard_map/ppermute | solution.py:662
  599.6 7.8 %all-to-all-done.2 = bf16[8,72,640]{2,1,0:T(8,128)(2,1)} async-done(((bf16[8,72,640]{2,1,0:T(8,128)(2,1)}), bf16[8,72,640]{2,1,0:T(8,128)(2,1)}, u32[]{:S(2)}, u32[]{:S(2)}) %all-to-all-start.2) | async-done | bytes 737312 | tf_op jit(solution)/shard_map/all_to_all | solution.py:938
  (622 shorter events, 323.8 us)
Async XLA Ops:
  7.2 71.6 %all-gather.8.cloned.1.call-start = ((), (), s32[]{:S(2)}) async-start(), calls=%async_computation.10 | async-start | bytes 4718592 | tf_op jit(solution)/shard_map/all_gather | solution.py:699
  43.6 47.3 %all-to-all-start.1 = ((bf16[8,48,2048]{2,1,0:T(8,128)(2,1)}), bf16[8,48,2048]{2,1,0:T(8,128)(2,1)}, u32[]{:S(2)}, u32[]{:S(2)}) async-start(bf16[8,48,2048]{2,1,0:T(8,128)(2,1)} %select_direct.1), calls=%async_computation.1 | async-start | bytes 3145728 | tf_op jit(solution)/shard_map/all_to_all | solution.py:749
  47.9 81.5 %all-gather.6.cloned.1.call-start = ((), (), s32[]{:S(2)}) async-start(), calls=%async_computation.6 | async-start | bytes 2621440 | tf_op jit(solution)/shard_map/all_gather | solution.py:700
  78.9 108.8 %all-gather.10.cloned.1.call-start = ((), (), s32[]{:S(2)}) async-start(), calls=%async_computation.11 | async-start | bytes 2621440 | tf_op jit(solution)/shard_map/all_gather | solution.py:765
  129.5 374.5 %reduce-scatter.4.cloned.1.call-start = ((), (), s32[]{:S(2)}) async-start(), calls=%async_computation.7 | async-start | bytes 2621440 | tf_op jit(solution)/shard_map/reduce_scatter | solution.py:900
  201.5 37.0 %collective-permute-start.24 = (bf16[2,96,2048]{2,1,0:T(8,128)(2,1)}, bf16[2,96,2048]{2,1,0:T(8,128)(2,1)S(1)}, u32[]{:S(2)}, u32[]{:S(2)}) collective-permute-start(bf16[2,96,2048]{2,1,0:T(8,128)(2,1)} %get-tuple-element.259), channel_id=1, source_target_pairs={{0,24},{4,28},{8,16},{12,20},{16,8},{20,12},{24,0},{28,4},{1,25},{... | collective-permute-start | bytes 2359304 | tf_op jit(solution)/shard_map/ppermute | solution.py:662
  202.1 36.8 %collective-permute-start.23 = (bf16[2,96,2048]{2,1,0:T(8,128)(2,1)}, bf16[2,96,2048]{2,1,0:T(8,128)(2,1)}, u32[]{:S(2)}, u32[]{:S(2)}) collective-permute-start(bf16[2,96,2048]{2,1,0:T(8,128)(2,1)} %get-tuple-element.257), channel_id=1, source_target_pairs={{0,16},{4,20},{8,24},{12,28},{16,0},{20,4},{24,8},{28,12},{1,17},{... | collective-permute-start | bytes 2359304 | tf_op jit(solution)/shard_map/ppermute | solution.py:662
  203.3 36.1 %collective-permute-start.22 = (bf16[2,96,2048]{2,1,0:T(8,128)(2,1)}, bf16[2,96,2048]{2,1,0:T(8,128)(2,1)}, u32[]{:S(2)}, u32[]{:S(2)}) collective-permute-start(bf16[2,96,2048]{2,1,0:T(8,128)(2,1)} %get-tuple-element.255), channel_id=1, source_target_pairs={{0,8},{4,12},{8,0},{12,4},{16,24},{20,28},{24,16},{28,20},{1,9},{5... | collective-permute-start | bytes 2359304 | tf_op jit(solution)/shard_map/ppermute | solution.py:662
  211.8 31.0 %collective-permute-start.21 = (bf16[128,2048]{1,0:T(8,128)(2,1)S(1)}, bf16[128,2048]{1,0:T(8,128)(2,1)}, u32[]{:S(2)}, u32[]{:S(2)}) collective-permute-start(bf16[128,2048]{1,0:T(8,128)(2,1)S(1)} %collective-permute-done.16.refs_0_), channel_id=1, source_target_pairs={{0,1},{1,2},{2,3},{3,0},{4,5},{5,6},{6,7},{7,4},{8,9},{9,10},{10,1... | collective-permute-start | bytes 1572872 | tf_op jit(solution)/shard_map/ppermute | solution.py:668
  239.3 28.8 %collective-permute-start.27 = (bf16[2,96,2048]{2,1,0:T(8,128)(2,1)S(1)}, bf16[2,96,2048]{2,1,0:T(8,128)(2,1)}, u32[]{:S(2)}, u32[]{:S(2)}) collective-permute-start(bf16[2,96,2048]{2,1,0:T(8,128)(2,1)S(1)} %get-tuple-element.270), channel_id=1, source_target_pairs={{0,8},{4,12},{8,0},{12,4},{16,24},{20,28},{24,16},{28,20},{1,9},{5... | collective-permute-start | bytes 2359304 | tf_op jit(solution)/shard_map/ppermute | solution.py:662
  240.0 36.6 %collective-permute-start.28 = (bf16[2,96,2048]{2,1,0:T(8,128)(2,1)S(1)}, bf16[2,96,2048]{2,1,0:T(8,128)(2,1)}, u32[]{:S(2)}, u32[]{:S(2)}) collective-permute-start(bf16[2,96,2048]{2,1,0:T(8,128)(2,1)S(1)} %get-tuple-element.272), channel_id=1, source_target_pairs={{0,16},{4,20},{8,24},{12,28},{16,0},{20,4},{24,8},{28,12},{1,17},{... | collective-permute-start | bytes 2359304 | tf_op jit(solution)/shard_map/ppermute | solution.py:662
  240.8 35.8 %collective-permute-start.29 = (bf16[2,96,2048]{2,1,0:T(8,128)(2,1)S(1)}, bf16[2,96,2048]{2,1,0:T(8,128)(2,1)}, u32[]{:S(2)}, u32[]{:S(2)}) collective-permute-start(bf16[2,96,2048]{2,1,0:T(8,128)(2,1)S(1)} %get-tuple-element.274), channel_id=1, source_target_pairs={{0,24},{4,28},{8,16},{12,20},{16,8},{20,12},{24,0},{28,4},{1,25},{... | collective-permute-start | bytes 2359304 | tf_op jit(solution)/shard_map/ppermute | solution.py:662
  276.6 23.2 %collective-permute-start.30 = (bf16[2,96,2048]{2,1,0:T(8,128)(2,1)S(1)}, bf16[2,96,2048]{2,1,0:T(8,128)(2,1)S(1)}, u32[]{:S(2)}, u32[]{:S(2)}) collective-permute-start(bf16[2,96,2048]{2,1,0:T(8,128)(2,1)S(1)} %get-tuple-element.283), channel_id=1, source_target_pairs={{0,8},{4,12},{8,0},{12,4},{16,24},{20,28},{24,16},{28,20},{1,9},{5... | collective-permute-start | bytes 2359304 | tf_op jit(solution)/shard_map/ppermute | solution.py:662
  277.2 35.7 %collective-permute-start.31 = (bf16[2,96,2048]{2,1,0:T(8,128)(2,1)S(1)}, bf16[2,96,2048]{2,1,0:T(8,128)(2,1)S(1)}, u32[]{:S(2)}, u32[]{:S(2)}) collective-permute-start(bf16[2,96,2048]{2,1,0:T(8,128)(2,1)S(1)} %get-tuple-element.286), channel_id=1, source_target_pairs={{0,16},{4,20},{8,24},{12,28},{16,0},{20,4},{24,8},{28,12},{1,17},{... | collective-permute-start | bytes 2359304 | tf_op jit(solution)/shard_map/ppermute | solution.py:662
  278.4 34.6 %collective-permute-start.32 = (bf16[2,96,2048]{2,1,0:T(8,128)(2,1)S(1)}, bf16[2,96,2048]{2,1,0:T(8,128)(2,1)S(1)}, u32[]{:S(2)}, u32[]{:S(2)}) collective-permute-start(bf16[2,96,2048]{2,1,0:T(8,128)(2,1)S(1)} %get-tuple-element.289), channel_id=1, source_target_pairs={{0,24},{4,28},{8,16},{12,20},{16,8},{20,12},{24,0},{28,4},{1,25},{... | collective-permute-start | bytes 2359304 | tf_op jit(solution)/shard_map/ppermute | solution.py:662
  412.2 24.9 %collective-permute-start.55 = (bf16[128,2048]{1,0:T(8,128)(2,1)S(1)}, bf16[128,2048]{1,0:T(8,128)(2,1)S(1)}, u32[]{:S(2)}, u32[]{:S(2)}) collective-permute-start(bf16[128,2048]{1,0:T(8,128)(2,1)S(1)} %get-tuple-element.373.refs_0_), channel_id=1, source_target_pairs={{0,16},{4,20},{8,24},{12,28},{16,0},{20,4},{24,8},{28,12},{1,17},{... | collective-permute-start | bytes 1572872 | tf_op jit(solution)/shard_map/ppermute | solution.py:662
  413.6 23.5 %collective-permute-start.53 = (bf16[128,2048]{1,0:T(8,128)(2,1)S(1)}, bf16[128,2048]{1,0:T(8,128)(2,1)S(1)}, u32[]{:S(2)}, u32[]{:S(2)}) collective-permute-start(bf16[128,2048]{1,0:T(8,128)(2,1)S(1)} %get-tuple-element.373.refs_0_), channel_id=1, source_target_pairs={{0,8},{4,12},{8,0},{12,4},{16,24},{20,28},{24,16},{28,20},{1,9},{5... | collective-permute-start | bytes 1572872 | tf_op jit(solution)/shard_map/ppermute | solution.py:662
  414.5 24.9 %collective-permute-start.52 = (bf16[128,2048]{1,0:T(8,128)(2,1)S(1)}, bf16[128,2048]{1,0:T(8,128)(2,1)S(1)}, u32[]{:S(2)}, u32[]{:S(2)}) collective-permute-start(bf16[128,2048]{1,0:T(8,128)(2,1)S(1)} %get-tuple-element.373.refs_0_), channel_id=1, source_target_pairs={{0,4},{4,0},{8,12},{12,8},{16,20},{20,16},{24,28},{28,24},{1,5},{5... | collective-permute-start | bytes 1572872 | tf_op jit(solution)/shard_map/ppermute | solution.py:662
  447.5 113.8 %reduce-scatter.6.cloned.1.call-start = ((), (), s32[]{:S(2)}) async-start(), calls=%async_computation.8 | async-start | bytes 3686400 | tf_op jit(solution)/shard_map/reduce_scatter | solution.py:937
  447.5 31.7 %collective-permute-start.59 = (bf16[96,2048]{1,0:T(8,128)(2,1)}, bf16[96,2048]{1,0:T(8,128)(2,1)S(1)}, u32[]{:S(2)}, u32[]{:S(2)}) collective-permute-start(bf16[96,2048]{1,0:T(8,128)(2,1)} %copy-done.99), channel_id=1, source_target_pairs={{0,8},{4,12},{8,0},{12,4},{16,24},{20,28},{24,16},{28,20},{1,9},{5... | collective-permute-start | bytes 1179656 | tf_op jit(solution)/shard_map/ppermute | solution.py:662
  448.7 31.2 %collective-permute-start.60 = (bf16[96,2048]{1,0:T(8,128)(2,1)}, bf16[96,2048]{1,0:T(8,128)(2,1)S(1)}, u32[]{:S(2)}, u32[]{:S(2)}) collective-permute-start(bf16[96,2048]{1,0:T(8,128)(2,1)} %copy-done.98), channel_id=1, source_target_pairs={{0,16},{4,20},{8,24},{12,28},{16,0},{20,4},{24,8},{28,12},{1,17},{... | collective-permute-start | bytes 1179656 | tf_op jit(solution)/shard_map/ppermute | solution.py:662
  449.4 31.3 %collective-permute-start.61 = (bf16[96,2048]{1,0:T(8,128)(2,1)}, bf16[96,2048]{1,0:T(8,128)(2,1)S(1)}, u32[]{:S(2)}, u32[]{:S(2)}) collective-permute-start(bf16[96,2048]{1,0:T(8,128)(2,1)} %copy-done.97), channel_id=1, source_target_pairs={{0,24},{4,28},{8,16},{12,20},{16,8},{20,12},{24,0},{28,4},{1,25},{... | collective-permute-start | bytes 1179656 | tf_op jit(solution)/shard_map/ppermute | solution.py:662
  504.0 109.5 %reduce-scatter.8.cloned.1.call-start = ((), (), s32[]{:S(2)}) async-start(), calls=%async_computation.9 | async-start | bytes 2621440 | tf_op jit(solution)/shard_map/reduce_scatter | solution.py:959
  564.6 23.7 %collective-permute-start.79 = (bf16[128,2048]{1,0:T(8,128)(2,1)S(1)}, bf16[128,2048]{1,0:T(8,128)(2,1)}, u32[]{:S(2)}, u32[]{:S(2)}) collective-permute-start(bf16[128,2048]{1,0:T(8,128)(2,1)S(1)} %copy-done.62), channel_id=1, source_target_pairs={{0,16},{4,20},{8,24},{12,28},{16,0},{20,4},{24,8},{28,12},{1,17},{... | collective-permute-start | bytes 1572872 | tf_op jit(solution)/shard_map/ppermute | solution.py:662
  (219 other events, 1821.2 us)
Sparse Core Ops, SparseCore 0:
  9.9 51.8 all-gather.7
  79.0 50.4 all-gather.5
  131.0 45.3 all-gather.9
  447.6 43.5 reduce-scatter.3
  504.1 57.1 reduce-scatter.5
  563.4 43.7 reduce-scatter.7

commit v5 on v4

--- a/solution.py
+++ b/solution.py
@@ -772,7 +772,6 @@
     cos, sin = (jnp.asarray(v) for v in rope_tables(seq))
     x_all = after(x_all, cot_first, send[max(0, ne - 2)], row_chosen[max(0, ne - 2)])
     xa, raw = project(x_all, gain_attn, w_in, wrows)
-    q_raw = raw[:, :width]
     kv_own = raw[:, width:]
     kv_parts = [kv_own] + [mate(kv_own, bit) for bit in range(1, share)]
     ordered = []
@@ -783,7 +782,7 @@
         ordered.append(chosen)
     kv_raw = jnp.concatenate(ordered, axis=1) if share > 1 else ordered[0]
     k_raw, v_raw = kv_raw[:, :HD], kv_raw[:, HD:]
-    attn = attn_forward(q_raw, k_raw, v_raw, cos, sin, gain_query, gain_key, 0, heads)
+    attn = attn_forward(raw, k_raw, v_raw, cos, sin, gain_query, gain_key, 0, heads)
     w_gate, w_up, w_down = gate_weight[0], up_weight[0], down_weight[0]
     cot_all = after(cot_all, attn)
     cot_moving = [
@@ -905,7 +904,7 @@
         mix_home.append(waits)
 
     grad_q_low, grad_k, grad_v, grad_gain_query = attn_backward(
-        q_raw, k_raw, v_raw, cos, sin, gain_query, gain_key, grad_attn, 0, heads, ()
+        raw, k_raw, v_raw, cos, sin, gain_query, gain_key, grad_attn, 0, heads, ()
     )
     grad_q_low, grad_k, grad_v, grad_gain_query, *_ = lax.optimization_barrier(
         (grad_q_low, grad_k, grad_v, grad_gain_query) + tuple(mix_home[0])

time: 633 us -> 635 us (level)
  waiting for transfers between devices: 215 us -> 225 us
  local copies, waits for them, and re-layouts: 84.4 us -> 74.9 us
    ppermute x72, waiting for transfers between devices: 128 us -> 136 us  [mate(): return lax.ppermute(values, 'ctx', [(i, i ^ bit) for i in range(nc)])]
    unnamed x322 -> x286, local copies, waits for them, and re-layouts: 62 us -> 58.1 us
  transfers between devices with their start and end apart: 90 -> 90, of which waited for: 37 -> 34; matrix products, arithmetic and copies ran while one was open for 8% -> 7% of each run, Pallas kernels for 31% -> 31%
where the time goes in v5:
time: 635 us; the launch traced here: 624 us
  waiting for transfers between devices  225 us (35%)
  Pallas kernels  207 us (33%)
  local copies, waits for them, and re-layouts  74.9 us (12%)
  starting transfers between devices  73.5 us (12%)
  other arithmetic  25.9 us (4%)
  between operations  16 us (3%)
    ppermute x72, waiting for transfers between devices, mate(): return lax.ppermute(values, 'ctx', [(i, i ^ bit) for i in range(nc)])  136 us
    pallas_call x4, Pallas kernels, expert_rows(): call(kernel, 'expert_rows', micros=2, out_shape=out_shape, grid_spec=pltp...  58.4 us
    unnamed x286, local copies, waits for them, and re-layouts  58.1 us
    ppermute x72, starting transfers between devices, mate(): return lax.ppermute(values, 'ctx', [(i, i ^ bit) for i in range(nc)])  57.4 us
    ppermute x9, waiting for transfers between devices, along(): return lax.ppermute(values, 'exp', [(i, (i + 1) % ne) for i in range(ne)])  50.3 us
    pallas_call x16, Pallas kernels, part_product(): call(kernel, 'part_product', micros=2, out_shape=jax.ShapeDtypeStruct((ro...  27.1 us
    pallas_call x1, Pallas kernels, attn_backward(): pl.pallas_call(lambda *refs: attn_backward_kernel(blocks, *refs), grid=(h...  22.5 us
    pallas_call x2, Pallas kernels, grad_in_weight(): call(kernel, 'grad_in_weight', micros=10, out_shape=jax.ShapeDtypeStruct(...  20.1 us
  transfers between devices with their start and end apart: 90, of which 34 were waited for; matrix products, arithmetic and copies ran while one was open for 7% of the time, Pallas kernels for 31%

profile of v5, /device:TPU:0, one launch (start us, length us, event | category | flops | bytes accessed | tf_op | source)
XLA Modules:
  0.0 624.0 jit_solution(14500404427904873039)
XLA Ops:
  20.5 16.8 %all-to-all-done = bf16[8,72,640]{2,1,0:T(8,128)(2,1)S(1)} async-done(((bf16[8,72,640]{2,1,0:T(8,128)(2,1)}), bf16[8,72,640]{2,1,0:T(8,128)(2,1)S(1)}, u32[]{:S(2)}, u32[]{:S(2)}) %all-to-all-start) | async-done | bytes 737312 | tf_op jit(solution)/shard_map/all_to_all | solution.py:725
  57.6 13.9 %collective-permute-done.1 = bf16[8,72,640]{2,1,0:T(8,128)(2,1)} collective-permute-done((bf16[8,72,640]{2,1,0:T(8,128)(2,1)}, bf16[8,72,640]{2,1,0:T(8,128)(2,1)}, u32[]{:S(2)}, u32[]{:S(2)}) %collective-permute-start.1) | collective-permute-done | bytes 737312 | tf_op jit(solution)/shard_map/ppermute | solution.py:668
  78.9 8.3 %collective-permute-done.2 = bf16[8,72,640]{2,1,0:T(8,128)(2,1)} collective-permute-done((bf16[8,72,640]{2,1,0:T(8,128)(2,1)}, bf16[8,72,640]{2,1,0:T(8,128)(2,1)}, u32[]{:S(2)}, u32[]{:S(2)}) %collective-permute-start.2) | collective-permute-done | bytes 737312 | tf_op jit(solution)/shard_map/ppermute | solution.py:668
  102.6 12.7 %attn_fw.1.part.a = bf16[1024,512]{1,0:T(8,128)(2,1)S(1)} custom-call(f32[1024,640]{1,0:T(8,128)S(1)} %copy-done.15, f32[1024,128]{1,0:T(8,128)S(1)} %get-tuple-element.467.refs_1_.refs_0_, f32[1024,128]{1,0:T(8,128)S(1)} %get-tuple-element.466.refs_2_, f32[1024,128]{1,0:T(8,128)S(1)} %copy-done.100, f32[1024,128]{1,0:T(8,128)S(1)} %copy-done.97, ...), custom_call_target="tpu_custom_call" | custom-call | flops 14300000256 | bytes 1000 | tf_op jit(solution)/shard_map/attn_fw/pallas_call | solution.py:167
  116.1 13.3 %all-gather.6.cloned.1.call-done.w = bf16[512,2048]{1,0:T(8,128)(2,1)} async-done(((bf16[128,2048]{1,0:T(8,128)(2,1)}), bf16[512,2048]{1,0:T(8,128)(2,1)}) %all-gather.6.cloned.1.call-update) | async-done | bytes 2097168 | tf_op jit(solution)/shard_map/all_gather | solution.py:700
  158.5 10.3 %collective-permute-done.8 = bf16[128,2048]{1,0:T(8,128)(2,1)} collective-permute-done((bf16[128,2048]{1,0:T(8,128)(2,1)}, bf16[128,2048]{1,0:T(8,128)(2,1)}, u32[]{:S(2)}, u32[]{:S(2)}) %collective-permute-start.8) | collective-permute-done | bytes 524320 | tf_op jit(solution)/shard_map/ppermute | solution.py:662
  189.8 8.0 %collective-permute-done.14.refs_2_ = bf16[1,96,2048]{2,1,0:T(8,128)(2,1)} collective-permute-done((bf16[1,96,2048]{2,1,0:T(8,128)(2,1)}, bf16[1,96,2048]{2,1,0:T(8,128)(2,1)}, u32[]{:S(2)}, u32[]{:S(2)}) %collective-permute-start.14) | collective-permute-done | bytes 393248 | tf_op jit(solution)/shard_map/ppermute | solution.py:662
  223.1 14.9 %expert_rows.4 = (bf16[96,2176]{1,0:T(8,128)(2,1)S(1)}, bf16[96,2176]{1,0:T(8,128)(2,1)S(1)}, bf16[96,2176]{1,0:T(8,128)(2,1)S(1)}, bf16[96,2176]{1,0:T(8,128)(2...) custom-call(s32[8]{0:T(128)S(1)} %fusion.23._.at, ...), custom_call_target="tpu_custom_call" | custom-call | flops 2200000000 | bytes 1000 | tf_op jit(solution)/shard_map/expert_rows/pallas_call | solution.py:439
  251.9 14.3 %expert_rows.5 = (bf16[96,2176]{1,0:T(8,128)(2,1)S(1)}, bf16[96,2176]{1,0:T(8,128)(2,1)S(1)}, bf16[96,2176]{1,0:T(8,128)(2,1)S(1)}, bf16[96,2176]{1,0:T(8,128)(2...) custom-call(s32[8]{0:T(128)S(1)} %fusion.23._.at, ...), custom_call_target="tpu_custom_call" | custom-call | flops 2200000000 | bytes 1000 | tf_op jit(solution)/shard_map/expert_rows/pallas_call | solution.py:439
  270.0 8.6 %collective-permute-done.28.refs_2_.refs_11_ = bf16[2,96,2048]{2,1,0:T(8,128)(2,1)} collective-permute-done((bf16[2,96,2048]{2,1,0:T(8,128)(2,1)S(1)}, bf16[2,96,2048]{2,1,0:T(8,128)(2,1)}, u32[]{:S(2)}, u32[]{:S(2)}) %collective-permute-start.28) | collective-permute-done | bytes 786464 | tf_op jit(solution)/shard_map/ppermute | solution.py:662
  282.1 14.6 %expert_rows.6 = (bf16[96,2176]{1,0:T(8,128)(2,1)S(1)}, bf16[96,2176]{1,0:T(8,128)(2,1)S(1)}, bf16[96,2176]{1,0:T(8,128)(2,1)S(1)}, bf16[96,2176]{1,0:T(8,128)(2...) custom-call(s32[8]{0:T(128)S(1)} %fusion.23._.at, ...), custom_call_target="tpu_custom_call" | custom-call | flops 2200000000 | bytes 1000 | tf_op jit(solution)/shard_map/expert_rows/pallas_call | solution.py:439
  299.1 15.7 %collective-permute-done.31.refs_2_.refs_15_ = bf16[2,96,2048]{2,1,0:T(8,128)(2,1)} collective-permute-done((bf16[2,96,2048]{2,1,0:T(8,128)(2,1)S(1)}, bf16[2,96,2048]{2,1,0:T(8,128)(2,1)}, u32[]{:S(2)}, u32[]{:S(2)}) %collective-permute-start.31) | collective-permute-done | bytes 786464 | tf_op jit(solution)/shard_map/ppermute | solution.py:662
  318.3 14.5 %expert_rows.7 = (bf16[96,2176]{1,0:T(8,128)(2,1)S(1)}, bf16[96,2176]{1,0:T(8,128)(2,1)S(1)}, bf16[96,2176]{1,0:T(8,128)(2,1)S(1)}, bf16[96,2176]{1,0:T(8,128)(2...) custom-call(s32[8]{0:T(128)S(1)} %fusion.23._.at, ...), custom_call_target="tpu_custom_call" | custom-call | flops 2200000000 | bytes 1000 | tf_op jit(solution)/shard_map/expert_rows/pallas_call | solution.py:439
  340.2 10.3 %grad_in_weight.2 = f32[2048,768]{1,0:T(8,128)} custom-call(bf16[384,2048]{1,0:T(8,128)(2,1)S(1)} %copy-done.39, bf16[384,2048]{1,0:T(8,128)(2,1)S(1)} %copy-done.40, bf16[384,2048]{1,0:T(8,128)(2,1)} %get-tuple-element.280.refs_2_, bf16[384,2048]{1,0:T(8,128)(2,1)} %get-tuple-element.318.refs_3_, bf16[384,768]{1,0:T(8,128)(2,1)S(1)} %copy-done.48, ...), custom_call_target="tpu_custom_call" | custom-call | flops 11000000512 | bytes 1000 | tf_op jit(solution)/shard_map/grad_in_weight/pallas_call | solution.py:468
  363.6 9.9 %grad_in_weight.3 = f32[2048,768]{1,0:T(8,128)} custom-call(bf16[384,2048]{1,0:T(8,128)(2,1)S(1)} %copy-done.39, bf16[384,2048]{1,0:T(8,128)(2,1)S(1)} %copy-done.40, bf16[384,2048]{1,0:T(8,128)(2,1)} %get-tuple-element.280.refs_2_, bf16[384,2048]{1,0:T(8,128)(2,1)} %get-tuple-element.318.refs_3_, bf16[384,768]{1,0:T(8,128)(2,1)S(1)} %copy-done.43, ...), custom_call_target="tpu_custom_call" | custom-call | flops 11000000512 | bytes 1000 | tf_op jit(solution)/shard_map/grad_in_weight/pallas_call | solution.py:468
  390.6 10.0 %grad_down_weight.1 = f32[768,2048]{1,0:T(8,128)} custom-call(s32[8]{0:T(128)S(1)} %fusion.23._.at, bf16[384,768]{1,0:T(8,128)(2,1)S(1)} %copy-done.42, bf16[384,768]{1,0:T(8,128)(2,1)S(1)} %copy-done.45, bf16[384,768]{1,0:T(8,128)(2,1)S(1)} %copy-done.47, bf16[384,768]{1,0:T(8,128)(2,1)S(1)} %copy-done.50, ...), custom_call_target="tpu_custom_call" | custom-call | flops 11000000512 | bytes 1000 | tf_op jit(solution)/shard_map/grad_down_weight/pallas_call | solution.py:497
  418.2 11.0 %collective-permute-done.57.refs_6_ = bf16[128,2048]{1,0:T(8,128)(2,1)S(1)} collective-permute-done((bf16[128,2048]{1,0:T(8,128)(2,1)S(1)}, bf16[128,2048]{1,0:T(8,128)(2,1)S(1)}, u32[]{:S(2)}, u32[]{:S(2)}) %collective-permute-start.57) | collective-permute-done | bytes 524320 | tf_op jit(solution)/shard_map/ppermute | solution.py:662
  429.2 10.4 %collective-permute-done.55.refs_4_ = bf16[128,2048]{1,0:T(8,128)(2,1)S(1)} collective-permute-done((bf16[128,2048]{1,0:T(8,128)(2,1)S(1)}, bf16[128,2048]{1,0:T(8,128)(2,1)S(1)}, u32[]{:S(2)}, u32[]{:S(2)}) %collective-permute-start.55) | collective-permute-done | bytes 524320 | tf_op jit(solution)/shard_map/ppermute | solution.py:662
  459.1 22.5 %attn_bw.1 = (bf16[1024,512]{1,0:T(8,128)(2,1)S(1)}, f32[1024,128]{1,0:T(8,128)}, f32[1024,128]{1,0:T(8,128)}, f32[1,128]{1,0:T(1,128)S(1)}) custom-call(f32[1024,640]{1,0:T(8,128)S(1)} %copy-done.16, f32[1024,128]{1,0:T(8,128)S(1)} %get-tuple-element.467.refs_1_.refs_0_, f32[1024,128]{1,0:T(8,128)S(1)} %copy-done.11, f32[1024,128]{1,0:T(8,128)S(1)} %copy-done.101, ...), custom_call_target="tpu_custom_call" | custom-call | flops 24199999488 | bytes 1000 | tf_op jit(solution)/shard_map/attn_bw/pallas_call | solution.py:183
  494.7 8.6 %projection_grads.1 = bf16[4,8,72,640]{3,2,1,0:T(8,128)(2,1)} custom-call(bf16[1024,2048]{1,0:T(8,128)(2,1)} %get-tuple-element.390.x, bf16[1024,640]{1,0:T(8,128)(2,1)S(1)} %pad_maximum_fusion.g.part, bf16[4,8,7,640]{3,2,1,0:T(8,128)(2,1)S(1)} %copy.67.refs_0_, bf16[4,8,1,640]{3,2,1,0:T(2,128)(2,1)S(1)} %copy.68.refs_1_), custom_call_target="tpu_custom_call" | custom-call | flops 2200000000 | bytes 1000 | tf_op jit(solution)/shard_map/projection_grads/pallas_call | solution.py:604
  518.1 10.6 %collective-permute-done.70.refs_15_ = bf16[96,2048]{1,0:T(8,128)(2,1)S(1)} collective-permute-done((bf16[96,2048]{1,0:T(8,128)(2,1)S(1)}, bf16[96,2048]{1,0:T(8,128)(2,1)S(1)}, u32[]{:S(2)}, u32[]{:S(2)}) %collective-permute-start.70) | collective-permute-done | bytes 393248 | tf_op jit(solution)/shard_map/ppermute | solution.py:662
  568.2 12.2 %collective-permute-done.78 = bf16[128,2048]{1,0:T(8,128)(2,1)} collective-permute-done((bf16[128,2048]{1,0:T(8,128)(2,1)S(1)}, bf16[128,2048]{1,0:T(8,128)(2,1)}, u32[]{:S(2)}, u32[]{:S(2)}) %collective-permute-start.78) | collective-permute-done | bytes 524320 | tf_op jit(solution)/shard_map/ppermute | solution.py:662
  580.4 10.4 %collective-permute-done.79 = bf16[128,2048]{1,0:T(8,128)(2,1)} collective-permute-done((bf16[128,2048]{1,0:T(8,128)(2,1)S(1)}, bf16[128,2048]{1,0:T(8,128)(2,1)}, u32[]{:S(2)}, u32[]{:S(2)}) %collective-permute-start.79) | collective-permute-done | bytes 524320 | tf_op jit(solution)/shard_map/ppermute | solution.py:662
  601.2 7.8 %all-to-all-done.2 = bf16[8,72,640]{2,1,0:T(8,128)(2,1)} async-done(((bf16[8,72,640]{2,1,0:T(8,128)(2,1)}), bf16[8,72,640]{2,1,0:T(8,128)(2,1)}, u32[]{:S(2)}, u32[]{:S(2)}) %all-to-all-start.2) | async-done | bytes 737312 | tf_op jit(solution)/shard_map/all_to_all | solution.py:937
  (585 shorter events, 318.6 us)
Async XLA Ops:
  7.2 71.7 %all-gather.8.cloned.1.call-start = ((), (), s32[]{:S(2)}) async-start(), calls=%async_computation.10 | async-start | bytes 4718592 | tf_op jit(solution)/shard_map/all_gather | solution.py:699
  42.9 46.6 %all-to-all-start.1 = ((bf16[8,48,2048]{2,1,0:T(8,128)(2,1)}), bf16[8,48,2048]{2,1,0:T(8,128)(2,1)}, u32[]{:S(2)}, u32[]{:S(2)}) async-start(bf16[8,48,2048]{2,1,0:T(8,128)(2,1)} %select_direct.1), calls=%async_computation.1 | async-start | bytes 3145728 | tf_op jit(solution)/shard_map/all_to_all | solution.py:749
  47.2 82.2 %all-gather.6.cloned.1.call-start = ((), (), s32[]{:S(2)}) async-start(), calls=%async_computation.6 | async-start | bytes 2621440 | tf_op jit(solution)/shard_map/all_gather | solution.py:700
  78.9 108.9 %all-gather.10.cloned.1.call-start = ((), (), s32[]{:S(2)}) async-start(), calls=%async_computation.11 | async-start | bytes 2621440 | tf_op jit(solution)/shard_map/all_gather | solution.py:765
  129.5 376.0 %reduce-scatter.4.cloned.1.call-start = ((), (), s32[]{:S(2)}) async-start(), calls=%async_computation.7 | async-start | bytes 2621440 | tf_op jit(solution)/shard_map/reduce_scatter | solution.py:899
  202.0 38.4 %collective-permute-start.24 = (bf16[2,96,2048]{2,1,0:T(8,128)(2,1)}, bf16[2,96,2048]{2,1,0:T(8,128)(2,1)S(1)}, u32[]{:S(2)}, u32[]{:S(2)}) collective-permute-start(bf16[2,96,2048]{2,1,0:T(8,128)(2,1)} %get-tuple-element.259), channel_id=1, source_target_pairs={{0,24},{4,28},{8,16},{12,20},{16,8},{20,12},{24,0},{28,4},{1,25},{... | collective-permute-start | bytes 2359304 | tf_op jit(solution)/shard_map/ppermute | solution.py:662
  203.4 37.1 %collective-permute-start.23 = (bf16[2,96,2048]{2,1,0:T(8,128)(2,1)}, bf16[2,96,2048]{2,1,0:T(8,128)(2,1)}, u32[]{:S(2)}, u32[]{:S(2)}) collective-permute-start(bf16[2,96,2048]{2,1,0:T(8,128)(2,1)} %get-tuple-element.257), channel_id=1, source_target_pairs={{0,16},{4,20},{8,24},{12,28},{16,0},{20,4},{24,8},{28,12},{1,17},{... | collective-permute-start | bytes 2359304 | tf_op jit(solution)/shard_map/ppermute | solution.py:662
  204.6 35.9 %collective-permute-start.22 = (bf16[2,96,2048]{2,1,0:T(8,128)(2,1)}, bf16[2,96,2048]{2,1,0:T(8,128)(2,1)}, u32[]{:S(2)}, u32[]{:S(2)}) collective-permute-start(bf16[2,96,2048]{2,1,0:T(8,128)(2,1)} %get-tuple-element.255), channel_id=1, source_target_pairs={{0,8},{4,12},{8,0},{12,4},{16,24},{20,28},{24,16},{28,20},{1,9},{5... | collective-permute-start | bytes 2359304 | tf_op jit(solution)/shard_map/ppermute | solution.py:662
  213.3 30.7 %collective-permute-start.21 = (bf16[128,2048]{1,0:T(8,128)(2,1)}, bf16[128,2048]{1,0:T(8,128)(2,1)}, u32[]{:S(2)}, u32[]{:S(2)}) collective-permute-start(bf16[128,2048]{1,0:T(8,128)(2,1)} %collective-permute-done.16.refs_0_), channel_id=1, source_target_pairs={{0,1},{1,2},{2,3},{3,0},{4,5},{5,6},{6,7},{7,4},{8,9},{9,10},{10,1... | collective-permute-start | bytes 1572872 | tf_op jit(solution)/shard_map/ppermute | solution.py:668
  240.5 29.5 %collective-permute-start.27 = (bf16[2,96,2048]{2,1,0:T(8,128)(2,1)S(1)}, bf16[2,96,2048]{2,1,0:T(8,128)(2,1)S(1)}, u32[]{:S(2)}, u32[]{:S(2)}) collective-permute-start(bf16[2,96,2048]{2,1,0:T(8,128)(2,1)S(1)} %get-tuple-element.270), channel_id=1, source_target_pairs={{0,8},{4,12},{8,0},{12,4},{16,24},{20,28},{24,16},{28,20},{1,9},{5... | collective-permute-start | bytes 2359304 | tf_op jit(solution)/shard_map/ppermute | solution.py:662
  242.0 36.6 %collective-permute-start.28 = (bf16[2,96,2048]{2,1,0:T(8,128)(2,1)S(1)}, bf16[2,96,2048]{2,1,0:T(8,128)(2,1)}, u32[]{:S(2)}, u32[]{:S(2)}) collective-permute-start(bf16[2,96,2048]{2,1,0:T(8,128)(2,1)S(1)} %get-tuple-element.272), channel_id=1, source_target_pairs={{0,16},{4,20},{8,24},{12,28},{16,0},{20,4},{24,8},{28,12},{1,17},{... | collective-permute-start | bytes 2359304 | tf_op jit(solution)/shard_map/ppermute | solution.py:662
  242.6 36.0 %collective-permute-start.29 = (bf16[2,96,2048]{2,1,0:T(8,128)(2,1)S(1)}, bf16[2,96,2048]{2,1,0:T(8,128)(2,1)}, u32[]{:S(2)}, u32[]{:S(2)}) collective-permute-start(bf16[2,96,2048]{2,1,0:T(8,128)(2,1)S(1)} %get-tuple-element.274), channel_id=1, source_target_pairs={{0,24},{4,28},{8,16},{12,20},{16,8},{20,12},{24,0},{28,4},{1,25},{... | collective-permute-start | bytes 2359304 | tf_op jit(solution)/shard_map/ppermute | solution.py:662
  279.2 35.6 %collective-permute-start.31 = (bf16[2,96,2048]{2,1,0:T(8,128)(2,1)S(1)}, bf16[2,96,2048]{2,1,0:T(8,128)(2,1)}, u32[]{:S(2)}, u32[]{:S(2)}) collective-permute-start(bf16[2,96,2048]{2,1,0:T(8,128)(2,1)S(1)} %get-tuple-element.286), channel_id=1, source_target_pairs={{0,16},{4,20},{8,24},{12,28},{16,0},{20,4},{24,8},{28,12},{1,17},{... | collective-permute-start | bytes 2359304 | tf_op jit(solution)/shard_map/ppermute | solution.py:662
  280.3 34.5 %collective-permute-start.32 = (bf16[2,96,2048]{2,1,0:T(8,128)(2,1)S(1)}, bf16[2,96,2048]{2,1,0:T(8,128)(2,1)}, u32[]{:S(2)}, u32[]{:S(2)}) collective-permute-start(bf16[2,96,2048]{2,1,0:T(8,128)(2,1)S(1)} %get-tuple-element.289), channel_id=1, source_target_pairs={{0,24},{4,28},{8,16},{12,20},{16,8},{20,12},{24,0},{28,4},{1,25},{... | collective-permute-start | bytes 2359304 | tf_op jit(solution)/shard_map/ppermute | solution.py:662
  414.9 24.7 %collective-permute-start.55 = (bf16[128,2048]{1,0:T(8,128)(2,1)S(1)}, bf16[128,2048]{1,0:T(8,128)(2,1)S(1)}, u32[]{:S(2)}, u32[]{:S(2)}) collective-permute-start(bf16[128,2048]{1,0:T(8,128)(2,1)S(1)} %get-tuple-element.373.refs_0_), channel_id=1, source_target_pairs={{0,16},{4,20},{8,24},{12,28},{16,0},{20,4},{24,8},{28,12},{1,17},{... | collective-permute-start | bytes 1572872 | tf_op jit(solution)/shard_map/ppermute | solution.py:662
  416.2 23.4 %collective-permute-start.53 = (bf16[128,2048]{1,0:T(8,128)(2,1)S(1)}, bf16[128,2048]{1,0:T(8,128)(2,1)}, u32[]{:S(2)}, u32[]{:S(2)}) collective-permute-start(bf16[128,2048]{1,0:T(8,128)(2,1)S(1)} %get-tuple-element.373.refs_0_), channel_id=1, source_target_pairs={{0,8},{4,12},{8,0},{12,4},{16,24},{20,28},{24,16},{28,20},{1,9},{5... | collective-permute-start | bytes 1572872 | tf_op jit(solution)/shard_map/ppermute | solution.py:662
  416.9 23.3 %collective-permute-start.52 = (bf16[128,2048]{1,0:T(8,128)(2,1)S(1)}, bf16[128,2048]{1,0:T(8,128)(2,1)}, u32[]{:S(2)}, u32[]{:S(2)}) collective-permute-start(bf16[128,2048]{1,0:T(8,128)(2,1)S(1)} %get-tuple-element.373.refs_0_), channel_id=1, source_target_pairs={{0,4},{4,0},{8,12},{12,8},{16,20},{20,16},{24,28},{28,24},{1,5},{5... | collective-permute-start | bytes 1572872 | tf_op jit(solution)/shard_map/ppermute | solution.py:662
  450.4 113.2 %reduce-scatter.6.cloned.1.call-start = ((), (), s32[]{:S(2)}) async-start(), calls=%async_computation.8 | async-start | bytes 3686400 | tf_op jit(solution)/shard_map/reduce_scatter | solution.py:936
  450.4 31.2 %collective-permute-start.59 = (bf16[96,2048]{1,0:T(8,128)(2,1)}, bf16[96,2048]{1,0:T(8,128)(2,1)S(1)}, u32[]{:S(2)}, u32[]{:S(2)}) collective-permute-start(bf16[96,2048]{1,0:T(8,128)(2,1)} %get-tuple-element.380), channel_id=1, source_target_pairs={{0,8},{4,12},{8,0},{12,4},{16,24},{20,28},{24,16},{28,20},{1,9},{5... | collective-permute-start | bytes 1179656 | tf_op jit(solution)/shard_map/ppermute | solution.py:662
  451.8 30.6 %collective-permute-start.60 = (bf16[96,2048]{1,0:T(8,128)(2,1)}, bf16[96,2048]{1,0:T(8,128)(2,1)S(1)}, u32[]{:S(2)}, u32[]{:S(2)}) collective-permute-start(bf16[96,2048]{1,0:T(8,128)(2,1)} %get-tuple-element.382), channel_id=1, source_target_pairs={{0,16},{4,20},{8,24},{12,28},{16,0},{20,4},{24,8},{28,12},{1,17},{... | collective-permute-start | bytes 1179656 | tf_op jit(solution)/shard_map/ppermute | solution.py:662
  452.5 30.7 %collective-permute-start.61 = (bf16[96,2048]{1,0:T(8,128)(2,1)S(1)}, bf16[96,2048]{1,0:T(8,128)(2,1)S(1)}, u32[]{:S(2)}, u32[]{:S(2)}) collective-permute-start(bf16[96,2048]{1,0:T(8,128)(2,1)S(1)} %copy-done.90), channel_id=1, source_target_pairs={{0,24},{4,28},{8,16},{12,20},{16,8},{20,12},{24,0},{28,4},{1,25},{... | collective-permute-start | bytes 1179656 | tf_op jit(solution)/shard_map/ppermute | solution.py:662
  505.5 109.5 %reduce-scatter.8.cloned.1.call-start = ((), (), s32[]{:S(2)}) async-start(), calls=%async_computation.9 | async-start | bytes 2621440 | tf_op jit(solution)/shard_map/reduce_scatter | solution.py:958
  566.1 24.7 %collective-permute-start.79 = (bf16[128,2048]{1,0:T(8,128)(2,1)S(1)}, bf16[128,2048]{1,0:T(8,128)(2,1)}, u32[]{:S(2)}, u32[]{:S(2)}) collective-permute-start(bf16[128,2048]{1,0:T(8,128)(2,1)S(1)} %copy-done.52), channel_id=1, source_target_pairs={{0,16},{4,20},{8,24},{12,28},{16,0},{20,4},{24,8},{28,12},{1,17},{... | collective-permute-start | bytes 1572872 | tf_op jit(solution)/shard_map/ppermute | solution.py:662
  567.5 23.3 %collective-permute-start.80 = (bf16[128,2048]{1,0:T(8,128)(2,1)S(1)}, bf16[128,2048]{1,0:T(8,128)(2,1)}, u32[]{:S(2)}, u32[]{:S(2)}) collective-permute-start(bf16[128,2048]{1,0:T(8,128)(2,1)S(1)} %part_product.29), channel_id=1, source_target_pairs={{0,8},{4,12},{8,0},{12,4},{16,24},{20,28},{24,16},{28,20},{1,9},{5... | collective-permute-start | bytes 1572872 | tf_op jit(solution)/shard_map/ppermute | solution.py:662
  (201 other events, 1949.7 us)
Sparse Core Ops, SparseCore 0:
  9.9 56.6 all-gather.7
  79.0 50.4 all-gather.5
  131.0 44.7 all-gather.9
  450.5 43.6 reduce-scatter.3
  505.6 57.0 reduce-scatter.5
  564.9 43.7 reduce-scatter.7
